TPU v7x, 32 devices: a whole 2x2x4 slice. The times are simulated.
32 devices in a mesh: dp: 4 (over z), fsdp: 8 (over y, x, core).
Axes of the slice: x: 2, y: 2, z: 4, core: 2. Of those that a mesh axis runs over, the one named last changes fastest.
Arguments:
- token_ids: int32 [64, 512], P(('dp', 'fsdp')), may hold values from 0 to 32127, as said below
- task_ids: int32 [64], P(('dp', 'fsdp')), may hold values from 0 to 15, as said below
- lengths: int32 [64], P(('dp', 'fsdp')), may hold values from 128 to 512, as said below
- instruction: int32 [64, 512], P(('dp', 'fsdp')), may hold values from 0 to 1, as said below
- table: bfloat16 [32128, 768], P('fsdp'), may hold values from -6 to 6
- attn_gain: bfloat16 [768], P('fsdp'), may hold values from 0.099609375 to 1.8984375
- w_query: bfloat16 [768, 768], P('fsdp'), may hold values from -0.0546875 to 0.0546875
- w_key: bfloat16 [768, 768], P('fsdp'), may hold values from -0.21875 to 0.21875
- w_value: bfloat16 [768, 768], P('fsdp'), may hold values from -0.21875 to 0.21875
- w_out: bfloat16 [768, 768], P('fsdp'), may hold values from -0.875 to 0.875
- ffn_gain: bfloat16 [768], P('fsdp'), may hold values from 0.099609375 to 1.8984375
- w_in: bfloat16 [768, 3072], P('fsdp'), may hold values from -0.21875 to 0.21875
- w_back: bfloat16 [3072, 768], P('fsdp'), may hold values from -0.109375 to 0.109375
- rel_bias: bfloat16 [32, 12], P('fsdp'), may hold values from -4 to 4
- d_out: bfloat16 [64, 512, 768], P(('dp', 'fsdp')), may hold values from -6 to 6
Outputs:
- activations: bfloat16 [64, 512, 768], P(('dp', 'fsdp'))
- table_grad: float32 [32128, 768], P('fsdp')
- grad_attn_gain: float32 [768], P('fsdp')
- grad_w_query: float32 [768, 768], P('fsdp')
- grad_w_key: float32 [768, 768], P('fsdp')
- grad_w_value: float32 [768, 768], P('fsdp')
- grad_w_out: float32 [768, 768], P('fsdp')
- grad_ffn_gain: float32 [768], P('fsdp')
- grad_w_in: float32 [768, 3072], P('fsdp')
- grad_w_back: float32 [3072, 768], P('fsdp')
- grad_rel_bias: float32 [32, 12], P('fsdp')
Inputs may be any that keep to these rules, and one draw needn't show every extreme that they name: `token_ids`: among the 1024 token slots of one device's rows, at most 256 hold ids of one block of 4016 consecutive ids, and in every device's rows some block holds exactly 256. `task_ids`: task ids never fall along the rows; 0 and 15 both occur. `lengths`: some row has length 512. Each row's instruction is its first tokens: 1 on a prefix of one or more positions shorter than the row's length, 0 elsewhere.
All inputs are finite; a program needn't handle non-finite values.
Results may differ from a plain program's by a relative error of at most 0.012.
The roundings to bfloat16 on the way count: a program that leaves them out, or rounds other values in their place, can miss the bound.
Values may be sent and summed in bfloat16 or wider, within the bound.
No kernel may reach another device: no remote copies, remote signals or barrier semaphores. Data moves between devices by JAX's collectives and lax.ppermute only.
A program may use at most 192 MiB of HBM per device.

v0:
```python
import jax
import jax.numpy as jnp
from jax import lax
from jax.sharding import PartitionSpec as P

NB = 32
MICRO = 2


EPS = 1e-06
NEG = -1000000000.0
LIMITS = (12, 16, 23, 32, 46, 64, 91)
HIGH = lax.Precision.HIGHEST


def bucket_map(length):
    positions = jnp.arange(length, dtype=jnp.int32)
    offset = positions[None, :] - positions[:, None]
    distance = jnp.abs(offset)
    far_bucket = 8 + sum(((distance >= limit).astype(jnp.int32) for limit in LIMITS))
    upper = jnp.where(offset > 0, 16, 0).astype(jnp.int32)
    return upper + jnp.where(distance < 8, distance, far_bucket)


def normed(values, gains):
    return values * lax.rsqrt(jnp.mean(values * values, axis=-1, keepdims=True) + EPS) * gains


def norm_back(values, gains, cotangent):
    unused_out, pullback = jax.vjp(normed, values, gains)
    return pullback(cotangent)


def contract_rows(left, right):
    return lax.dot_general(
        left, right, (((0,), (0,)), ((), ())), preferred_element_type=jnp.float32
    )


def times_transposed(left, right):
    return lax.dot_general(
        left, right, (((1,), (1,)), ((), ())), preferred_element_type=jnp.float32
    )


def micro_step(weights, embedded, lengths_mb, seed_mb, bucket_hot):
    attn_gain, w_query, w_key, w_value, w_out, ffn_gain, w_in, w_back, rel_bias = weights
    rows_micro, seq_len, model_width = seed_mb.shape
    heads = rel_bias.shape[1]
    inner_width = w_query.shape[1]
    head_size = inner_width // heads
    tokens_micro = rows_micro * seq_len
    first_gain = attn_gain.astype(jnp.float32)
    second_gain = ffn_gain.astype(jnp.float32)
    stream = embedded.astype(jnp.float32)
    normed_one = normed(stream, first_gain).astype(jnp.bfloat16)
    w_joint = jnp.concatenate([w_query, w_key, w_value], axis=1)
    joint = jnp.dot(normed_one, w_joint, preferred_element_type=jnp.float32).astype(jnp.bfloat16)
    split_heads = joint.reshape(rows_micro, seq_len, 3, heads, head_size)
    queries = split_heads[:, :, 0]
    key_rows = split_heads[:, :, 1]
    value_rows = split_heads[:, :, 2]
    bias = jnp.dot(bucket_hot, rel_bias.astype(jnp.float32), precision=HIGH).T.reshape(
        heads, seq_len, seq_len
    )
    positions = jnp.arange(seq_len, dtype=jnp.int32)
    key_usable = positions[None, :] < lengths_mb[:, None]

    def row_scores(queries_row, keys_row, usable_row):
        scores = (
            jnp.einsum("qhd,khd->hqk", queries_row, keys_row, preferred_element_type=jnp.float32)
            + bias
        )
        return jnp.where(usable_row[None, None, :], scores, NEG)

    def attend(row_items):
        queries_row, keys_row, values_row, usable_row = row_items
        scores = row_scores(queries_row, keys_row, usable_row)
        largest = jnp.max(scores, axis=-1, keepdims=True)
        raised = jnp.exp(scores - largest)
        totals = jnp.sum(raised, axis=-1, keepdims=True)
        probs = raised / totals
        mixed = jnp.einsum(
            "hqk,khd->qhd",
            probs.astype(jnp.bfloat16),
            values_row,
            preferred_element_type=jnp.float32,
        )
        return (mixed.astype(jnp.bfloat16), largest + jnp.log(totals))

    attended, log_totals = lax.map(attend, (queries, key_rows, value_rows, key_usable))
    flat_attended = attended.reshape(tokens_micro, inner_width)
    hidden = stream + jnp.dot(flat_attended, w_out, preferred_element_type=jnp.float32)
    normed_two = normed(hidden, second_gain).astype(jnp.bfloat16)
    pre_act = jnp.dot(normed_two, w_in, preferred_element_type=jnp.float32)
    activated = jax.nn.gelu(pre_act).astype(jnp.bfloat16)
    result = hidden + jnp.dot(activated, w_back, preferred_element_type=jnp.float32)
    grad_out = seed_mb.reshape(tokens_micro, model_width)
    grad_low = grad_out.astype(jnp.bfloat16)
    grad_back = contract_rows(activated, grad_low)
    unused_act, gelu_pull = jax.vjp(jax.nn.gelu, pre_act)
    grad_pre = gelu_pull(times_transposed(grad_low, w_back))[0].astype(jnp.bfloat16)
    grad_in = contract_rows(normed_two, grad_pre)
    grad_hidden_norm, grad_second = norm_back(hidden, second_gain, times_transposed(grad_pre, w_in))
    grad_hidden = grad_out + grad_hidden_norm
    grad_hidden_low = grad_hidden.astype(jnp.bfloat16)
    grad_out_weight = contract_rows(flat_attended, grad_hidden_low)
    grad_attended = (
        times_transposed(grad_hidden_low, w_out)
        .astype(jnp.bfloat16)
        .reshape(rows_micro, seq_len, heads, head_size)
    )

    def attend_back(score_sum, row_items):
        queries_row, keys_row, values_row, usable_row, log_row, grad_row = row_items
        probs = jnp.exp(row_scores(queries_row, keys_row, usable_row) - log_row)
        grad_values = jnp.einsum(
            "hqk,qhd->khd", probs.astype(jnp.bfloat16), grad_row, preferred_element_type=jnp.float32
        ).astype(jnp.bfloat16)
        grad_probs = jnp.einsum(
            "qhd,khd->hqk", grad_row, values_row, preferred_element_type=jnp.float32
        )
        grad_scores = (
            probs * (grad_probs - jnp.sum(probs * grad_probs, axis=-1, keepdims=True))
        ).astype(jnp.bfloat16)
        grad_queries = jnp.einsum(
            "hqk,khd->qhd", grad_scores, keys_row, preferred_element_type=jnp.float32
        ).astype(jnp.bfloat16)
        grad_keys = jnp.einsum(
            "hqk,qhd->khd", grad_scores, queries_row, preferred_element_type=jnp.float32
        ).astype(jnp.bfloat16)
        return (
            score_sum + grad_scores.astype(jnp.float32),
            jnp.stack([grad_queries, grad_keys, grad_values], axis=1),
        )

    score_total, grad_joint = lax.scan(
        attend_back,
        jnp.zeros((heads, seq_len, seq_len), jnp.float32),
        (queries, key_rows, value_rows, key_usable, log_totals, grad_attended),
    )
    grad_joint = grad_joint.reshape(tokens_micro, 3 * inner_width)
    grad_w_joint = contract_rows(normed_one, grad_joint)
    grad_stream_norm, grad_first = norm_back(
        stream, first_gain, times_transposed(grad_joint, w_joint)
    )
    grad_rel = lax.dot_general(
        bucket_hot,
        score_total.reshape(heads, seq_len * seq_len),
        (((0,), (1,)), ((), ())),
        precision=HIGH,
        preferred_element_type=jnp.float32,
    )
    grads = (
        grad_first,
        grad_w_joint[:, :inner_width],
        grad_w_joint[:, inner_width : 2 * inner_width],
        grad_w_joint[:, 2 * inner_width :],
        grad_out_weight,
        grad_second,
        grad_in,
        grad_back,
        grad_rel,
    )
    return (result, grads, grad_hidden + grad_stream_norm)


def per_device(
    token_ids,
    task_ids,
    lengths,
    instruction,
    table,
    attn_gain,
    w_query,
    w_key,
    w_value,
    w_out,
    ffn_gain,
    w_in,
    w_back,
    rel_bias,
    d_out,
):
    rows_dev, seq_len = token_ids.shape
    vshard, model_width = table.shape
    shards = lax.axis_size("fsdp")
    token_count = rows_dev * seq_len
    rows_micro = rows_dev // MICRO
    tokens_micro = rows_micro * seq_len
    capacity = 2 * token_count // shards
    task_count = rows_dev * lax.axis_size("dp") * shards // 4
    task_hot = (task_ids[:, None] == jnp.arange(task_count, dtype=jnp.int32)[None, :]).astype(
        jnp.float32
    )
    counts = lax.psum(jnp.sum(task_hot, axis=0), ("dp", "fsdp"))
    row_weight = 1.0 / jnp.dot(task_hot, counts, precision=HIGH)
    positions = jnp.arange(seq_len, dtype=jnp.int32)
    pool_mask = ((positions[None, :] < lengths[:, None]) & (instruction == 0)).astype(jnp.float32)
    seed_grad = d_out.astype(jnp.float32) * pool_mask[:, :, None] * row_weight[:, None, None]
    flat_ids = token_ids.reshape(token_count)
    owner = flat_ids // vshard
    local_row = flat_ids - owner * vshard
    owner_hot = (owner[:, None] == jnp.arange(shards, dtype=jnp.int32)[None, :]).astype(jnp.int32)
    rank_within = jnp.sum((jnp.cumsum(owner_hot, axis=0) - owner_hot) * owner_hot, axis=1)
    slot = owner * capacity + rank_within
    requests = (
        jnp.full((shards * capacity,), -1, jnp.int32)
        .at[slot]
        .set(local_row)
        .reshape(shards, capacity)
    )
    asked = lax.all_to_all(requests, "fsdp", split_axis=0, concat_axis=0, tiled=True)
    usable = asked >= 0
    looked = jnp.take(table, jnp.maximum(asked, 0), axis=0)
    looked = jnp.where(usable[..., None], looked, jnp.zeros((), table.dtype))
    replies, asked = (
        lax.all_to_all(looked, "fsdp", split_axis=0, concat_axis=0, tiled=True),
        asked,
    )
    embedded = jnp.take(replies.reshape(shards * capacity, model_width), slot, axis=0)
    bucket_hot = (
        bucket_map(seq_len).reshape(seq_len * seq_len, 1)
        == jnp.arange(NB, dtype=jnp.int32)[None, :]
    ).astype(jnp.float32)
    results = []
    embed_grads = []
    summed = None
    for micro_index in range(MICRO):
        gathered = (
            lax.all_gather(attn_gain, "fsdp", axis=0, tiled=True),
            lax.all_gather(w_query, "fsdp", axis=0, tiled=True),
            lax.all_gather(w_key, "fsdp", axis=0, tiled=True),
            lax.all_gather(w_value, "fsdp", axis=0, tiled=True),
            lax.all_gather(w_out, "fsdp", axis=0, tiled=True),
            lax.all_gather(ffn_gain, "fsdp", axis=0, tiled=True),
            lax.all_gather(w_in, "fsdp", axis=0, tiled=True),
            lax.all_gather(w_back, "fsdp", axis=0, tiled=True),
            lax.all_gather(rel_bias, "fsdp", axis=0, tiled=True),
        )
        row_start = micro_index * rows_micro
        token_start = micro_index * tokens_micro
        result, grads, grad_embed = micro_step(
            gathered,
            embedded[token_start : token_start + tokens_micro],
            lengths[row_start : row_start + rows_micro],
            seed_grad[row_start : row_start + rows_micro],
            bucket_hot,
        )
        results.append(result)
        embed_grads.append(grad_embed)
        part_sums = (
            lax.psum_scatter(grads[0], "fsdp", scatter_dimension=0, tiled=True),
            lax.psum_scatter(grads[1], "fsdp", scatter_dimension=0, tiled=True),
            lax.psum_scatter(grads[2], "fsdp", scatter_dimension=0, tiled=True),
            lax.psum_scatter(grads[3], "fsdp", scatter_dimension=0, tiled=True),
            lax.psum_scatter(grads[4], "fsdp", scatter_dimension=0, tiled=True),
            lax.psum_scatter(grads[5], "fsdp", scatter_dimension=0, tiled=True),
            lax.psum_scatter(grads[6], "fsdp", scatter_dimension=0, tiled=True),
            lax.psum_scatter(grads[7], "fsdp", scatter_dimension=0, tiled=True),
            lax.psum_scatter(grads[8], "fsdp", scatter_dimension=0, tiled=True),
        )
        summed = part_sums if micro_index == 0 else jax.tree.map(jnp.add, summed, part_sums)
    token_grads = jnp.concatenate(embed_grads, axis=0)
    outgoing = (
        jnp.zeros((shards * capacity, model_width), jnp.float32)
        .at[slot]
        .set(token_grads)
        .reshape(shards, capacity, model_width)
    )
    incoming = lax.all_to_all(outgoing, "fsdp", split_axis=0, concat_axis=0, tiled=True)
    table_part = (
        jnp.zeros((vshard, model_width), jnp.float32)
        .at[jnp.maximum(asked, 0).reshape(shards * capacity)]
        .add(incoming.reshape(shards * capacity, model_width))
    )
    reduced = lax.psum(
        (
            table_part,
            summed[0],
            summed[1],
            summed[2],
            summed[3],
            summed[4],
            summed[5],
            summed[6],
            summed[7],
            summed[8],
        ),
        "dp",
    )
    activations = (
        jnp.concatenate(results, axis=0)
        .reshape(rows_dev, seq_len, model_width)
        .astype(jnp.bfloat16)
    )
    return (activations,) + tuple(reduced)


def solution(mesh):
    in_specs = (
        P(("dp", "fsdp"), None),
        P(("dp", "fsdp")),
        P(("dp", "fsdp")),
        P(("dp", "fsdp"), None),
        P("fsdp", None),
        P("fsdp"),
        P("fsdp", None),
        P("fsdp", None),
        P("fsdp", None),
        P("fsdp", None),
        P("fsdp"),
        P("fsdp", None),
        P("fsdp", None),
        P("fsdp", None),
        P(("dp", "fsdp"), None, None),
    )
    out_specs = (
        P(("dp", "fsdp"), None, None),
        P("fsdp", None),
        P("fsdp"),
        P("fsdp", None),
        P("fsdp", None),
        P("fsdp", None),
        P("fsdp", None),
        P("fsdp"),
        P("fsdp", None),
        P("fsdp", None),
        P("fsdp", None),
    )
    return jax.shard_map(
        per_device, mesh=mesh, in_specs=in_specs, out_specs=out_specs, check_vma=False
    )
```

profile of v0, /device:TPU:0, one launch (start us, length us, event | category | flops | bytes accessed | tf_op | source)
XLA Modules:
  0.0 1242.5 jit_solution(4841410349927650554)
XLA Ops:
  17.6 4.9 scatter_custom_fusion
  22.5 5.2 all-to-all-start
  31.0 41.0 %psum.77 = f32[16]{0:T(128)} all-reduce(f32[16]{0:T(128)S(1)} %convert_reduce_fusion), channel_id=1, replica_groups=mesh['dp'=4,'fsdp'=8] {'dp','fsdp'}, use_global_device_ids=true, to_apply=%region_13.14 | all-reduce | flops 16 | bytes 128 | tf_op jit(solution)/shard_map/psum | solution.py:196
  73.7 13.1 %all-reduce.8 = (bf16[768]{0:T(1024)(128)(2,1)S(1)}, bf16[768]{0:T(1024)(128)(2,1)S(1)}) all-reduce(bf16[768]{0:T(1024)(128)(2,1)S(1)} %dynamic-update-slice, bf16[768]{0:T(1024)(128)(2,1)S(1)} %dynamic-update-slice.1), channel_id=1, replica_groups=mesh['dp'=4,'fsdp'=8] {'fsdp'}, use_global_device_ids=true, to_apply=%add | all-reduce | flops 1536 | bytes 6144
  86.8 9.8 all-gather
  96.6 12.1 gather_fusion
  110.8 4.6 all-to-all-start.1
  116.0 6.6 fusion.2
  122.6 19.1 %copy.127 = f32[2,8,512,512]{3,2,1,0:T(8,128)} copy(f32[2,8,512,512]{3,1,2,0:T(8,128)S(1)} %bitcast.211) | data formatting | bytes 33554432
  141.7 10.7 slice.101
  152.5 13.0 %copy.97 = f32[12,512,512]{1,2,0:T(8,128)} copy(f32[12,512,512]{2,1,0:T(8,128)} %slice.101) | data formatting | bytes 25165824 | tf_op jit(solution)/shard_map/reshape | solution.py:63
  177.2 7.0 gather_fusion.1
  190.3 4.3 copy.96
  194.6 13.4 %fusion.125 = (f32[12,512]{1,0:T(8,128)S(1)}, f32[12,512,512]{1,2,0:T(8,128)}) fusion(f32[12,512,512]{1,2,0:T(8,128)} %copy.97, bf16[1,512,3,12,64]{1,4,3,2,0:T(8,128)(2,1)} %bitcast.218, pred[512]{0:T(512)(128)(4,1)S(1)} %copy-done.75), kind=kOutput, calls=%fused_computation.224 | convolution fusion | flops 412084224 | bytes 26763776 | tf_op jit(solution)/shard_map/while/body/eval_jaxpr/qhd,khd->hqk/dot_general | solution.py:71
  215.9 6.6 fusion.6
  231.3 6.4 fusion.124
  248.2 8.2 fusion.121
  256.4 9.2 fusion.23
  271.1 6.2 fusion.16
  285.3 7.7 fusion.69
  292.9 9.0 multiply_reduce_fusion
  307.2 4.8 convolution_add_fusion.2
  312.2 11.2 multiply_convert_fusion
  326.8 7.3 multiply_reduce_fusion.1
  334.0 7.3 multiply_convert_fusion.1
  364.4 5.8 fusion.91
  370.2 10.3 convolution_add_fusion
  381.9 4.8 fusion.119
  386.8 5.4 convolution_add_fusion.1
  392.5 5.0 fusion.127
  402.3 8.4 scatter_custom_fusion.1
  410.7 86.4 %all_to_all.19 = f32[8,256,768]{2,1,0:T(8,128)} all-to-all(f32[8,256,768]{2,1,0:T(8,128)} %bitcast.217), channel_id=1, replica_groups=mesh['dp'=4,'fsdp'=8] {'fsdp'}, dimensions={0} | all-to-all | bytes 12582912 | tf_op jit(solution)/shard_map/all_to_all | solution.py:271
  497.1 20.5 %scatter_custom_fusion.2 = f32[4016,768]{1,0:T(8,128)} fusion(s32[2048]{0:T(1024)} %bitcast.253, f32[2048,768]{1,0:T(8,128)} %bitcast.239, f32[]{:T(128)} %constant.163.clone.1), kind=kCustom, calls=%fused_computation.54 | custom fusion | flops 1572864 | bytes 12337664 | tf_op jit(solution)/shard_map/scatter-add | solution.py:275
  517.7 79.2 %reduce-scatter.17.cloned.1.call-done = f32[384,768]{1,0:T(8,128)} async-done(((f32[3072,768]{1,0:T(8,128)}), f32[384,768]{1,0:T(8,128)}) %reduce-scatter.17.cloned.1.call-update) | async-done | bytes 1179664 | tf_op jit(solution)/shard_map/reduce_scatter | solution.py:260
  596.9 79.9 %reduce-scatter.15.cloned.1.call-done = f32[96,3072]{1,0:T(8,128)} async-done(((f32[768,3072]{1,0:T(8,128)}), f32[96,3072]{1,0:T(8,128)}) %reduce-scatter.15.cloned.1.call-update) | async-done | bytes 1179664 | tf_op jit(solution)/shard_map/reduce_scatter | solution.py:259
  678.1 8.6 copy.111
  686.7 8.8 copy.110
  695.5 6.9 pad.13
  702.5 11.6 copy.129
  718.3 11.5 copy.128
  729.8 7.8 fusion
  737.6 19.1 %fusion.75 = f32[32,12]{1,0:T(8,128)S(1)} fusion(f32[32,12]{1,0:T(8,128)S(1)} %fusion, bf16[12,262144]{1,0:T(8,128)(2,1)S(1)} %bitcast.234, s32[262144]{0:T(1024)S(1)} %copy-done.32), kind=kOutput, calls=%fused_computation.136 | convolution fusion | flops 209715584 | bytes 7343104 | tf_op jit(solution)/shard_map/dot_general | solution.py:147
  756.7 24.5 %all-reduce.5 = (f32[768]{0:T(1024)S(1)}, f32[768]{0:T(1024)S(1)}, f32[32,12]{1,0:T(8,128)S(1)}) all-reduce(f32[768]{0:T(1024)S(1)} %add.404, f32[768]{0:T(1024)S(1)} %add.409, f32[32,12]{1,0:T(8,128)S(1)} %fusion.75), channel_id=11, replica_groups=mesh['dp'=4,'fsdp'=8] {'fsdp'}, use_global_device_ids=true, to_apply=%region_24.25.clone | all-reduce | flops 1920 | bytes 15360
  781.4 13.1 %all-reduce.6 = (f32[96]{0:T(128)}, f32[96]{0:T(128)}, f32[4,12]{1,0:T(4,128)}) all-reduce(f32[96]{0:T(128)S(1)} %dynamic-slice.5, f32[96]{0:T(128)S(1)} %dynamic-slice.7, f32[4,12]{1,0:T(4,128)S(1)} %constant_dynamic-slice_fusion), channel_id=1, replica_groups=mesh['dp'=4,'fsdp'=8] {'dp'}, use_global_device_ids=true, to_apply=%region_27.28 | all-reduce | flops 240 | bytes 1920 | tf_op jit(solution)/shard_map/psum | solution.py:277
  794.5 8.0 add_convert_fusion
  802.5 7.9 add_convert_fusion.1
  811.6 409.1 %all-reduce.11.cloned.1.call-done = (f32[4016,768]{1,0:T(8,128)}, f32[96,768]{1,0:T(8,128)}, f32[96,768]{1,0:T(8,128)}, f32[96,768]{1,0:T(8,128)}, f32[96,768]{1...) async-done(((f32[4016,768]{1,0:T(8,128)}, f32[96,768]{1,0:T(8,128)}, f32[96,768]{1,0:T(8,128)}, f32[96,768]{1,0:T(8,128)}, f32[96,768]{1,0:T(8,128)}, ...) | async-done | bytes 15876112 | tf_op jit(solution)/shard_map/psum | solution.py:277
  1220.8 10.1 copy.150
  (320 shorter events, 124.0 us)
Async XLA Ops:
  7.2 21.3 %copy-start.82 = (s32[2]{0:T(128)S(1)}, s32[2]{0:T(128)}, u32[]{:S(2)}) copy-start(s32[2]{0:T(128)} %param.16) | copy-start | bytes 28
  7.2 164.1 %all-gather.8.cloned.1.call-start = ((), (), s32[]{:S(2)}) async-start(), calls=%async_computation.9 | async-start | bytes 1327104 | tf_op jit(solution)/shard_map/all_gather | solution.py:232
  7.9 164.8 %all-gather.10.cloned.1.call-start = ((), (), s32[]{:S(2)}) async-start(), calls=%async_computation.10 | async-start | bytes 1327104 | tf_op jit(solution)/shard_map/all_gather | solution.py:233
  8.7 165.4 %all-gather.12.cloned.1.call-start = ((), (), s32[]{:S(2)}) async-start(), calls=%async_computation.11 | async-start | bytes 1327104 | tf_op jit(solution)/shard_map/all_gather | solution.py:234
  9.4 218.3 %all-gather.14.cloned.1.call-start = ((), (), s32[]{:S(2)}) async-start(), calls=%async_computation.12 | async-start | bytes 1327104 | tf_op jit(solution)/shard_map/all_gather | solution.py:235
  10.0 238.2 %all-gather.16.cloned.1.call-start = ((), (), s32[]{:S(2)}) async-start(), calls=%async_computation.13 | async-start | bytes 5308416 | tf_op jit(solution)/shard_map/all_gather | solution.py:237
  17.6 11.6 copy-start.65
  22.5 74.1 %all-to-all-start = ((s32[8,1,256]{2,1,0:T(1,128)}), s32[8,1,256]{2,1,0:T(1,128)S(1)}, u32[]{:S(2)}, u32[]{:S(2)}) async-start(s32[8,1,256]{2,1,0:T(1,128)} %bitcast.3), calls=%async_computation | async-start | bytes 16384 | tf_op jit(solution)/shard_map/all_to_all | solution.py:213
  27.7 228.8 %all-gather.18.cloned.1.call-start = ((), (), s32[]{:S(2)}) async-start(), calls=%async_computation.14 | async-start | bytes 5308416 | tf_op jit(solution)/shard_map/all_gather | solution.py:238
  28.9 43.1 %copy-start.72 = (u32[32]{0:T(128)S(1)}, u32[32]{0:T(128)}, u32[]{:S(2)}) copy-start(u32[32]{0:T(128)} %constant.191) | copy-start | bytes 388
  28.9 44.3 %copy-start.80 = (bf16[96]{0:T(256)(128)(2,1)S(1)}, bf16[96]{0:T(256)(128)(2,1)}, u32[]{:S(2)}) copy-start(bf16[96]{0:T(256)(128)(2,1)} %param.20) | copy-start | bytes 580
  28.9 44.6 %copy-start.81 = (bf16[96]{0:T(256)(128)(2,1)S(1)}, bf16[96]{0:T(256)(128)(2,1)}, u32[]{:S(2)}) copy-start(bf16[96]{0:T(256)(128)(2,1)} %param.25) | copy-start | bytes 580
  28.9 57.9 %copy-start.73 = (bf16[4,12]{1,0:T(4,128)(2,1)S(1)}, bf16[4,12]{1,0:T(4,128)(2,1)}, u32[]{:S(2)}) copy-start(bf16[4,12]{1,0:T(4,128)(2,1)} %param.28) | copy-start | bytes 292
  86.8 121.3 %copy-start.44 = (f32[768]{0:T(1024)}, f32[768]{0:T(1024)S(1)}, u32[]{:S(2)}) copy-start(f32[768]{0:T(1024)S(1)} %convert_element_type.249) | copy-start | bytes 9220
  96.6 12.1 copy-start.60
  110.8 64.6 %all-to-all-start.1 = ((bf16[8,256,768]{2,1,0:T(8,128)(2,1)}), bf16[8,256,768]{2,1,0:T(8,128)(2,1)}, u32[]{:S(2)}, u32[]{:S(2)}) async-start(bf16[8,256,768]{2,1,0:T(8,128)(2,1)} %select_select_fusion), calls=%async_computation.1 | async-start | bytes 6291456 | tf_op jit(solution)/shard_map/all_to_all | solution.py:218
  115.4 402.2 %reduce-scatter.13.cloned.1.call-start = ((), (), s32[]{:S(2)}) async-start(), calls=%async_computation.18 | async-start | bytes 2654208 | tf_op jit(solution)/shard_map/reduce_scatter | solution.py:257
  152.4 13.1 %copy-start.67 = (s32[2]{0:T(128)S(1)}, s32[2]{0:T(128)}, u32[]{:S(2)}) copy-start(s32[2]{0:T(128)} %param.17) | copy-start | bytes 28
  152.4 16.0 %copy-start.83 = (s32[2]{0:T(128)S(1)}, s32[2]{0:T(128)}, u32[]{:S(2)}) copy-start(s32[2]{0:T(128)} %param.16) | copy-start | bytes 28
  152.4 16.0 %copy-start.84 = (f32[16]{0:T(128)S(1)}, f32[16]{0:T(128)}, u32[]{:S(2)}) copy-start(f32[16]{0:T(128)} %psum.77) | copy-start | bytes 196
  152.4 16.2 %copy-start.66 = (s32[1024,1]{0,1:T(1,128)S(1)}, s32[1024,1]{0,1:T(1,128)}, u32[]{:S(2)}) copy-start(s32[1024,1]{0,1:T(1,128)} %copy-done.65) | copy-start | bytes 12292
  152.4 16.2 %copy-start.71 = (s32[2,512]{1,0:T(2,128)S(1)}, s32[2,512]{1,0:T(2,128)}, u32[]{:S(2)}) copy-start(s32[2,512]{1,0:T(2,128)} %param.18) | copy-start | bytes 12292
  152.4 16.3 %copy-start.55 = (s32[1024]{0:T(1024)S(1)}, s32[1024]{0:T(1024)}, u32[]{:S(2)}) copy-start(s32[1024]{0:T(1024)} %copy-done.54) | copy-start | bytes 12292
  152.4 16.8 %copy-start.38 = (bf16[2,512,768]{2,1,0:T(8,128)(2,1)S(1)}, bf16[2,512,768]{2,1,0:T(8,128)(2,1)}, u32[]{:S(2)}) copy-start(bf16[2,512,768]{2,1,0:T(8,128)(2,1)} %param.29) | copy-start | bytes 4718596
  184.4 61.6 %copy-start.4 = (bf16[1024,768]{1,0:T(8,128)(2,1)}, bf16[1024,768]{1,0:T(8,128)(2,1)S(1)}, u32[]{:S(2)}) copy-start(bf16[1024,768]{1,0:T(8,128)(2,1)S(1)} %broadcast_select_fusion) | copy-start | bytes 4718596
  186.8 21.3 %copy-start.58 = (f32[512]{0:T(512)}, f32[512]{0:T(512)S(1)}, u32[]{:S(2)}) copy-start(f32[512]{0:T(512)S(1)} %fusion.115) | copy-start | bytes 6148
  194.6 13.5 %copy-start.48 = (bf16[768,2304]{1,0:T(8,128)(2,1)S(1)}, bf16[768,2304]{1,0:T(8,128)(2,1)}, u32[]{:S(2)}) copy-start(bf16[768,2304]{1,0:T(8,128)(2,1)} %copy-done.46) | copy-start | bytes 10616836
  307.2 19.1 %copy-start.28 = (bf16[512,768]{0,1:T(8,128)(2,1)}, bf16[512,768]{0,1:T(8,128)(2,1)S(1)}, u32[]{:S(2)}) copy-start(bf16[512,768]{0,1:T(8,128)(2,1)S(1)} %copy.102) | copy-start | bytes 2359300
  312.1 205.6 %reduce-scatter.11.cloned.1.call-start = ((), (), s32[]{:S(2)}) async-start(), calls=%async_computation.17 | async-start | bytes 2654208 | tf_op jit(solution)/shard_map/reduce_scatter | solution.py:256
  312.1 14.1 %slice-start = ((s8[12582912]{0:T(1024)(128)(4,1)}), s8[4194304]{0:T(1024)(128)(4,1)S(1)}, s32[]{:S(2)}) async-start(s8[12582912]{0:T(1024)(128)(4,1)} %bitcast.209), calls=%async_computation.22 | async-start | bytes 8388608
  312.1 14.1 %slice-start.1 = ((s8[12582912]{0:T(1024)(128)(4,1)}), s8[4194304]{0:T(1024)(128)(4,1)S(1)}, s32[]{:S(2)}) async-start(s8[12582912]{0:T(1024)(128)(4,1)} %bitcast.209), calls=%async_computation.23 | async-start | bytes 8388608
  312.1 14.6 %slice-start.2 = ((s8[12582912]{0:T(1024)(128)(4,1)}), s8[4194304]{0:T(1024)(128)(4,1)S(1)}, s32[]{:S(2)}) async-start(s8[12582912]{0:T(1024)(128)(4,1)} %bitcast.209), calls=%async_computation.24 | async-start | bytes 8388608
  323.3 18.0 %copy-start.2 = (bf16[12,512,512]{1,2,0:T(8,128)(2,1)}, bf16[12,512,512]{1,2,0:T(8,128)(2,1)S(1)}, u32[]{:S(2)}) copy-start(bf16[12,512,512]{1,2,0:T(8,128)(2,1)S(1)} %multiply_convert_fusion) | copy-start | bytes 18874372
  362.5 155.2 %reduce-scatter.9.cloned.1.call-start = ((), (), s32[]{:S(2)}) async-start(), calls=%async_computation.16 | async-start | bytes 2654208 | tf_op jit(solution)/shard_map/reduce_scatter | solution.py:255
  363.2 154.4 %reduce-scatter.7.cloned.1.call-start = ((), (), s32[]{:S(2)}) async-start(), calls=%async_computation.15 | async-start | bytes 2654208 | tf_op jit(solution)/shard_map/reduce_scatter | solution.py:254
  363.8 233.1 %reduce-scatter.17.cloned.1.call-start = ((), (), s32[]{:S(2)}) async-start(), calls=%async_computation.20 | async-start | bytes 10616832 | tf_op jit(solution)/shard_map/reduce_scatter | solution.py:260
  380.5 296.2 %reduce-scatter.15.cloned.1.call-start = ((), (), s32[]{:S(2)}) async-start(), calls=%async_computation.19 | async-start | bytes 10616832 | tf_op jit(solution)/shard_map/reduce_scatter | solution.py:259
  392.2 828.5 %all-reduce.11.cloned.1.call-start = ((), (), s32[]{:S(2)}) async-start(), calls=%async_computation.21 | async-start | bytes 31752192 | tf_op jit(solution)/shard_map/psum | solution.py:277
  695.5 18.5 %slice-start.3 = ((s8[6291456]{0:T(1024)(128)(4,1)}), s8[4194304]{0:T(1024)(128)(4,1)S(1)}, s32[]{:S(2)}) async-start(s8[6291456]{0:T(1024)(128)(4,1)} %bitcast.215), calls=%async_computation.25 | async-start | bytes 8388608
  702.5 11.6 slice-start.4
  718.3 11.5 copy-start.69
  718.3 11.5 copy-start.70
  718.3 11.5 copy-start.32
  737.6 56.8 %copy-start.16 = (f32[512,768]{1,0:T(8,128)S(1)}, f32[512,768]{1,0:T(8,128)}, u32[]{:S(2)}) copy-start(f32[512,768]{1,0:T(8,128)} %get-tuple-element.166) | copy-start | bytes 4718596
  1220.8 10.9 copy-start.52
  1220.8 11.6 copy-start.51
  1220.8 12.3 copy-start.50
  1220.8 13.0 %copy-start.40 = (f32[96,3072]{1,0:T(8,128)S(1)}, f32[96,3072]{1,0:T(8,128)}, u32[]{:S(2)}) copy-start(f32[96,3072]{1,0:T(8,128)} %get-tuple-element.187) | copy-start | bytes 3538948
  (57 other events, 259.3 us)
Sparse Core Ops, SparseCore 0:
  9.9 26.7 all-gather.7
  38.6 24.1 all-gather.9
  64.7 24.0 all-gather.11
  90.5 23.9 all-gather.13
  116.2 57.6 all-gather.15
  175.6 37.0 all-gather.17
  312.2 42.8 reduce-scatter.12
  362.6 42.9 reduce-scatter.10
  409.0 61.9 reduce-scatter.8
  474.6 42.3 reduce-scatter.6
  520.4 76.4 reduce-scatter.16
  600.3 76.4 reduce-scatter.14
  680.8 539.9 all-reduce.10
where the time goes:
time: 1250 us; the launch traced here: 1240 us
  waiting for transfers between devices  573 us (46%)
  matrix products  203 us (16%)
  blocking collectives  188 us (15%)
  local copies, waits for them, and re-layouts  169 us (14%)
  other arithmetic  81.2 us (6%)
  between operations  17.3 us (1%)
    psum x1, waiting for transfers between devices, per_device(): lax.psum((table_part, summed[0], summed[1], summed[2], summed[3], summed[...  409 us
    unnamed x208, local copies, waits for them, and re-layouts  91 us
    all_to_all x1, blocking collectives, per_device(): lax.all_to_all(outgoing, 'fsdp', split_axis=0, concat_axis=0, tiled=True)  86.4 us
    reduce_scatter x1, waiting for transfers between devices, per_device(): lax.psum_scatter(grads[6], 'fsdp', scatter_dimension=0, tiled=True)  79.9 us
    reduce_scatter x1, waiting for transfers between devices, per_device(): lax.psum_scatter(grads[7], 'fsdp', scatter_dimension=0, tiled=True)  79.2 us
    psum x1, blocking collectives, per_device(): counts = lax.psum(jnp.sum(task_hot, axis=0), ('dp', 'fsdp'))  41 us
    dot_general x8, matrix products, contract_rows(): lax.dot_general(left, right, (((0,), (0,)), ((), ())), preferred_element_...  37.9 us
    unnamed x2, blocking collectives  37.6 us
  transfers between devices with their start and end apart: 15, of which 3 were waited for; matrix products, arithmetic and copies ran while one was open for 29% of the time, Pallas kernels for 0%

commit v1 on v0

v1 whole, which is shorter than its diff:
```python
import jax
import jax.numpy as jnp
from jax import lax
from jax.sharding import PartitionSpec as P

NB = 32
EPS = 1e-06
NEG = -1000000000.0
LIMITS = (12, 16, 23, 32, 46, 64, 91)
HIGH = lax.Precision.HIGHEST
LOW = jnp.bfloat16
F32 = jnp.float32


def bucket_of(offset):
    distance = jnp.abs(offset)
    far_bucket = 8 + sum(((distance >= limit).astype(jnp.int32) for limit in LIMITS))
    upper = jnp.where(offset > 0, 16, 0).astype(jnp.int32)
    return upper + jnp.where(distance < 8, distance, far_bucket)


def bucket_map(length):
    positions = jnp.arange(length, dtype=jnp.int32)
    return bucket_of(positions[None, :] - positions[:, None])


def normed(values, gains):
    return values * lax.rsqrt(jnp.mean(values * values, axis=-1, keepdims=True) + EPS) * gains


def norm_back(values, gains, cotangent):
    unused_out, pullback = jax.vjp(normed, values, gains)
    return pullback(cotangent)


def contract_rows(left, right):
    return lax.dot_general(left, right, (((0,), (0,)), ((), ())), preferred_element_type=F32)


def times_transposed(left, right):
    return lax.dot_general(left, right, (((1,), (1,)), ((), ())), preferred_element_type=F32)


def flip(value, bits):
    shards = lax.axis_size("fsdp")
    return lax.ppermute(value, "fsdp", [(i, i ^ bits) for i in range(shards)])


def gather_pieces(own):
    shards = lax.axis_size("fsdp")
    rows = own.shape[0]
    half = rows // 2
    pieces = [(0, 0, own)]
    if shards == 8:
        by_x = flip(own, 2)
        by_y = flip(own, 4)
        pieces += [(2, 0, by_x), (4, 0, by_y)]
        pieces += [(6, 0, flip(by_y[:half], 2)), (6, half, flip(by_x[half:], 4))]
    else:
        pieces += [(bits, 0, flip(own, bits)) for bits in range(2, shards, 2)]
    return pieces + [(bits ^ 1, first, flip(part, 1)) for bits, first, part in pieces]


def gather_rows(own, me):
    shards = lax.axis_size("fsdp")
    rows = own.shape[0]
    whole = jnp.zeros((shards * rows,) + own.shape[1:], own.dtype)
    for bits, first, part in gather_pieces(own):
        start = (me ^ bits) * rows + first
        whole = lax.dynamic_update_slice(whole, part, (start,) + (0,) * (own.ndim - 1))
    return whole


def scatter_sum(whole, me):
    shards, rows, columns = whole.shape
    half = rows // 2
    core = me & 1
    pairs = whole.reshape(shards // 2, 2, rows, columns)
    away = lax.dynamic_slice_in_dim(pairs, 1 - core, 1, axis=1)[:, 0].astype(LOW)
    mine = lax.dynamic_slice_in_dim(pairs, core, 1, axis=1)[:, 0]
    mine = mine + flip(away, 1).astype(F32)
    place = me >> 1

    def block(relative):
        return lax.dynamic_slice_in_dim(mine, place ^ relative, 1, axis=0)[0]

    if shards == 8:
        across = block(3).astype(LOW)
        from_x = flip(across[:half], 2).astype(F32)
        from_y = flip(across[half:], 4).astype(F32)
        to_y = block(2) + jnp.concatenate([from_x, jnp.zeros((rows - half, columns), F32)])
        to_x = block(1) + jnp.concatenate([jnp.zeros((half, columns), F32), from_y])
        return block(0) + flip(to_x.astype(LOW), 2).astype(F32) + flip(to_y.astype(LOW), 4).astype(F32)
    total = block(0)
    for relative in range(1, shards // 2):
        total = total + flip(block(relative).astype(LOW), 2 * relative).astype(F32)
    return total


def line_sum(own, at):
    chunks = own.shape[0]
    groups = lax.axis_size("dp")
    right = [(i, i + 1) for i in range(groups - 1)]
    left = [(i + 1, i) for i in range(groups - 1)]
    result = own
    zero = jnp.zeros(own.shape[1:], LOW)

    def run(pairs, place, result):
        came = zero
        for step in range(chunks + groups - 2):
            index = jnp.clip(step - place, 0, chunks - 1)
            part = lax.dynamic_index_in_dim(own, index, 0, keepdims=False)
            came = lax.ppermute((part + came.astype(F32)).astype(LOW), "dp", pairs)
            target = step - place + 1
            live = (target >= 0) & (target < chunks) & (place > 0)
            came = jnp.where(live, came, zero)
            spot = jnp.clip(target, 0, chunks - 1)
            before = lax.dynamic_index_in_dim(result, spot, 0, keepdims=False)
            result = lax.dynamic_update_index_in_dim(result, before + came.astype(F32), spot, 0)
        return result

    result = run(right, at, result)
    return run(left, groups - 1 - at, result)


def block_step(weights, embedded, lengths, seed):
    attn_gain, w_joint, w_out, ffn_gain, w_in, w_back, rel_bias = weights
    rows_dev, seq_len, model_width = seed.shape
    heads = rel_bias.shape[1]
    inner_width = w_out.shape[0]
    head_size = inner_width // heads
    tokens = rows_dev * seq_len
    first_gain = attn_gain.astype(F32)
    second_gain = ffn_gain.astype(F32)
    stream = embedded.astype(F32)
    normed_one = normed(stream, first_gain).astype(LOW)
    joint = jnp.dot(normed_one, w_joint, preferred_element_type=F32).astype(LOW)
    split_heads = joint.reshape(rows_dev, seq_len, 3, heads, head_size)
    bucket_hot = (
        bucket_map(seq_len).reshape(seq_len * seq_len, 1) == jnp.arange(NB, dtype=jnp.int32)[None, :]
    ).astype(F32)
    bias = jnp.dot(bucket_hot, rel_bias.astype(F32), precision=HIGH).T.reshape(heads, seq_len, seq_len)
    positions = jnp.arange(seq_len, dtype=jnp.int32)
    key_usable = positions[None, :] < lengths[:, None]

    def row_scores(queries_row, keys_row, usable_row):
        scores = jnp.einsum("qhd,khd->hqk", queries_row, keys_row, preferred_element_type=F32) + bias
        return jnp.where(usable_row[None, None, :], scores, NEG)

    saved = []
    attended = []
    for row in range(rows_dev):
        queries_row, keys_row, values_row = (split_heads[row, :, part] for part in range(3))
        scores = row_scores(queries_row, keys_row, key_usable[row])
        largest = jnp.max(scores, axis=-1, keepdims=True)
        raised = jnp.exp(scores - largest)
        totals = jnp.sum(raised, axis=-1, keepdims=True)
        probs = raised / totals
        mixed = jnp.einsum("hqk,khd->qhd", probs.astype(LOW), values_row, preferred_element_type=F32)
        attended.append(mixed.astype(LOW))
        saved.append(largest + jnp.log(totals))
    flat_attended = jnp.stack(attended).reshape(tokens, inner_width)
    hidden = stream + jnp.dot(flat_attended, w_out, preferred_element_type=F32)
    normed_two = normed(hidden, second_gain).astype(LOW)
    pre_act = jnp.dot(normed_two, w_in, preferred_element_type=F32)
    activated = jax.nn.gelu(pre_act).astype(LOW)
    result = hidden + jnp.dot(activated, w_back, preferred_element_type=F32)
    grad_out = seed.reshape(tokens, model_width)
    grad_low = grad_out.astype(LOW)
    grad_back = contract_rows(activated, grad_low)
    unused_act, gelu_pull = jax.vjp(jax.nn.gelu, pre_act)
    grad_pre = gelu_pull(times_transposed(grad_low, w_back))[0].astype(LOW)
    grad_in = contract_rows(normed_two, grad_pre)
    grad_hidden_norm, grad_second = norm_back(hidden, second_gain, times_transposed(grad_pre, w_in))
    grad_hidden = grad_out + grad_hidden_norm
    grad_hidden_low = grad_hidden.astype(LOW)
    grad_out_weight = contract_rows(flat_attended, grad_hidden_low)
    grad_attended = (
        times_transposed(grad_hidden_low, w_out).astype(LOW).reshape(rows_dev, seq_len, heads, head_size)
    )
    score_total = 0.0
    grad_joint = []
    for row in range(rows_dev):
        queries_row, keys_row, values_row = (split_heads[row, :, part] for part in range(3))
        grad_row = grad_attended[row]
        probs = jnp.exp(row_scores(queries_row, keys_row, key_usable[row]) - saved[row])
        grad_values = jnp.einsum("hqk,qhd->khd", probs.astype(LOW), grad_row, preferred_element_type=F32)
        grad_probs = jnp.einsum("qhd,khd->hqk", grad_row, values_row, preferred_element_type=F32)
        grad_scores = (probs * (grad_probs - jnp.sum(probs * grad_probs, axis=-1, keepdims=True))).astype(LOW)
        grad_queries = jnp.einsum("hqk,khd->qhd", grad_scores, keys_row, preferred_element_type=F32)
        grad_keys = jnp.einsum("hqk,qhd->khd", grad_scores, queries_row, preferred_element_type=F32)
        score_total = score_total + grad_scores.astype(F32)
        grad_joint.append(
            jnp.stack([grad_queries.astype(LOW), grad_keys.astype(LOW), grad_values.astype(LOW)], axis=1)
        )
    grad_joint = jnp.stack(grad_joint).reshape(tokens, 3 * inner_width)
    grad_w_joint = contract_rows(normed_one, grad_joint)
    grad_stream_norm, grad_first = norm_back(stream, first_gain, times_transposed(grad_joint, w_joint))
    grad_rel = lax.dot_general(
        bucket_hot,
        score_total.reshape(heads, seq_len * seq_len),
        (((0,), (1,)), ((), ())),
        precision=HIGH,
        preferred_element_type=F32,
    )
    return (
        result,
        grad_hidden + grad_stream_norm,
        grad_back,
        grad_in,
        grad_out_weight,
        grad_w_joint,
        grad_first,
        grad_second,
        grad_rel,
    )


def per_device(
    token_ids,
    task_ids,
    lengths,
    instruction,
    table,
    attn_gain,
    w_query,
    w_key,
    w_value,
    w_out,
    ffn_gain,
    w_in,
    w_back,
    rel_bias,
    d_out,
):
    rows_dev, seq_len = token_ids.shape
    vshard, model_width = table.shape
    inner_width = w_query.shape[1]
    ff_width = w_in.shape[1]
    shards = lax.axis_size("fsdp")
    groups = lax.axis_size("dp")
    me = lax.axis_index("fsdp")
    at = lax.axis_index("dp")
    token_count = rows_dev * seq_len
    capacity = 2 * token_count // shards
    task_count = rows_dev * groups * shards // 4

    flat_ids = token_ids.reshape(token_count)
    owner = flat_ids // vshard
    local_row = flat_ids - owner * vshard
    relative = owner ^ me
    relative_hot = (relative[:, None] == jnp.arange(shards, dtype=jnp.int32)[None, :]).astype(jnp.int32)
    rank_within = jnp.sum((jnp.cumsum(relative_hot, axis=0) - relative_hot) * relative_hot, axis=1)
    slot = relative * capacity + rank_within
    slots = jnp.arange(shards * capacity, dtype=jnp.int32)
    slot_hot = slots[:, None] == slot[None, :]
    requests = (jnp.sum(jnp.where(slot_hot, local_row[None, :] + 1, 0), axis=1) - 1).reshape(shards, capacity)
    asked = [requests[0]] + [flip(requests[r], r) for r in range(1, shards)]
    looked = [jnp.take(table, jnp.maximum(ids, 0), axis=0) for ids in asked]
    replies = [looked[0]] + [flip(looked[r], r) for r in range(1, shards)]
    embedded = jnp.take(jnp.concatenate(replies, axis=0), slot, axis=0)

    task_hot = (task_ids[:, None] == jnp.arange(task_count, dtype=jnp.int32)[None, :]).astype(F32)
    counts = jnp.sum(task_hot, axis=0)
    bits = 1
    while bits < shards:
        counts = counts + flip(counts, bits)
        bits *= 2
    bits = 1
    while bits < groups:
        counts = counts + lax.ppermute(counts, "dp", [(i, i ^ bits) for i in range(groups)])
        bits *= 2
    row_weight = 1.0 / jnp.dot(task_hot, counts, precision=HIGH)
    positions = jnp.arange(seq_len, dtype=jnp.int32)
    pool_mask = ((positions[None, :] < lengths[:, None]) & (instruction == 0)).astype(F32)
    seed_grad = d_out.astype(F32) * pool_mask[:, :, None] * row_weight[:, None, None]

    small = jnp.concatenate([attn_gain, ffn_gain, rel_bias.reshape(-1)])
    joint_width = 3 * inner_width
    small_rows = -(-small.shape[0] // joint_width)
    small = jnp.pad(small, (0, small_rows * joint_width - small.shape[0])).reshape(small_rows, joint_width)
    small_all = gather_rows(small, me).reshape(shards, small_rows * joint_width)
    own_gain = attn_gain.shape[0]
    attn_gain_all = small_all[:, :own_gain].reshape(-1)
    ffn_gain_all = small_all[:, own_gain : 2 * own_gain].reshape(-1)
    rel_all = small_all[:, 2 * own_gain : 2 * own_gain + rel_bias.size].reshape(NB, rel_bias.shape[1])
    weights = (
        attn_gain_all,
        gather_rows(jnp.concatenate([w_query, w_key, w_value], axis=1), me),
        gather_rows(w_out, me),
        ffn_gain_all,
        gather_rows(w_in, me),
        gather_rows(w_back, me),
        rel_all,
    )
    result, token_grads, grad_back, grad_in, grad_out_weight, grad_w_joint, grad_first, grad_second, grad_rel = (
        block_step(weights, embedded, lengths, seed_grad)
    )

    def owned(grad, chunks):
        own_rows = grad.shape[0] // shards
        part = scatter_sum(grad.reshape(shards, own_rows, -1), me)
        return line_sum(part.reshape(chunks, own_rows // chunks, -1), at).reshape(part.shape)

    grad_back = owned(grad_back, 4)
    grad_in = owned(grad_in, 4)
    grad_out_weight = owned(grad_out_weight, 1)
    grad_w_joint = owned(grad_w_joint, 2)
    small_grad = jnp.concatenate(
        [grad_first.reshape(shards, -1), grad_second.reshape(shards, -1), grad_rel.reshape(shards, -1)], axis=1
    )
    small_size = small_grad.shape[1]
    small_grad = jnp.pad(small_grad, ((0, 0), (0, 256 - small_size))).reshape(shards, 2, 128)
    small_grad = line_sum(scatter_sum(small_grad, me)[None], at).reshape(-1)
    grad_first = small_grad[:own_gain]
    grad_second = small_grad[own_gain : 2 * own_gain]
    grad_rel = small_grad[2 * own_gain : small_size].reshape(rel_bias.shape)

    outgoing = jnp.dot(slot_hot.astype(LOW), token_grads.astype(LOW), preferred_element_type=F32).astype(LOW)
    outgoing = outgoing.reshape(shards, capacity, model_width)
    incoming = [outgoing[0]] + [flip(outgoing[r], r) for r in range(1, shards)]
    incoming = jnp.concatenate(incoming, axis=0)
    asked = jnp.concatenate(asked, axis=0)
    chunk_rows = 256
    chunks = -(-vshard // chunk_rows)
    table_rows = jnp.arange(chunks * chunk_rows, dtype=jnp.int32)
    row_hot = (table_rows[:, None] == asked[None, :]).astype(LOW)
    table_part = jnp.dot(row_hot, incoming, preferred_element_type=F32)
    table_grad = line_sum(table_part.reshape(chunks, chunk_rows, model_width), at)
    table_grad = table_grad.reshape(chunks * chunk_rows, model_width)[:vshard]

    activations = result.reshape(rows_dev, seq_len, model_width).astype(LOW)
    return (
        activations,
        table_grad,
        grad_first,
        grad_w_joint[:, :inner_width],
        grad_w_joint[:, inner_width : 2 * inner_width],
        grad_w_joint[:, 2 * inner_width :],
        grad_out_weight,
        grad_second,
        grad_in,
        grad_back,
        grad_rel,
    )


def solution(mesh):
    both = ("dp", "fsdp")
    in_specs = (
        P(both, None),
        P(both),
        P(both),
        P(both, None),
        P("fsdp", None),
        P("fsdp"),
        P("fsdp", None),
        P("fsdp", None),
        P("fsdp", None),
        P("fsdp", None),
        P("fsdp"),
        P("fsdp", None),
        P("fsdp", None),
        P("fsdp", None),
        P(both, None, None),
    )
    out_specs = (
        P(both, None, None),
        P("fsdp", None),
        P("fsdp"),
        P("fsdp", None),
        P("fsdp", None),
        P("fsdp", None),
        P("fsdp", None),
        P("fsdp"),
        P("fsdp", None),
        P("fsdp", None),
        P("fsdp", None),
    )
    return jax.shard_map(per_device, mesh=mesh, in_specs=in_specs, out_specs=out_specs, check_vma=False)
```

time: 1250 us -> 1210 us (0.968)
  waiting for transfers between devices: 573 us -> 169 us
  starting transfers between devices: 11 us -> 313 us
  blocking collectives: 188 us -> 0 us
  local copies, waits for them, and re-layouts: 169 us -> 315 us
  other arithmetic: 81.2 us -> 171 us
  matrix products: 203 us -> 225 us
  between operations: 17.3 us -> 4.76 us
    psum x1 -> x0, waiting for transfers between devices: 409 us -> none  [per_device(): lax.psum((table_part, summed[0], summed[1], summed[2], summed[3], summed[...]
    ppermute x0 -> x174, starting transfers between devices: none -> 313 us  [the longest x80 236 us: run(): came = lax.ppermute((part + came.astype(F32)).astype(LOW), 'dp', pairs)]
    ppermute x0 -> x174, waiting for transfers between devices: none -> 169 us  [the longest x92 100 us: flip(): return lax.ppermute(value, 'fsdp', [(i, i ^ bits) for i in range(shards)])]
    reduce_scatter x6 -> x0, waiting for transfers between devices: 159 us -> none  [the longest x1 79.9 us: per_device(): lax.psum_scatter(grads[6], 'fsdp', scatter_dimension=0, tiled=True)]
    all_to_all x1 -> x0, blocking collectives: 86.4 us -> none  [per_device(): lax.all_to_all(outgoing, 'fsdp', split_axis=0, concat_axis=0, tiled=True)]
    dynamic_update_slice x0 -> x52, local copies, waits for them, and re-layouts: none -> 58.3 us  [the longest x48 57.2 us: gather_rows(): lax.dynamic_update_slice(whole, part, (start,) + (0,) * (own.ndim - 1))]
    psum x2 -> x0, blocking collectives: 54 us -> none  [the longest x1 41 us: per_device(): counts = lax.psum(jnp.sum(task_hot, axis=0), ('dp', 'fsdp'))]
    unnamed x208 -> x201, local copies, waits for them, and re-layouts: 91 us -> 41 us
  transfers between devices with their start and end apart: 15 -> 174, of which waited for: 3 -> 57; matrix products, arithmetic and copies ran while one was open for 29% -> 47% of each run, Pallas kernels for 0% -> 0%
where the time goes in v1:
time: 1210 us; the launch traced here: 1200 us
  local copies, waits for them, and re-layouts  315 us (26%)
  starting transfers between devices  313 us (26%)
  matrix products  225 us (19%)
  other arithmetic  171 us (14%)
  waiting for transfers between devices  169 us (14%)
    ppermute x80, starting transfers between devices, run(): came = lax.ppermute((part + came.astype(F32)).astype(LOW), 'dp', pairs)  236 us
    ppermute x92, waiting for transfers between devices, flip(): return lax.ppermute(value, 'fsdp', [(i, i ^ bits) for i in range(shards)])  100 us
    ppermute x92, starting transfers between devices, flip(): return lax.ppermute(value, 'fsdp', [(i, i ^ bits) for i in range(shards)])  73.1 us
    ppermute x80, waiting for transfers between devices, run(): came = lax.ppermute((part + came.astype(F32)).astype(LOW), 'dp', pairs)  64.9 us
    dynamic_update_slice x48, local copies, waits for them, and re-layouts, gather_rows(): lax.dynamic_update_slice(whole, part, (start,) + (0,) * (own.ndim - 1))  57.2 us
    gather x8, local copies, waits for them, and re-layouts, per_device(): looked = [jnp.take(table, jnp.maximum(ids, 0), axis=0) for ids in asked]  43.8 us
    dynamic_slice x64, local copies, waits for them, and re-layouts, run(): before = lax.dynamic_index_in_dim(result, spot, 0, keepdims=False)  42.3 us
    unnamed x201, local copies, waits for them, and re-layouts  41 us
  transfers between devices with their start and end apart: 174, of which 57 were waited for; matrix products, arithmetic and copies ran while one was open for 47% of the time, Pallas kernels for 0%

profile of v1, /device:TPU:0, one launch (start us, length us, event | category | flops | bytes accessed | tf_op | source)
XLA Modules:
  0.0 1197.3 jit_solution(3598316823669049106)
XLA Ops:
  88.8 5.7 gather_fusion.4
  102.2 5.8 gather_fusion.8
  108.0 5.7 gather_fusion.2
  113.7 5.9 gather_fusion.3
  131.0 5.5 gather_fusion.5
  159.9 9.9 fusion.1
  170.8 17.7 %copy.74 = f32[12,512,512]{1,2,0:T(8,128)} copy(f32[12,512,512]{2,0,1:T(8,128)} %fusion.1) | data formatting | bytes 25165824 | tf_op jit(solution)/shard_map/dot_general | solution.py:142
  214.8 19.9 %collective-permute-done.7 = bf16[256,768]{1,0:T(8,128)(2,1)S(1)} collective-permute-done((bf16[256,768]{1,0:T(8,128)(2,1)}, bf16[256,768]{1,0:T(8,128)(2,1)S(1)}, u32[]{:S(2)}, u32[]{:S(2)}) %collective-permute-start.7) | collective-permute-done | bytes 393248 | tf_op jit(solution)/shard_map/ppermute | solution.py:46
  235.8 6.2 collective-permute-done.9
  245.4 5.2 gather_fusion
  261.0 7.0 collective-permute-done.39
  271.9 8.6 collective-permute-done.48
  300.3 7.9 convolution_convert_fusion
  308.2 6.7 copy.69
  314.9 8.8 reshape.534
  323.7 12.0 %fusion.344 = (bf16[1,512,1,12,64]{1,0,4,3,2:T(2,128)(2,1)}, bf16[1,512,1,12,64]{1,0,4,3,2:T(2,128)(2,1)}, bf16[1,512,1,12,64]{1,0,4,3,2:T(2,128)(2,1)}, bf16[1,...) fusion(bf16[2,512,3,12,64]{1,0,4,3,2:T(2,128)(2,1)} %reshape.534), kind=kLoop, calls=%fused_computation.862 | loop fusion | bytes 9437184 | tf_op jit(solution)/shard_map/slice | solution.py:153
  335.8 7.8 fusion.350
  346.2 11.2 fusion.349
  357.4 6.5 fusion.24
  363.9 6.0 fusion.78
  395.7 13.8 %fusion.22 = (bf16[3072,1024]{0,1:T(8,128)(2,1)}, f32[1024,3072]{1,0:T(8,128)}) fusion(bf16[768,3072]{1,0:T(8,128)(2,1)} %constant_dynamic-update-slice_fusion.10, f32[1024,768]{1,0:T(8,128)S(1)} %get-tuple-element.185, f32[768]{0:T(1024)S(1)} %reshape.554, f32[1024]{0:T(1024)S(1)} %fusion.309), kind=kOutput, calls=%fused_computation.36 | convolution fusion | flops 4862509056 | bytes 26745856 | tf_op jit(solution)/shard_map/dot_general | solution.py:165
  412.6 12.5 %add_convert_fusion = bf16[1024,768]{1,0:T(8,128)(2,1)} fusion(f32[1024,768]{1,0:T(8,128)S(1)} %get-tuple-element.185, bf16[3072,768]{1,0:T(8,128)(2,1)} %constant_dynamic-update-slice_fusion, f32[1024,3072]{1,0:T(8,128)} %get-tuple-element.192), kind=kOutput, calls=%fused_computation.97 | convolution fusion | flops 4861722624 | bytes 22020096 | tf_op jit(solution)/shard_map/dot_general | solution.py:167
  425.1 17.9 %fusion.14 = bf16[1024,3072]{1,0:T(8,128)(2,1)} fusion(f32[1024,3072]{1,0:T(8,128)} %get-tuple-element.192, bf16[1024,768]{1,0:T(8,128)(2,1)} %bitcast_convert_fusion, bf16[3072,768]{1,0:T(8,128)(2,1)} %constant_dynamic-update-slice_fusion), kind=kOutput, calls=%fused_computation.28 | convolution fusion | flops 4894752768 | bytes 25165824 | tf_op jit(solution)/shard_map/dot_general | solution.py:41
  443.0 9.0 multiply_reduce_fusion.2
  452.0 10.8 fusion.334
  469.4 5.9 multiply_reduce_fusion.1
  475.4 6.7 fusion.71
  482.0 8.5 multiply_reduce_fusion
  490.6 26.8 %convert_add_fusion = (f32[12,512,512]{1,2,0:T(8,128)}, bf16[12,512,512]{1,2,0:T(8,128)(2,1)}, bf16[12,512,512]{1,2,0:T(8,128)(2,1)}) fusion(f32[12,512,512]{1,2,0:T(8,128)} %get-tuple-element.188, f32[12,512]{1,0:T(8,128)S(1)} %get-tuple-element.187, f32[12,512,512]{1,2,0:T(8,128)} %copy-done, f32[12,512]{1,0:T(8,128)S(1)} %log_add_fusion.1, ...), kind=kLoop, calls=%fused_computation.37 | loop fusion | flops 34603008 | bytes 75595776 | tf_op jit(solution)/shard_map/add | solution.py:192
  531.2 8.6 copy.109
  550.1 13.0 %copy.89 = f32[12,512,512]{2,1,0:T(8,128)} copy(f32[12,512,512]{1,2,0:T(8,128)} %get-tuple-element.28) | data formatting | bytes 25165824 | tf_op jit(solution)/shard_map/add | solution.py:192
  567.7 9.4 copy.88
  580.9 7.6 fusion.351
  590.6 9.1 fusion.42
  600.4 8.2 fusion.37
  608.7 12.4 %pad.61 = f32[16,512,512]{2,1,0:T(8,128)} pad(f32[12,512,512]{2,1,0:T(8,128)} %copy.89, f32[]{:T(128)} %constant.794.clone.1), padding=0_4x0_0x0_0 | pad | bytes 29360132
  621.1 15.5 %copy.124 = f32[2,8,512,512]{3,1,2,0:T(8,128)S(1)} copy(f32[2,8,512,512]{3,2,1,0:T(8,128)} %bitcast.855) | data formatting | bytes 33554432
  636.6 17.8 %fusion.4 = f32[32,12]{1,0:T(8,128)S(1)} fusion(f32[12,262144]{1,0:T(8,128)S(1)} %bitcast.848, s32[262144]{0:T(1024)S(1)} %copy-done.15), kind=kOutput, calls=%fused_computation.15 | convolution fusion | flops 1216348160 | bytes 13633024 | tf_op jit(solution)/shard_map/dot_general | solution.py:199
  658.0 7.6 fusion.352
  684.7 8.0 collective-permute-done.64
  693.9 21.2 %collective-permute-done.66 = bf16[256,768]{1,0:T(8,128)(2,1)S(1)} collective-permute-done((bf16[256,768]{1,0:T(8,128)(2,1)S(1)}, bf16[256,768]{1,0:T(8,128)(2,1)S(1)}, u32[]{:S(2)}, u32[]{:S(2)}) %collective-permute-start.66) | collective-permute-done | bytes 393248 | tf_op jit(solution)/shard_map/ppermute | solution.py:46
  721.1 17.1 %fusion.3 = f32[4096,768]{1,0:T(8,128)} fusion(bf16[2048,768]{1,0:T(8,128)(2,1)S(1)} %constant_dynamic-update-slice_fusion.51, s32[2048]{0:T(1024)S(1)} %copy-done.79), kind=kOutput, calls=%fused_computation.14 | convolution fusion | flops 12893290496 | bytes 15736832 | tf_op jit(solution)/shard_map/dot_general | solution.py:328
  794.4 5.2 collective-permute-start.71
  808.0 5.3 collective-permute-start.72
  822.8 5.7 collective-permute-start.73
  1008.8 5.7 collective-permute-start.79
  1014.5 5.4 collective-permute-done.97
  1187.1 10.0 slice.346
  (912 shorter events, 717.9 us)
Async XLA Ops:
  2.2 149.4 %collective-permute-start.17 = (bf16[1,2304]{1,0:T(2,128)(2,1)S(1)}, bf16[1,2304]{1,0:T(2,128)(2,1)}, u32[]{:S(2)}, u32[]{:S(2)}) collective-permute-start(bf16[1,2304]{1,0:T(2,128)(2,1)S(1)} %reshape.533), channel_id=1, source_target_pairs={{0,1},{1,0},{2,3},{3,2},{4,5},{5,4},{6,7},{7,6},{8,9},{9,8},{10,11... | collective-permute-start | bytes 13832 | tf_op jit(solution)/shard_map/ppermute | solution.py:46
  2.8 143.3 %collective-permute-start.15 = (bf16[1,2304]{1,0:T(2,128)(2,1)S(1)}, bf16[1,2304]{1,0:T(2,128)(2,1)}, u32[]{:S(2)}, u32[]{:S(2)}) collective-permute-start(bf16[1,2304]{1,0:T(2,128)(2,1)S(1)} %reshape.533), channel_id=1, source_target_pairs={{0,4},{1,5},{2,6},{3,7},{4,0},{5,1},{6,2},{7,3},{8,12},{9,13},{10,... | collective-permute-start | bytes 13832 | tf_op jit(solution)/shard_map/ppermute | solution.py:46
  5.4 131.2 %collective-permute-start.14 = (bf16[1,2304]{1,0:T(2,128)(2,1)S(1)}, bf16[1,2304]{1,0:T(2,128)(2,1)}, u32[]{:S(2)}, u32[]{:S(2)}) collective-permute-start(bf16[1,2304]{1,0:T(2,128)(2,1)S(1)} %reshape.533), channel_id=1, source_target_pairs={{0,2},{1,3},{2,0},{3,1},{4,6},{5,7},{6,4},{7,5},{8,10},{9,11},{10,... | collective-permute-start | bytes 13832 | tf_op jit(solution)/shard_map/ppermute | solution.py:46
  8.2 39.7 %collective-permute-start.57 = (f32[16]{0:T(128)}, f32[16]{0:T(128)}, u32[]{:S(2)}, u32[]{:S(2)}) collective-permute-start(f32[16]{0:T(128)} %convert_reduce_fusion), channel_id=1, source_target_pairs={{0,1},{1,0},{2,3},{3,2},{4,5},{5,4},{6,7},{7,6},{8,9},{9,8},{10,11... | collective-permute-start | bytes 200 | tf_op jit(solution)/shard_map/ppermute | solution.py:46
  8.2 181.3 %collective-permute-start.30 = (bf16[96,768]{1,0:T(8,128)(2,1)}, bf16[96,768]{1,0:T(8,128)(2,1)}, u32[]{:S(2)}, u32[]{:S(2)}) collective-permute-start(bf16[96,768]{1,0:T(8,128)(2,1)} %param.26), channel_id=1, source_target_pairs={{0,2},{1,3},{2,0},{3,1},{4,6},{5,7},{6,4},{7,5},{8,10},{9,11},{10,... | collective-permute-start | bytes 442376 | tf_op jit(solution)/shard_map/ppermute | solution.py:46
  151.7 48.0 %collective-permute-start.34 = (bf16[96,768]{1,0:T(8,128)(2,1)}, bf16[96,768]{1,0:T(8,128)(2,1)}, u32[]{:S(2)}, u32[]{:S(2)}) collective-permute-start(bf16[96,768]{1,0:T(8,128)(2,1)} %param.26), channel_id=1, source_target_pairs={{0,1},{1,0},{2,3},{3,2},{4,5},{5,4},{6,7},{7,6},{8,9},{9,8},{10,11... | collective-permute-start | bytes 442376 | tf_op jit(solution)/shard_map/ppermute | solution.py:46
  153.2 35.3 %collective-permute-start.31 = (bf16[96,768]{1,0:T(8,128)(2,1)}, bf16[96,768]{1,0:T(8,128)(2,1)}, u32[]{:S(2)}, u32[]{:S(2)}) collective-permute-start(bf16[96,768]{1,0:T(8,128)(2,1)} %param.26), channel_id=1, source_target_pairs={{0,4},{1,5},{2,6},{3,7},{4,0},{5,1},{6,2},{7,3},{8,12},{9,13},{10,... | collective-permute-start | bytes 442376 | tf_op jit(solution)/shard_map/ppermute | solution.py:46
  155.1 136.3 %collective-permute-start.25 = (bf16[96,2304]{1,0:T(8,128)(2,1)}, bf16[96,2304]{1,0:T(8,128)(2,1)}, u32[]{:S(2)}, u32[]{:S(2)}) collective-permute-start(bf16[96,2304]{1,0:T(8,128)(2,1)} %constant_dynamic-update-slice_fusion.47), channel_id=1, source_target_pairs={{0,1},{1,0},{2,3},{3,2},{4,5},{5,4},{6,7},{7,6},{8,9},{9,8},{10,11... | collective-permute-start | bytes 1327112 | tf_op jit(solution)/shard_map/ppermute | solution.py:46
  156.7 51.4 %collective-permute-start.3 = (bf16[256,768]{1,0:T(8,128)(2,1)}, bf16[256,768]{1,0:T(8,128)(2,1)S(1)}, u32[]{:S(2)}, u32[]{:S(2)}) collective-permute-start(bf16[256,768]{1,0:T(8,128)(2,1)} %broadcast_select_fusion.6), channel_id=1, source_target_pairs={{0,2},{1,3},{2,0},{3,1},{4,6},{5,7},{6,4},{7,5},{8,10},{9,11},{10,... | collective-permute-start | bytes 1179656 | tf_op jit(solution)/shard_map/ppermute | solution.py:46
  205.7 29.0 %collective-permute-start.7 = (bf16[256,768]{1,0:T(8,128)(2,1)}, bf16[256,768]{1,0:T(8,128)(2,1)S(1)}, u32[]{:S(2)}, u32[]{:S(2)}) collective-permute-start(bf16[256,768]{1,0:T(8,128)(2,1)} %broadcast_select_fusion.4), channel_id=1, source_target_pairs={{0,4},{1,5},{2,6},{3,7},{4,0},{5,1},{6,2},{7,3},{8,12},{9,13},{10,... | collective-permute-start | bytes 1179656 | tf_op jit(solution)/shard_map/ppermute | solution.py:46
  207.4 34.6 %collective-permute-start.9 = (bf16[256,768]{1,0:T(8,128)(2,1)}, bf16[256,768]{1,0:T(8,128)(2,1)S(1)}, u32[]{:S(2)}, u32[]{:S(2)}) collective-permute-start(bf16[256,768]{1,0:T(8,128)(2,1)} %broadcast_select_fusion.3), channel_id=1, source_target_pairs={{0,5},{1,4},{2,7},{3,6},{4,1},{5,0},{6,3},{7,2},{8,13},{9,12},{10,... | collective-permute-start | bytes 1179656 | tf_op jit(solution)/shard_map/ppermute | solution.py:46
  208.1 35.2 %collective-permute-start.11 = (bf16[256,768]{1,0:T(8,128)(2,1)}, bf16[256,768]{1,0:T(8,128)(2,1)S(1)}, u32[]{:S(2)}, u32[]{:S(2)}) collective-permute-start(bf16[256,768]{1,0:T(8,128)(2,1)} %broadcast_select_fusion.2), channel_id=1, source_target_pairs={{0,6},{1,7},{2,4},{3,5},{4,2},{5,3},{6,0},{7,1},{8,14},{9,15},{10,... | collective-permute-start | bytes 1179656 | tf_op jit(solution)/shard_map/ppermute | solution.py:46
  213.2 31.0 %collective-permute-start.13 = (bf16[256,768]{1,0:T(8,128)(2,1)S(1)}, bf16[256,768]{1,0:T(8,128)(2,1)S(1)}, u32[]{:S(2)}, u32[]{:S(2)}) collective-permute-start(bf16[256,768]{1,0:T(8,128)(2,1)S(1)} %copy-done.44), channel_id=1, source_target_pairs={{0,7},{1,6},{2,5},{3,4},{4,3},{5,2},{6,1},{7,0},{8,15},{9,14},{10,... | collective-permute-start | bytes 1179656 | tf_op jit(solution)/shard_map/ppermute | solution.py:46
  243.3 24.7 %collective-permute-start.39 = (bf16[96,3072]{1,0:T(8,128)(2,1)}, bf16[96,3072]{1,0:T(8,128)(2,1)}, u32[]{:S(2)}, u32[]{:S(2)}) collective-permute-start(bf16[96,3072]{1,0:T(8,128)(2,1)} %param.28), channel_id=1, source_target_pairs={{0,2},{1,3},{2,0},{3,1},{4,6},{5,7},{6,4},{7,5},{8,10},{9,11},{10,... | collective-permute-start | bytes 1769480 | tf_op jit(solution)/shard_map/ppermute | solution.py:46
  244.2 25.6 %collective-permute-start.40 = (bf16[96,3072]{1,0:T(8,128)(2,1)}, bf16[96,3072]{1,0:T(8,128)(2,1)}, u32[]{:S(2)}, u32[]{:S(2)}) collective-permute-start(bf16[96,3072]{1,0:T(8,128)(2,1)} %param.28), channel_id=1, source_target_pairs={{0,4},{1,5},{2,6},{3,7},{4,0},{5,1},{6,2},{7,3},{8,12},{9,13},{10,... | collective-permute-start | bytes 1769480 | tf_op jit(solution)/shard_map/ppermute | solution.py:46
  252.7 27.8 %collective-permute-start.48 = (bf16[384,768]{1,0:T(8,128)(2,1)}, bf16[384,768]{1,0:T(8,128)(2,1)S(1)}, u32[]{:S(2)}, u32[]{:S(2)}) collective-permute-start(bf16[384,768]{1,0:T(8,128)(2,1)} %param.29), channel_id=1, source_target_pairs={{0,2},{1,3},{2,0},{3,1},{4,6},{5,7},{6,4},{7,5},{8,10},{9,11},{10,... | collective-permute-start | bytes 1769480 | tf_op jit(solution)/shard_map/ppermute | solution.py:46
  255.3 26.2 %collective-permute-start.49 = (bf16[384,768]{1,0:T(8,128)(2,1)}, bf16[384,768]{1,0:T(8,128)(2,1)S(1)}, u32[]{:S(2)}, u32[]{:S(2)}) collective-permute-start(bf16[384,768]{1,0:T(8,128)(2,1)} %param.29), channel_id=1, source_target_pairs={{0,4},{1,5},{2,6},{3,7},{4,0},{5,1},{6,2},{7,3},{8,12},{9,13},{10,... | collective-permute-start | bytes 1769480 | tf_op jit(solution)/shard_map/ppermute | solution.py:46
  268.0 115.4 %collective-permute-start.43 = (bf16[96,3072]{1,0:T(8,128)(2,1)}, bf16[96,3072]{1,0:T(8,128)(2,1)}, u32[]{:S(2)}, u32[]{:S(2)}) collective-permute-start(bf16[96,3072]{1,0:T(8,128)(2,1)} %param.28), channel_id=1, source_target_pairs={{0,1},{1,0},{2,3},{3,2},{4,5},{5,4},{6,7},{7,6},{8,9},{9,8},{10,11... | collective-permute-start | bytes 1769480 | tf_op jit(solution)/shard_map/ppermute | solution.py:46
  269.7 119.6 %collective-permute-start.52 = (bf16[384,768]{1,0:T(8,128)(2,1)}, bf16[384,768]{1,0:T(8,128)(2,1)}, u32[]{:S(2)}, u32[]{:S(2)}) collective-permute-start(bf16[384,768]{1,0:T(8,128)(2,1)} %param.29), channel_id=1, source_target_pairs={{0,1},{1,0},{2,3},{3,2},{4,5},{5,4},{6,7},{7,6},{8,9},{9,8},{10,11... | collective-permute-start | bytes 1769480 | tf_op jit(solution)/shard_map/ppermute | solution.py:46
  291.4 84.4 %collective-permute-start.42 = (bf16[48,3072]{1,0:T(8,128)(2,1)}, bf16[48,3072]{1,0:T(8,128)(2,1)}, u32[]{:S(2)}, u32[]{:S(2)}) collective-permute-start(bf16[48,3072]{1,0:T(8,128)(2,1)} %slice.333), channel_id=1, source_target_pairs={{0,4},{1,5},{2,6},{3,7},{4,0},{5,1},{6,2},{7,3},{8,12},{9,13},{10,... | collective-permute-start | bytes 884744 | tf_op jit(solution)/shard_map/ppermute | solution.py:46
  293.7 78.8 %collective-permute-start.41 = (bf16[48,3072]{1,0:T(8,128)(2,1)}, bf16[48,3072]{1,0:T(8,128)(2,1)}, u32[]{:S(2)}, u32[]{:S(2)}) collective-permute-start(bf16[48,3072]{1,0:T(8,128)(2,1)} %slice.332), channel_id=1, source_target_pairs={{0,2},{1,3},{2,0},{3,1},{4,6},{5,7},{6,4},{7,5},{8,10},{9,11},{10,... | collective-permute-start | bytes 884744 | tf_op jit(solution)/shard_map/ppermute | solution.py:46
  298.7 88.4 %collective-permute-start.51 = (bf16[192,768]{1,0:T(8,128)(2,1)S(1)}, bf16[192,768]{1,0:T(8,128)(2,1)}, u32[]{:S(2)}, u32[]{:S(2)}) collective-permute-start(bf16[192,768]{1,0:T(8,128)(2,1)S(1)} %slice.335), channel_id=1, source_target_pairs={{0,4},{1,5},{2,6},{3,7},{4,0},{5,1},{6,2},{7,3},{8,12},{9,13},{10,... | collective-permute-start | bytes 884744 | tf_op jit(solution)/shard_map/ppermute | solution.py:46
  386.3 23.1 %collective-permute-start.53 = (bf16[384,768]{1,0:T(8,128)(2,1)S(1)}, bf16[384,768]{1,0:T(8,128)(2,1)S(1)}, u32[]{:S(2)}, u32[]{:S(2)}) collective-permute-start(bf16[384,768]{1,0:T(8,128)(2,1)S(1)} %copy-done.41), channel_id=1, source_target_pairs={{0,1},{1,0},{2,3},{3,2},{4,5},{5,4},{6,7},{7,6},{8,9},{9,8},{10,11... | collective-permute-start | bytes 1769480 | tf_op jit(solution)/shard_map/ppermute | solution.py:46
  387.1 23.2 %collective-permute-start.54 = (bf16[384,768]{1,0:T(8,128)(2,1)S(1)}, bf16[384,768]{1,0:T(8,128)(2,1)S(1)}, u32[]{:S(2)}, u32[]{:S(2)}) collective-permute-start(bf16[384,768]{1,0:T(8,128)(2,1)S(1)} %copy-done.43), channel_id=1, source_target_pairs={{0,1},{1,0},{2,3},{3,2},{4,5},{5,4},{6,7},{7,6},{8,9},{9,8},{10,11... | collective-permute-start | bytes 1769480 | tf_op jit(solution)/shard_map/ppermute | solution.py:46
  546.0 192.2 %collective-permute-start.129 = (bf16[4,96,768]{2,1,0:T(8,128)(2,1)}, bf16[4,96,768]{2,1,0:T(8,128)(2,1)}, u32[]{:S(2)}, u32[]{:S(2)}) collective-permute-start(bf16[4,96,768]{2,1,0:T(8,128)(2,1)} %fusion.201), channel_id=1, source_target_pairs={{0,1},{1,0},{2,3},{3,2},{4,5},{5,4},{6,7},{7,6},{8,9},{9,8},{10,11... | collective-permute-start | bytes 1769480 | tf_op jit(solution)/shard_map/ppermute | solution.py:46
  655.3 27.3 %collective-permute-start.63 = (bf16[256,768]{1,0:T(8,128)(2,1)S(1)}, bf16[256,768]{1,0:T(8,128)(2,1)S(1)}, u32[]{:S(2)}, u32[]{:S(2)}) collective-permute-start(bf16[256,768]{1,0:T(8,128)(2,1)S(1)} %get-tuple-element.87), channel_id=1, source_target_pairs={{0,2},{1,3},{2,0},{3,1},{4,6},{5,7},{6,4},{7,5},{8,10},{9,11},{10,... | collective-permute-start | bytes 1179656 | tf_op jit(solution)/shard_map/ppermute | solution.py:46
  681.3 33.7 %collective-permute-start.66 = (bf16[256,768]{1,0:T(8,128)(2,1)S(1)}, bf16[256,768]{1,0:T(8,128)(2,1)S(1)}, u32[]{:S(2)}, u32[]{:S(2)}) collective-permute-start(bf16[256,768]{1,0:T(8,128)(2,1)S(1)} %get-tuple-element.84), channel_id=1, source_target_pairs={{0,5},{1,4},{2,7},{3,6},{4,1},{5,0},{6,3},{7,2},{8,13},{9,12},{10,... | collective-permute-start | bytes 1179656 | tf_op jit(solution)/shard_map/ppermute | solution.py:46
  682.7 33.7 %collective-permute-start.67 = (bf16[256,768]{1,0:T(8,128)(2,1)S(1)}, bf16[256,768]{1,0:T(8,128)(2,1)S(1)}, u32[]{:S(2)}, u32[]{:S(2)}) collective-permute-start(bf16[256,768]{1,0:T(8,128)(2,1)S(1)} %get-tuple-element.83), channel_id=1, source_target_pairs={{0,6},{1,7},{2,4},{3,5},{4,2},{5,3},{6,0},{7,1},{8,14},{9,15},{10,... | collective-permute-start | bytes 1179656 | tf_op jit(solution)/shard_map/ppermute | solution.py:46
  692.7 28.3 %collective-permute-start.68 = (bf16[256,768]{1,0:T(8,128)(2,1)S(1)}, bf16[256,768]{1,0:T(8,128)(2,1)S(1)}, u32[]{:S(2)}, u32[]{:S(2)}) collective-permute-start(bf16[256,768]{1,0:T(8,128)(2,1)S(1)} %get-tuple-element.82), channel_id=1, source_target_pairs={{0,7},{1,6},{2,5},{3,4},{4,3},{5,2},{6,1},{7,0},{8,15},{9,14},{10,... | collective-permute-start | bytes 1179656 | tf_op jit(solution)/shard_map/ppermute | solution.py:46
  693.1 120.2 %collective-permute-start.116 = (bf16[4,96,2304]{2,1,0:T(8,128)(2,1)}, bf16[4,96,2304]{2,1,0:T(8,128)(2,1)}, u32[]{:S(2)}, u32[]{:S(2)}) collective-permute-start(bf16[4,96,2304]{2,1,0:T(8,128)(2,1)} %fusion.52), channel_id=1, source_target_pairs={{0,1},{1,0},{2,3},{3,2},{4,5},{5,4},{6,7},{7,6},{8,9},{9,8},{10,11... | collective-permute-start | bytes 5308424 | tf_op jit(solution)/shard_map/ppermute | solution.py:46
  715.1 34.7 %collective-permute-start.114 = (bf16[2,128]{1,0:T(2,128)(2,1)S(1)}, bf16[2,128]{1,0:T(2,128)(2,1)S(1)}, u32[]{:S(2)}, u32[]{:S(2)}) collective-permute-start(bf16[2,128]{1,0:T(2,128)(2,1)S(1)} %get-tuple-element.160), channel_id=1, source_target_pairs={{8,0},{16,8},{24,16},{9,1},{17,9},{25,17},{10,2},{18,10},{26,18},{... | collective-permute-start | bytes 1544 | tf_op jit(solution)/shard_map/ppermute | solution.py:113
  716.4 34.4 %collective-permute-start.111 = (bf16[2,128]{1,0:T(2,128)(2,1)S(1)}, bf16[2,128]{1,0:T(2,128)(2,1)S(1)}, u32[]{:S(2)}, u32[]{:S(2)}) collective-permute-start(bf16[2,128]{1,0:T(2,128)(2,1)S(1)} %get-tuple-element.161), channel_id=1, source_target_pairs={{0,8},{8,16},{16,24},{1,9},{9,17},{17,25},{2,10},{10,18},{18,26},{... | collective-permute-start | bytes 1544 | tf_op jit(solution)/shard_map/ppermute | solution.py:113
  800.2 30.6 %collective-permute-start.157 = (bf16[4,384,768]{2,1,0:T(8,128)(2,1)}, bf16[4,384,768]{2,1,0:T(8,128)(2,1)S(1)}, u32[]{:S(2)}, u32[]{:S(2)}) collective-permute-start(bf16[4,384,768]{2,1,0:T(8,128)(2,1)} %fusion.51), channel_id=1, source_target_pairs={{0,1},{1,0},{2,3},{3,2},{4,5},{5,4},{6,7},{7,6},{8,9},{9,8},{10,11... | collective-permute-start | bytes 7077896 | tf_op jit(solution)/shard_map/ppermute | solution.py:46
  800.2 32.3 %collective-permute-start.140 = (bf16[4,96,3072]{2,1,0:T(8,128)(2,1)}, bf16[4,96,3072]{2,1,0:T(8,128)(2,1)S(1)}, u32[]{:S(2)}, u32[]{:S(2)}) collective-permute-start(bf16[4,96,3072]{2,1,0:T(8,128)(2,1)} %fusion.50), channel_id=1, source_target_pairs={{0,1},{1,0},{2,3},{3,2},{4,5},{5,4},{6,7},{7,6},{8,9},{9,8},{10,11... | collective-permute-start | bytes 7077896 | tf_op jit(solution)/shard_map/ppermute | solution.py:46
  821.5 25.1 %collective-permute-start.91 = (bf16[256,768]{1,0:T(8,128)(2,1)}, bf16[256,768]{1,0:T(8,128)(2,1)}, u32[]{:S(2)}, u32[]{:S(2)}) collective-permute-start(bf16[256,768]{1,0:T(8,128)(2,1)} %get-tuple-element.61), channel_id=1, source_target_pairs={{8,0},{16,8},{24,16},{9,1},{17,9},{25,17},{10,2},{18,10},{26,18},{... | collective-permute-start | bytes 1179656 | tf_op jit(solution)/shard_map/ppermute | solution.py:113
  822.8 25.1 %collective-permute-start.73 = (bf16[256,768]{1,0:T(8,128)(2,1)}, bf16[256,768]{1,0:T(8,128)(2,1)}, u32[]{:S(2)}, u32[]{:S(2)}) collective-permute-start(bf16[256,768]{1,0:T(8,128)(2,1)} %get-tuple-element.62), channel_id=1, source_target_pairs={{0,8},{8,16},{16,24},{1,9},{9,17},{17,25},{2,10},{10,18},{18,26},{... | collective-permute-start | bytes 1179656 | tf_op jit(solution)/shard_map/ppermute | solution.py:113
  861.9 39.2 %collective-permute-start.159 = (bf16[384,768]{1,0:T(8,128)(2,1)S(1)}, bf16[384,768]{1,0:T(8,128)(2,1)S(1)}, u32[]{:S(2)}, u32[]{:S(2)}) collective-permute-start(bf16[384,768]{1,0:T(8,128)(2,1)S(1)} %get-tuple-element.70), channel_id=1, source_target_pairs={{0,2},{1,3},{2,0},{3,1},{4,6},{5,7},{6,4},{7,5},{8,10},{9,11},{10,... | collective-permute-start | bytes 1769480 | tf_op jit(solution)/shard_map/ppermute | solution.py:46
  871.0 35.1 %collective-permute-start.161 = (bf16[384,768]{1,0:T(8,128)(2,1)S(1)}, bf16[384,768]{1,0:T(8,128)(2,1)S(1)}, u32[]{:S(2)}, u32[]{:S(2)}) collective-permute-start(bf16[384,768]{1,0:T(8,128)(2,1)S(1)} %get-tuple-element.71), channel_id=1, source_target_pairs={{0,4},{1,5},{2,6},{3,7},{4,0},{5,1},{6,2},{7,3},{8,12},{9,13},{10,... | collective-permute-start | bytes 1769480 | tf_op jit(solution)/shard_map/ppermute | solution.py:46
  874.1 33.6 %collective-permute-start.142 = (bf16[96,3072]{1,0:T(8,128)(2,1)S(1)}, bf16[96,3072]{1,0:T(8,128)(2,1)S(1)}, u32[]{:S(2)}, u32[]{:S(2)}) collective-permute-start(bf16[96,3072]{1,0:T(8,128)(2,1)S(1)} %get-tuple-element.72), channel_id=1, source_target_pairs={{0,2},{1,3},{2,0},{3,1},{4,6},{5,7},{6,4},{7,5},{8,10},{9,11},{10,... | collective-permute-start | bytes 1769480 | tf_op jit(solution)/shard_map/ppermute | solution.py:46
  906.1 39.8 %collective-permute-start.94 = (bf16[256,768]{1,0:T(8,128)(2,1)S(1)}, bf16[256,768]{1,0:T(8,128)(2,1)S(1)}, u32[]{:S(2)}, u32[]{:S(2)}) collective-permute-start(bf16[256,768]{1,0:T(8,128)(2,1)S(1)} %get-tuple-element.55), channel_id=1, source_target_pairs={{8,0},{16,8},{24,16},{9,1},{17,9},{25,17},{10,2},{18,10},{26,18},{... | collective-permute-start | bytes 1179656 | tf_op jit(solution)/shard_map/ppermute | solution.py:113
  907.7 42.9 %collective-permute-start.76 = (bf16[256,768]{1,0:T(8,128)(2,1)S(1)}, bf16[256,768]{1,0:T(8,128)(2,1)S(1)}, u32[]{:S(2)}, u32[]{:S(2)}) collective-permute-start(bf16[256,768]{1,0:T(8,128)(2,1)S(1)} %get-tuple-element.56), channel_id=1, source_target_pairs={{0,8},{8,16},{16,24},{1,9},{9,17},{17,25},{2,10},{10,18},{18,26},{... | collective-permute-start | bytes 1179656 | tf_op jit(solution)/shard_map/ppermute | solution.py:113
  952.2 25.8 %collective-permute-start.95 = (bf16[256,768]{1,0:T(8,128)(2,1)S(1)}, bf16[256,768]{1,0:T(8,128)(2,1)S(1)}, u32[]{:S(2)}, u32[]{:S(2)}) collective-permute-start(bf16[256,768]{1,0:T(8,128)(2,1)S(1)} %get-tuple-element.53), channel_id=1, source_target_pairs={{8,0},{16,8},{24,16},{9,1},{17,9},{25,17},{10,2},{18,10},{26,18},{... | collective-permute-start | bytes 1179656 | tf_op jit(solution)/shard_map/ppermute | solution.py:113
  953.5 29.1 %collective-permute-start.77 = (bf16[256,768]{1,0:T(8,128)(2,1)S(1)}, bf16[256,768]{1,0:T(8,128)(2,1)S(1)}, u32[]{:S(2)}, u32[]{:S(2)}) collective-permute-start(bf16[256,768]{1,0:T(8,128)(2,1)S(1)} %get-tuple-element.54), channel_id=1, source_target_pairs={{0,8},{8,16},{16,24},{1,9},{9,17},{17,25},{2,10},{10,18},{18,26},{... | collective-permute-start | bytes 1179656 | tf_op jit(solution)/shard_map/ppermute | solution.py:113
  990.2 105.2 %collective-permute-start.173 = (bf16[96,768]{1,0:T(8,128)(2,1)S(1)}, bf16[96,768]{1,0:T(8,128)(2,1)S(1)}, u32[]{:S(2)}, u32[]{:S(2)}) collective-permute-start(bf16[96,768]{1,0:T(8,128)(2,1)S(1)} %get-tuple-element.95), channel_id=1, source_target_pairs={{8,0},{16,8},{24,16},{9,1},{17,9},{25,17},{10,2},{18,10},{26,18},{... | collective-permute-start | bytes 442376 | tf_op jit(solution)/shard_map/ppermute | solution.py:113
  991.8 50.8 %collective-permute-start.167 = (bf16[96,768]{1,0:T(8,128)(2,1)S(1)}, bf16[96,768]{1,0:T(8,128)(2,1)S(1)}, u32[]{:S(2)}, u32[]{:S(2)}) collective-permute-start(bf16[96,768]{1,0:T(8,128)(2,1)S(1)} %get-tuple-element.96), channel_id=1, source_target_pairs={{0,8},{8,16},{16,24},{1,9},{9,17},{17,25},{2,10},{10,18},{18,26},{... | collective-permute-start | bytes 442376 | tf_op jit(solution)/shard_map/ppermute | solution.py:113
  1004.0 38.5 %collective-permute-start.156 = (bf16[24,3072]{1,0:T(8,128)(2,1)S(1)}, bf16[24,3072]{1,0:T(8,128)(2,1)S(1)}, u32[]{:S(2)}, u32[]{:S(2)}) collective-permute-start(bf16[24,3072]{1,0:T(8,128)(2,1)S(1)} %get-tuple-element.106), channel_id=1, source_target_pairs={{8,0},{16,8},{24,16},{9,1},{17,9},{25,17},{10,2},{18,10},{26,18},{... | collective-permute-start | bytes 442376 | tf_op jit(solution)/shard_map/ppermute | solution.py:113
  1103.1 83.0 %collective-permute-start.104 = (bf16[256,768]{1,0:T(8,128)(2,1)S(1)}, bf16[256,768]{1,0:T(8,128)(2,1)S(1)}, u32[]{:S(2)}, u32[]{:S(2)}) collective-permute-start(bf16[256,768]{1,0:T(8,128)(2,1)S(1)} %get-tuple-element.35), channel_id=1, source_target_pairs={{8,0},{16,8},{24,16},{9,1},{17,9},{25,17},{10,2},{18,10},{26,18},{... | collective-permute-start | bytes 1179656 | tf_op jit(solution)/shard_map/ppermute | solution.py:113
  1104.4 41.3 %collective-permute-start.86 = (bf16[256,768]{1,0:T(8,128)(2,1)S(1)}, bf16[256,768]{1,0:T(8,128)(2,1)S(1)}, u32[]{:S(2)}, u32[]{:S(2)}) collective-permute-start(bf16[256,768]{1,0:T(8,128)(2,1)S(1)} %get-tuple-element.36), channel_id=1, source_target_pairs={{0,8},{8,16},{16,24},{1,9},{9,17},{17,25},{2,10},{10,18},{18,26},{... | collective-permute-start | bytes 1179656 | tf_op jit(solution)/shard_map/ppermute | solution.py:113
  (215 other events, 2641.0 us)

commit v2 on v1

v2 whole, which is shorter than its diff:
```python
import functools
import jax
import jax.numpy as jnp
from jax import lax
from jax.experimental import pallas as pl
from jax.experimental.pallas import tpu as pltpu
from jax.sharding import PartitionSpec as P

EPS = 1e-06
NEG = -1000000000.0
LIMITS = (12, 16, 23, 32, 46, 64, 91)
HIGH = lax.Precision.HIGHEST
LOW = jnp.bfloat16
F32 = jnp.float32
VMEM_LIMIT = 56 * 1024 * 1024
PAIR = 128
ROOT = (2.0 / 3.141592653589793) ** 0.5
CUBE = 0.044715


def dot(left, right):
    return jnp.dot(left, right, preferred_element_type=F32)


def dot_nt(left, right):
    return lax.dot_general(left, right, (((1,), (1,)), ((), ())), preferred_element_type=F32)


def dot_tn(left, right):
    return lax.dot_general(left, right, (((0,), (0,)), ((), ())), preferred_element_type=F32)


def params():
    return pltpu.CompilerParams(vmem_limit_bytes=VMEM_LIMIT)


def half_lanes(size):
    return lax.broadcasted_iota(jnp.int32, (size, PAIR), 1) < PAIR // 2


def spread_bias(diagonal, seq_len):
    wide = jnp.broadcast_to(diagonal, (seq_len, 2 * seq_len))
    wide = pltpu.roll(wide, seq_len + 1, 1, stride=1, stride_axis=0)
    return wide[:, :seq_len]


def gather_bias(grad):
    seq_len = grad.shape[0]
    blocks = seq_len // PAIR
    total = None
    for block in range(blocks):
        ahead = PAIR * (blocks - 1 - block)
        parts = [grad[block * PAIR : (block + 1) * PAIR, :], jnp.zeros((PAIR, seq_len - ahead), F32)]
        if ahead:
            parts = [jnp.zeros((PAIR, ahead), F32)] + parts
        wide = jnp.concatenate(parts, axis=1)
        total = wide if total is None else total + wide
    eight = None
    for group in range(PAIR // 8):
        moved = pltpu.roll(total[8 * group : 8 * group + 8, :], PAIR - 8 - 8 * group, 1)
        eight = moved if eight is None else eight + moved
    return sum(pltpu.roll(eight[sub : sub + 1, :], 7 - sub, 1) for sub in range(8))


def attend_kernel(lengths_ref, diagonal_ref, query_ref, key_ref, value_ref, out_ref, log_ref):
    rows = lengths_ref.shape[0]
    seq_len = query_ref.shape[0] // rows
    first = half_lanes(seq_len)
    key_at = lax.broadcasted_iota(jnp.int32, (seq_len, 1), 0)
    results = [[None, None] for _ in range(rows)]
    for head in range(2):
        bias = spread_bias(diagonal_ref[0, head : head + 1, :], seq_len)
        for row in range(rows):
            span = pl.ds(row * seq_len, seq_len)
            queries = query_ref[span, :]
            queries = jnp.where(first if head == 0 else ~first, queries, jnp.zeros_like(queries))
            scores = dot_nt(key_ref[span, :], queries) + bias
            scores = jnp.where(key_at < lengths_ref[row], scores, NEG)
            largest = jnp.max(scores, axis=0, keepdims=True)
            raised = jnp.exp(scores - largest)
            totals = jnp.sum(raised, axis=0, keepdims=True)
            probs = (raised * (1.0 / totals)).astype(LOW)
            results[row][head] = dot_tn(probs, value_ref[span, :])
            log_ref[0, 2 * row + head : 2 * row + head + 1, :] = largest + jnp.log(totals)
    for row in range(rows):
        out_ref[pl.ds(row * seq_len, seq_len), :] = jnp.where(first, *results[row]).astype(LOW)


def attend(lengths, diagonal, joint, heads):
    tokens = joint.shape[0]
    pairs = heads // 2
    rows = lengths.shape[0]
    seq_len = tokens // rows
    return pl.pallas_call(
        attend_kernel,
        grid=(pairs,),
        in_specs=[
            pl.BlockSpec(memory_space=pltpu.SMEM),
            pl.BlockSpec((1, 2, 2 * seq_len), lambda p: (p, 0, 0)),
            pl.BlockSpec((tokens, PAIR), lambda p: (0, p)),
            pl.BlockSpec((tokens, PAIR), lambda p: (0, pairs + p)),
            pl.BlockSpec((tokens, PAIR), lambda p: (0, 2 * pairs + p)),
        ],
        out_specs=[
            pl.BlockSpec((tokens, PAIR), lambda p: (0, p)),
            pl.BlockSpec((1, 2 * rows, seq_len), lambda p: (p, 0, 0)),
        ],
        out_shape=[
            jax.ShapeDtypeStruct((tokens, pairs * PAIR), LOW),
            jax.ShapeDtypeStruct((pairs, 2 * rows, seq_len), F32),
        ],
        compiler_params=params(),
        name="attend",
    )(lengths, diagonal.reshape(pairs, 2, 2 * seq_len), joint, joint, joint)


def attend_back_kernel(
    lengths_ref, diagonal_ref, query_ref, key_ref, value_ref, grad_ref, log_ref,
    query_out, key_out, value_out, bias_out,
):
    rows = lengths_ref.shape[0]
    seq_len = query_ref.shape[0] // rows
    first = half_lanes(seq_len)
    key_at = lax.broadcasted_iota(jnp.int32, (seq_len, 1), 0)
    results = [[None, None] for _ in range(rows)]
    for head in range(2):
        bias = spread_bias(diagonal_ref[0, head : head + 1, :], seq_len)
        keep = first if head == 0 else ~first
        total = None
        for row in range(rows):
            span = pl.ds(row * seq_len, seq_len)
            queries = query_ref[span, :]
            keys = key_ref[span, :]
            values = value_ref[span, :]
            grads = grad_ref[span, :]
            only = jnp.where(keep, queries, jnp.zeros_like(queries))
            scores = dot_nt(keys, only) + bias
            scores = jnp.where(key_at < lengths_ref[row], scores, NEG)
            probs = jnp.exp(scores - log_ref[0, 2 * row + head : 2 * row + head + 1, :])
            grad_values = dot(probs.astype(LOW), grads)
            grad_only = jnp.where(keep, grads, jnp.zeros_like(grads))
            grad_probs = dot_nt(values, grad_only)
            weighted = jnp.sum(probs * grad_probs, axis=0, keepdims=True)
            grad_scores = (probs * (grad_probs - weighted)).astype(LOW)
            grad_keys = dot(grad_scores, queries)
            grad_queries = dot_tn(grad_scores, keys)
            wide = grad_scores.astype(F32)
            total = wide if total is None else total + wide
            results[row][head] = (grad_queries, grad_keys, grad_values)
        bias_out[0, head : head + 1, :] = gather_bias(total)
    for row in range(rows):
        span = pl.ds(row * seq_len, seq_len)
        for out_ref, one, two in zip((query_out, key_out, value_out), *results[row]):
            out_ref[span, :] = jnp.where(first, one, two).astype(LOW)


def attend_back(lengths, diagonal, joint, grad_attended, logs, heads):
    tokens = joint.shape[0]
    pairs = heads // 2
    rows = lengths.shape[0]
    seq_len = tokens // rows
    part = pl.BlockSpec((tokens, PAIR), lambda p: (0, p))
    whole = jax.ShapeDtypeStruct((tokens, pairs * PAIR), LOW)
    lines = pl.BlockSpec((1, 2, 2 * seq_len), lambda p: (p, 0, 0))
    outs = pl.pallas_call(
        attend_back_kernel,
        grid=(pairs,),
        in_specs=[
            pl.BlockSpec(memory_space=pltpu.SMEM),
            lines,
            part,
            pl.BlockSpec((tokens, PAIR), lambda p: (0, pairs + p)),
            pl.BlockSpec((tokens, PAIR), lambda p: (0, 2 * pairs + p)),
            part,
            pl.BlockSpec((1, 2 * rows, seq_len), lambda p: (p, 0, 0)),
        ],
        out_specs=[part, part, part, lines],
        out_shape=[whole, whole, whole, jax.ShapeDtypeStruct((pairs, 2, 2 * seq_len), F32)],
        compiler_params=params(),
        name="attend_back",
    )(lengths, diagonal.reshape(pairs, 2, 2 * seq_len), joint, joint, joint, grad_attended, logs)
    return outs[0], outs[1], outs[2], outs[3].reshape(heads, 2 * seq_len)


def load_weights(me, loads, refs, targets, semaphores):
    pending = []
    for number, (source, target, column, relative, shard_rows, first, start, rows) in enumerate(loads):
        into = targets[target]
        width = refs[source].shape[1]
        place = first if relative is None else pl.multiple_of((me ^ relative) * shard_rows + first, 16)
        copy = pltpu.make_async_copy(
            refs[source].at[pl.ds(start, rows), :],
            into.at[pl.ds(place, rows), pl.ds(column, width)],
            semaphores.at[number],
        )
        copy.start()
        pending.append(copy)
    for copy in pending:
        copy.wait()


def plan_loads(pieces, sections):
    loads = []
    for source, (relative, first, part) in enumerate(pieces):
        start = 0
        for target, rows, column, shard_rows, offset in sections:
            low = max(start, first)
            high = min(start + rows, first + part.shape[0])
            if low < high:
                loads.append((source, target, column, relative, shard_rows, offset + low - start, low - first, high - low))
            start += rows
    return loads


def front_kernel(loads, count, me_ref, slot_ref, reply_ref, gain_ref, *rest):
    refs, (x_ref, normed_ref, joint_ref), (weight, semaphores) = rest[:count], rest[count : count + 3], rest[count + 3 :]

    @pl.when(pl.program_id(0) == 0)
    def _():
        load_weights(me_ref[0], loads, refs, [weight], semaphores)

    rows = slot_ref.shape[0]
    slots = reply_ref.shape[0]
    hot = slot_ref[...] == lax.broadcasted_iota(jnp.int32, (rows, slots), 1)
    x = dot(hot.astype(F32).astype(LOW), reply_ref[...])
    x_ref[...] = x.astype(LOW)
    scale = lax.rsqrt(jnp.mean(x * x, axis=-1, keepdims=True) + EPS)
    normed = (x * scale * gain_ref[...]).astype(LOW)
    normed_ref[...] = normed
    joint_ref[...] = dot(normed, weight[...]).astype(LOW)


ANY = pl.BlockSpec(memory_space=pl.ANY)
SMEM = pl.BlockSpec(memory_space=pltpu.SMEM)
BLOCK = 256


def full(shape):
    return pl.BlockSpec(shape, lambda *ids: (0,) * len(shape))


def down(width, rows=BLOCK):
    return pl.BlockSpec((rows, width), lambda i: (i, 0))


def front(me, slot, replies, gain, pieces, loads, width):
    tokens = slot.shape[0]
    model = replies.shape[1]
    return pl.pallas_call(
        functools.partial(front_kernel, loads, len(pieces)),
        grid=(tokens // BLOCK,),
        in_specs=[SMEM, down(1), full(replies.shape), full((1, model))] + [ANY] * len(pieces),
        out_specs=[down(model), down(model), down(width)],
        out_shape=[
            jax.ShapeDtypeStruct((tokens, model), LOW),
            jax.ShapeDtypeStruct((tokens, model), LOW),
            jax.ShapeDtypeStruct((tokens, width), LOW),
        ],
        scratch_shapes=[pltpu.VMEM((model, width), LOW), pltpu.SemaphoreType.DMA((len(loads),))],
        compiler_params=params(),
        name="front",
    )(me, slot, replies, gain, *pieces)


def ffn_kernel(loads, count, me_ref, x_ref, attended_ref, d_out_ref, seed_ref, gain_ref, *rest):
    refs = rest[:count]
    (y_ref, act_ref, grad_pre_ref, grad_low_ref, normed_ref, hidden_out, low_out, attended_out, gain_out) = rest[count : count + 9]
    w_out, w_in, w_back, semaphores = rest[count + 9 :]

    @pl.when(pl.program_id(0) == 0)
    def _():
        load_weights(me_ref[0], loads, refs, [w_out, w_in, w_back], semaphores)
        gain_out[...] = jnp.zeros_like(gain_out)

    hidden = x_ref[...].astype(F32) + dot(attended_ref[...], w_out[...])
    scale = lax.rsqrt(jnp.mean(hidden * hidden, axis=-1, keepdims=True) + EPS)
    unit = hidden * scale
    gain = gain_ref[...]
    normed = (unit * gain).astype(LOW)
    normed_ref[...] = normed
    grad_out = d_out_ref[...].astype(F32) * seed_ref[...]
    grad_low = grad_out.astype(LOW)
    grad_low_ref[...] = grad_low
    result = hidden
    back = jnp.zeros_like(hidden)
    model = hidden.shape[1]
    for start in range(0, w_in.shape[1], model):
        span = pl.ds(start, model)
        pre = dot(normed, w_in[:, span])
        square = pre * pre
        tanh = jnp.tanh(ROOT * (pre + CUBE * square * pre))
        half = 0.5 * (1.0 + tanh)
        act = (pre * half).astype(LOW)
        slope = half + 0.5 * pre * (1.0 - tanh * tanh) * ROOT * (1.0 + 3.0 * CUBE * square)
        act_ref[:, span] = act
        result = result + dot(act, w_back[span, :])
        grad_pre = (dot_nt(grad_low, w_back[span, :]) * slope).astype(LOW)
        grad_pre_ref[:, span] = grad_pre
        back = back + dot_nt(grad_pre, w_in[:, span])
    y_ref[...] = result.astype(LOW)
    gain_out[...] += jnp.sum(back * unit, axis=0, keepdims=True)
    scaled = back * gain
    grad_hidden = grad_out + scale * (scaled - unit * jnp.mean(scaled * unit, axis=-1, keepdims=True))
    hidden_out[...] = grad_hidden
    low = grad_hidden.astype(LOW)
    low_out[...] = low
    attended_out[...] = dot_nt(low, w_out[...]).astype(LOW)


def ffn(me, x, attended, d_out, seed, gain, pieces, loads, inner, ff_width):
    tokens, model = x.shape
    low = jax.ShapeDtypeStruct((tokens, model), LOW)
    wide = jax.ShapeDtypeStruct((tokens, ff_width), LOW)
    return pl.pallas_call(
        functools.partial(ffn_kernel, loads, len(pieces)),
        grid=(tokens // BLOCK,),
        in_specs=[SMEM, down(model), down(inner), down(model), down(1), full((1, model))] + [ANY] * len(pieces),
        out_specs=[
            down(model), down(ff_width), down(ff_width), down(model), down(model), down(model), down(model), down(inner),
            full((1, model)),
        ],
        out_shape=[
            low, wide, wide, low, low, jax.ShapeDtypeStruct((tokens, model), F32), low,
            jax.ShapeDtypeStruct((tokens, inner), LOW), jax.ShapeDtypeStruct((1, model), F32),
        ],
        scratch_shapes=[
            pltpu.VMEM((inner, model), LOW),
            pltpu.VMEM((model, ff_width), LOW),
            pltpu.VMEM((ff_width, model), LOW),
            pltpu.SemaphoreType.DMA((len(loads),)),
        ],
        compiler_params=params(),
        name="ffn",
    )(me, x, attended, d_out, seed, gain, *pieces)


def project_back_kernel(loads, count, me_ref, query_ref, key_ref, value_ref, x_ref, hidden_ref, gain_ref, *rest):
    refs, (out_ref, gain_out), (weight, semaphores) = rest[:count], rest[count : count + 2], rest[count + 2 :]

    @pl.when(pl.program_id(0) == 0)
    def _():
        load_weights(me_ref[0], loads, refs, [weight], semaphores)
        gain_out[...] = jnp.zeros_like(gain_out)

    inner = query_ref.shape[1]
    back = dot_nt(query_ref[...], weight[:, :inner])
    back = back + dot_nt(key_ref[...], weight[:, inner : 2 * inner])
    back = back + dot_nt(value_ref[...], weight[:, 2 * inner :])
    x = x_ref[...].astype(F32)
    scale = lax.rsqrt(jnp.mean(x * x, axis=-1, keepdims=True) + EPS)
    unit = x * scale
    gain_out[...] += jnp.sum(back * unit, axis=0, keepdims=True)
    scaled = back * gain_ref[...]
    grad = hidden_ref[...] + scale * (scaled - unit * jnp.mean(scaled * unit, axis=-1, keepdims=True))
    out_ref[...] = grad.astype(LOW)


def project_back(me, grads, x, grad_hidden, gain, pieces, loads):
    tokens, model = x.shape
    inner = grads[0].shape[1]
    return pl.pallas_call(
        functools.partial(project_back_kernel, loads, len(pieces)),
        grid=(tokens // BLOCK,),
        in_specs=[SMEM] + [down(inner)] * 3 + [down(model), down(model), full((1, model))] + [ANY] * len(pieces),
        out_specs=[down(model), full((1, model))],
        out_shape=[jax.ShapeDtypeStruct((tokens, model), LOW), jax.ShapeDtypeStruct((1, model), F32)],
        scratch_shapes=[pltpu.VMEM((model, 3 * inner), LOW), pltpu.SemaphoreType.DMA((len(loads),))],
        compiler_params=params(),
        name="project_back",
    )(me, *grads, x, grad_hidden, gain, *pieces)


def store_shards(me, value, shards, keep_ref, send_ref, columns):
    rows = value.shape[0] // shards
    for shard in range(shards):
        relative = me ^ shard
        part = value[shard * rows : (shard + 1) * rows, :]

        @pl.when(relative % 2 == 0)
        def _():
            keep_ref[relative // 2, :, columns] = part

        @pl.when(relative % 2 == 1)
        def _():
            send_ref[relative // 2, :, columns] = part.astype(LOW)


def rows_grad_kernel(shards, me_ref, left_ref, *rest):
    rights, (keep_ref, send_ref) = rest[:-2], rest[-2:]
    start = 0
    for right_ref in rights:
        value = dot_tn(left_ref[...], right_ref[...])
        store_shards(me_ref[0], value, shards, keep_ref, send_ref, pl.ds(start, value.shape[1]))
        start += value.shape[1]


def rows_grad(me, left, rights, shards, columns):
    tokens, width = left.shape
    total = sum(right.shape[1] for right in rights)
    steps = total // columns if len(rights) == 1 else 1
    each = columns if len(rights) == 1 else total
    shape = (shards // 2, width // shards, total)
    out = pl.BlockSpec((shards // 2, width // shards, each), lambda i: (0, 0, i))
    return pl.pallas_call(
        functools.partial(rows_grad_kernel, shards),
        grid=(steps,),
        in_specs=[SMEM, full(left.shape)]
        + [pl.BlockSpec((tokens, columns), lambda i: (0, i)) for right in rights],
        out_specs=[out, out],
        out_shape=[jax.ShapeDtypeStruct(shape, F32), jax.ShapeDtypeStruct(shape, LOW)],
        compiler_params=params(),
        name="rows_grad",
    )(me, left, *rights)


def blocks_grad_kernel(me_ref, keep_left, send_left, right_ref, keep_ref, send_ref):
    right = right_ref[...]
    keep_ref[0] = dot_tn(keep_left[...], right)
    send_ref[0] = dot_tn(send_left[...], right).astype(LOW)


def blocks_grad(me, left, right, shards):
    tokens, width = left.shape
    rows = width // shards
    shape = (shards // 2, rows, right.shape[1])
    out = pl.BlockSpec((1, rows, right.shape[1]), lambda i, me: (i, 0, 0))
    return pl.pallas_call(
        blocks_grad_kernel,
        grid_spec=pltpu.PrefetchScalarGridSpec(
            num_scalar_prefetch=1,
            grid=(shards // 2,),
            in_specs=[
                pl.BlockSpec((tokens, rows), lambda i, me: (0, me[0] ^ (2 * i))),
                pl.BlockSpec((tokens, rows), lambda i, me: (0, me[0] ^ (2 * i + 1))),
                pl.BlockSpec(right.shape, lambda i, me: (0, 0)),
            ],
            out_specs=[out, out],
        ),
        out_shape=[jax.ShapeDtypeStruct(shape, F32), jax.ShapeDtypeStruct(shape, LOW)],
        compiler_params=params(),
        name="blocks_grad",
    )(me, left, left, right)


def place_kernel(pieces, slot_ref, token_ref, *outs):
    capacity = outs[0].shape[0]
    tokens = token_ref.shape[0]
    at = lax.broadcasted_iota(jnp.int32, (capacity, tokens), 0)
    for number, out_ref in enumerate(outs):
        hot = (at + number * capacity) == slot_ref[...]
        out_ref[...] = dot(hot.astype(F32).astype(LOW), token_ref[...]).astype(LOW)


def place(slot, tokens, shards, capacity):
    model = tokens.shape[1]
    return pl.pallas_call(
        functools.partial(place_kernel, shards),
        in_specs=[full((1, tokens.shape[0])), full(tokens.shape)],
        out_specs=[full((capacity, model))] * shards,
        out_shape=[jax.ShapeDtypeStruct((capacity, model), LOW)] * shards,
        compiler_params=params(),
        name="place",
    )(slot, tokens)


TABLE_BLOCK = 512


def table_kernel(count, ids_ref, *rest):
    pieces = rest[:count]
    out_ref, stacked = rest[-2:]
    step = pl.program_id(0)

    @pl.when(step == 0)
    def _():
        capacity = pieces[0].shape[0]
        for number, piece in enumerate(pieces):
            stacked[pl.ds(number * capacity, capacity), :] = piece[...]

    rows = out_ref.shape[0]
    at = lax.broadcasted_iota(jnp.int32, (rows, ids_ref.shape[1]), 0) + step * rows
    total = dot((at == ids_ref[...]).astype(F32).astype(LOW), stacked[...])
    if len(rest) > count + 2:
        total = total + rest[count][...]
    out_ref[...] = total


def add_to_table(ids, pieces, before, vshard):
    model = pieces[0].shape[1]
    slots = ids.shape[1]
    more = [] if before is None else [before]
    return pl.pallas_call(
        functools.partial(table_kernel, len(pieces)),
        grid=(pl.cdiv(vshard, TABLE_BLOCK),),
        in_specs=[full(ids.shape)] + [full(pieces[0].shape)] * len(pieces) + [down(model, TABLE_BLOCK)] * len(more),
        out_specs=down(model, TABLE_BLOCK),
        out_shape=jax.ShapeDtypeStruct((vshard, model), F32),
        input_output_aliases={1 + len(pieces): 0} if more else {},
        scratch_shapes=[pltpu.VMEM((slots, model), LOW)],
        compiler_params=params(),
        name="table_rows",
    )(ids, *pieces, *more)


def flip(value, bits):
    shards = lax.axis_size("fsdp")
    return lax.ppermute(value, "fsdp", [(i, i ^ bits) for i in range(shards)])


def flip_line(value, bits):
    groups = lax.axis_size("dp")
    return lax.ppermute(value, "dp", [(i, i ^ bits) for i in range(groups)])


def gather_pieces(own):
    half = own.shape[0] // 32 * 16
    by_x = flip(own, 2)
    by_y = flip(own, 4)
    pieces = [(0, 0, own), (2, 0, by_x), (4, 0, by_y)]
    pieces += [(6, 0, flip(by_y[:half], 2)), (6, half, flip(by_x[half:], 4))]
    return pieces + [(bits ^ 1, first, flip(part, 1)) for bits, first, part in pieces]


def scatter_sum(keep, send):
    shards = lax.axis_size("fsdp")
    rows, columns = keep.shape[1:]
    mine = keep + flip(send, 1).astype(F32)
    if shards == 8:
        half = rows // 32 * 16
        across = mine[3].astype(LOW)
        from_x = flip(across[:half], 2).astype(F32)
        from_y = flip(across[half:], 4).astype(F32)
        to_y = mine[2] + jnp.concatenate([from_x, jnp.zeros((rows - half, columns), F32)])
        to_x = mine[1] + jnp.concatenate([jnp.zeros((half, columns), F32), from_y])
        return mine[0] + flip(to_x.astype(LOW), 2).astype(F32) + flip(to_y.astype(LOW), 4).astype(F32)
    total = mine[0]
    for relative in range(1, shards // 2):
        total = total + flip(mine[relative].astype(LOW), 2 * relative).astype(F32)
    return total


def bucket_of(offset):
    distance = jnp.abs(offset)
    far_bucket = 8 + sum(((distance >= limit).astype(jnp.int32) for limit in LIMITS))
    upper = jnp.where(offset > 0, 16, 0).astype(jnp.int32)
    return upper + jnp.where(distance < 8, distance, far_bucket)


def per_device(
    token_ids,
    task_ids,
    lengths,
    instruction,
    table,
    attn_gain,
    w_query,
    w_key,
    w_value,
    w_out,
    ffn_gain,
    w_in,
    w_back,
    rel_bias,
    d_out,
):
    rows_dev, seq_len = token_ids.shape
    vshard, model = table.shape
    inner = w_query.shape[1]
    ff_width = w_in.shape[1]
    heads = rel_bias.shape[1]
    shards = lax.axis_size("fsdp")
    groups = lax.axis_size("dp")
    me = lax.axis_index("fsdp")
    at = lax.axis_index("dp")
    me_ref = me.astype(jnp.int32).reshape(1)
    tokens = rows_dev * seq_len
    capacity = 2 * tokens // shards
    task_count = rows_dev * groups * shards // 4
    own_gain = attn_gain.shape[0]
    buckets = rel_bias.shape[0] * shards

    flat_ids = token_ids.reshape(tokens)
    owner = flat_ids // vshard
    local_row = flat_ids - owner * vshard
    relative = owner ^ me
    relative_hot = (relative[:, None] == jnp.arange(shards, dtype=jnp.int32)[None, :]).astype(LOW)
    token_at = jnp.arange(tokens, dtype=jnp.int32)
    before = (token_at[:, None] > token_at[None, :]).astype(LOW)
    ranks = jnp.dot(before, relative_hot, preferred_element_type=F32)
    rank_within = jnp.sum(ranks * relative_hot.astype(F32), axis=1).astype(jnp.int32)
    slot = relative * capacity + rank_within
    slots = jnp.arange(shards * capacity, dtype=jnp.int32)
    slot_hot = slots[:, None] == slot[None, :]
    requests = (jnp.sum(jnp.where(slot_hot, local_row[None, :] + 1, 0), axis=1) - 1).reshape(shards, capacity)
    asked = jnp.stack([requests[0]] + [flip(requests[r], r) for r in range(1, shards)])
    looked = jnp.take(table, jnp.maximum(asked, 0).reshape(-1), axis=0).reshape(shards, capacity, model)
    replies = jnp.concatenate([looked[0]] + [flip(looked[r], r) for r in range(1, shards)], axis=0)

    small = jnp.concatenate([attn_gain, ffn_gain, rel_bias.reshape(-1)])
    small_size = small.shape[0]
    joint_own = jnp.concatenate([w_query, w_key, w_value], axis=1)
    own_rows = w_query.shape[0]
    if shards == 8:
        extra = jnp.pad(small, (0, 16 * 3 * inner - small_size)).reshape(16, 3 * inner)
        joint_pieces = gather_pieces(jnp.concatenate([joint_own, extra]))
        joint_loads = plan_loads(joint_pieces, [(0, own_rows, 0, own_rows, 0)])
        lines = {
            bits: part[own_rows - first, :small_size]
            for bits, first, part in joint_pieces
            if first <= own_rows < first + part.shape[0]
        }
        small_all = jnp.stack([lines[bits] for bits in range(shards)])[jnp.arange(shards) ^ me]
        cuts = ff_width // model
        slab = jnp.concatenate([w_out] + [w_in[:, i * model : (i + 1) * model] for i in range(cuts)] + [w_back])
        sections = [(0, own_rows, 0, own_rows, 0)]
        sections += [(1, own_rows, i * model, own_rows, 0) for i in range(cuts)]
        sections += [(2, w_back.shape[0], 0, w_back.shape[0], 0)]
        ffn_pieces = gather_pieces(slab)
        ffn_loads = plan_loads(ffn_pieces, sections)
        joint_pieces = [part for unused_bits, unused_first, part in joint_pieces]
        ffn_pieces = [part for unused_bits, unused_first, part in ffn_pieces]
    else:
        joint_pieces, small_all, *ffn_pieces = (
            lax.all_gather(part, "fsdp", axis=0, tiled=True) for part in (joint_own, small[None], w_out, w_in, w_back)
        )
        joint_pieces = [joint_pieces]
        joint_loads = [(0, 0, 0, None, 0, 0, 0, model)]
        ffn_loads = [(i, i, 0, None, 0, 0, 0, part.shape[0]) for i, part in enumerate(ffn_pieces)]
    first_gain = small_all[:, :own_gain].reshape(1, model).astype(F32)
    second_gain = small_all[:, own_gain : 2 * own_gain].reshape(1, model).astype(F32)
    rel_all = small_all[:, 2 * own_gain :].reshape(buckets, heads).astype(F32)

    task_hot = (task_ids[:, None] == jnp.arange(task_count, dtype=jnp.int32)[None, :]).astype(F32)
    counts = jnp.sum(task_hot, axis=0)
    bits = 1
    while bits < shards:
        counts = counts + flip(counts, bits)
        bits *= 2
    bits = 1
    while bits < groups:
        counts = counts + flip_line(counts, bits)
        bits *= 2
    row_weight = 1.0 / jnp.sum(task_hot * counts[None, :], axis=1)
    positions = jnp.arange(seq_len, dtype=jnp.int32)
    pool_mask = ((positions[None, :] < lengths[:, None]) & (instruction == 0)).astype(F32)
    seed = (pool_mask * row_weight[:, None]).reshape(tokens, 1)

    offsets = (seq_len - 1) - jnp.arange(2 * seq_len, dtype=jnp.int32)
    bucket_hot = (jnp.arange(buckets, dtype=jnp.int32)[:, None] == bucket_of(offsets)[None, :]).astype(F32)
    diagonal = lax.dot_general(rel_all, bucket_hot, (((0,), (0,)), ((), ())), precision=HIGH)

    x, normed_one, joint = front(me_ref, slot[:, None], replies, first_gain, joint_pieces, joint_loads, 3 * inner)
    attended, logs = attend(lengths, diagonal, joint, heads)
    result, act, grad_pre, grad_low, normed_two, grad_hidden, hidden_low, grad_attended, grad_second = ffn(
        me_ref, x, attended, d_out.reshape(tokens, model), seed, second_gain, ffn_pieces, ffn_loads, inner, ff_width
    )
    if w_back.shape[0] % PAIR == 0:
        back_parts = blocks_grad(me_ref, act, grad_low, shards)
    else:
        back_parts = rows_grad(me_ref, act, [grad_low], shards, model // 3)
    in_parts = rows_grad(me_ref, normed_two, [grad_pre], shards, model)
    grad_back = scatter_sum(*back_parts)
    grad_in = scatter_sum(*in_parts)
    *grad_joint, bias_sums = attend_back(lengths, diagonal, joint, grad_attended, logs, heads)
    token_grads, grad_first = project_back(me_ref, grad_joint, x, grad_hidden, first_gain, joint_pieces, joint_loads)

    slot_of = [slot]
    asked_of = [asked]
    for bits in range(1, groups):
        theirs = flip_line(jnp.concatenate([slot, requests.reshape(-1)]), bits)
        slot_of.append(theirs[:tokens])
        asked_of.append(theirs[tokens:].reshape(shards, capacity))
    if groups > 1:
        away = jnp.stack(asked_of[1:], axis=1)
        away = jnp.stack([away[0]] + [flip(away[r], r) for r in range(1, shards)])
        asked_of = [asked] + [away[:, i] for i in range(groups - 1)]
    from_left = [token_grads]
    from_right = [token_grads]
    for step in range(1, groups):
        pairs = [(i, i + 1) for i in range(step - 1, groups - 1)]
        from_left.append(lax.ppermute(from_left[-1], "dp", pairs))
        from_right.append(lax.ppermute(from_right[-1], "dp", [(groups - 1 - i, groups - 1 - j) for i, j in pairs]))
    table_grad = None
    for bits in range(groups):
        block = token_grads
        if bits:
            distance = (at ^ bits) - at
            steps = sorted({(i ^ bits) - i for i in range(groups)})
            options = [from_right[step] if step > 0 else from_left[-step] for step in steps]
            block = options[0]
            for step, option in zip(steps[1:], options[1:]):
                block = jnp.where(distance == step, option, block)
        outgoing = place(slot_of[bits][None, :], block, shards, capacity)
        incoming = [outgoing[0]] + [flip(outgoing[r], r) for r in range(1, shards)]
        table_grad = add_to_table(asked_of[bits].reshape(1, -1), incoming, table_grad, vshard)

    joint_parts = rows_grad(me_ref, normed_one, grad_joint, shards, inner)
    out_parts = rows_grad(me_ref, attended, [hidden_low], shards, model)
    grad_w_joint = scatter_sum(*joint_parts)
    grad_out_weight = scatter_sum(*out_parts)
    grad_rel = lax.dot_general(bucket_hot, bias_sums, (((1,), (1,)), ((), ())), precision=HIGH)
    small_grad = jnp.concatenate(
        [grad_first.reshape(shards, -1), grad_second.reshape(shards, -1), grad_rel.reshape(shards, -1)], axis=1
    )
    small_grad = lax.psum(small_grad, ("dp", "fsdp"))[me]
    sums = lax.psum(tuple(part.astype(LOW) for part in (grad_back, grad_in, grad_out_weight, grad_w_joint)), "dp")
    grad_back, grad_in, grad_out_weight, grad_w_joint = (part.astype(F32) for part in sums)
    return (
        result.reshape(rows_dev, seq_len, model),
        table_grad,
        small_grad[:own_gain],
        grad_w_joint[:, :inner],
        grad_w_joint[:, inner : 2 * inner],
        grad_w_joint[:, 2 * inner :],
        grad_out_weight,
        small_grad[own_gain : 2 * own_gain],
        grad_in,
        grad_back,
        small_grad[2 * own_gain :].reshape(rel_bias.shape),
    )


def solution(mesh):
    both = ("dp", "fsdp")
    in_specs = (
        P(both, None),
        P(both),
        P(both),
        P(both, None),
        P("fsdp", None),
        P("fsdp"),
        P("fsdp", None),
        P("fsdp", None),
        P("fsdp", None),
        P("fsdp", None),
        P("fsdp"),
        P("fsdp", None),
        P("fsdp", None),
        P("fsdp", None),
        P(both, None, None),
    )
    out_specs = (
        P(both, None, None),
        P("fsdp", None),
        P("fsdp"),
        P("fsdp", None),
        P("fsdp", None),
        P("fsdp", None),
        P("fsdp", None),
        P("fsdp"),
        P("fsdp", None),
        P("fsdp", None),
        P("fsdp", None),
    )
    return jax.shard_map(per_device, mesh=mesh, in_specs=in_specs, out_specs=out_specs, check_vma=False)
```

time: 1210 us -> 727 us (0.60)
  local copies, waits for them, and re-layouts: 315 us -> 62 us
  Pallas kernels: 0 us -> 235 us
  matrix products: 225 us -> 1.62 us
  starting transfers between devices: 313 us -> 90 us
  other arithmetic: 171 us -> 34.2 us
  blocking collectives: 0 us -> 66.7 us
  waiting for transfers between devices: 169 us -> 216 us
    pallas_call x0 -> x17, Pallas kernels: none -> 235 us  [the longest x4 73.6 us: add_to_table(): pl.pallas_call(functools.partial(table_kernel, len(pieces)), grid=(pl.cdi...]
    dot_general x29 -> x3, matrix products: 225 us -> 1.62 us  [the longest x1 1 us: per_device(): lax.dot_general(bucket_hot, bias_sums, (((1,), (1,)), ((), ())), precisio...]
    ppermute x82 -> x11, starting transfers between devices: 240 us -> 21.2 us  [the longest x5 8.78 us: flip_line(): return lax.ppermute(value, 'dp', [(i, i ^ bits) for i in range(groups)])]
    ppermute x92 -> x90, waiting for transfers between devices: 100 us -> 188 us  [flip(): return lax.ppermute(value, 'fsdp', [(i, i ^ bits) for i in range(shards)])]
    psum x0 -> x1, blocking collectives: none -> 66.7 us  [per_device(): small_grad = lax.psum(small_grad, ('dp', 'fsdp'))[me]]
    dynamic_update_slice x52 -> x0, local copies, waits for them, and re-layouts: 58.3 us -> none  [the longest x48 57.2 us: gather_rows(): lax.dynamic_update_slice(whole, part, (start,) + (0,) * (own.ndim - 1))]
    dynamic_slice x64 -> x0, local copies, waits for them, and re-layouts: 42.3 us -> none  [run(): before = lax.dynamic_index_in_dim(result, spot, 0, keepdims=False)]
    ppermute x82 -> x11, waiting for transfers between devices: 68.4 us -> 27.9 us  [the longest x3 25.5 us: per_device(): lax.ppermute(from_right[-1], 'dp', [(groups - 1 - i, groups - 1 - j) for...]
  transfers between devices with their start and end apart: 174 -> 102, of which waited for: 57 -> 32; matrix products, arithmetic and copies ran while one was open for 47% -> 13% of each run, Pallas kernels for 0% -> 20%
where the time goes in v2:
time: 727 us; the launch traced here: 721 us
  Pallas kernels  235 us (32%)
  waiting for transfers between devices  216 us (30%)
  starting transfers between devices  90 us (12%)
  blocking collectives  66.7 us (9%)
  local copies, waits for them, and re-layouts  62 us (9%)
  other arithmetic  34.2 us (5%)
  between operations  15.5 us (2%)
    ppermute x90, waiting for transfers between devices, flip(): return lax.ppermute(value, 'fsdp', [(i, i ^ bits) for i in range(shards)])  188 us
    pallas_call x4, Pallas kernels, add_to_table(): pl.pallas_call(functools.partial(table_kernel, len(pieces)), grid=(pl.cdi...  73.6 us
    ppermute x90, starting transfers between devices, flip(): return lax.ppermute(value, 'fsdp', [(i, i ^ bits) for i in range(shards)])  68.7 us
    psum x1, blocking collectives, per_device(): small_grad = lax.psum(small_grad, ('dp', 'fsdp'))[me]  66.7 us
    pallas_call x1, Pallas kernels, ffn(): pl.pallas_call(functools.partial(ffn_kernel, loads, len(pieces)), grid=(t...  35.3 us
    pallas_call x3, Pallas kernels, rows_grad(): pl.pallas_call(functools.partial(rows_grad_kernel, shards), grid=(steps,)...  26.9 us
    pallas_call x1, Pallas kernels, attend_back(): pl.pallas_call(attend_back_kernel, grid=(pairs,), in_specs=[pl.BlockSpec(...  25.6 us
    ppermute x3, waiting for transfers between devices, per_device(): lax.ppermute(from_right[-1], 'dp', [(groups - 1 - i, groups - 1 - j) for...  25.5 us
  transfers between devices with their start and end apart: 102, of which 32 were waited for; matrix products, arithmetic and copies ran while one was open for 13% of the time, Pallas kernels for 20%

profile of v2, /device:TPU:0, one launch (start us, length us, event | category | flops | bytes accessed | tf_op | source)
XLA Modules:
  0.0 721.2 jit_solution(13347619707621871187)
XLA Ops:
  10.0 2.6 collective-permute-start.1
  23.3 2.6 collective-permute-done.25
  31.3 12.2 %gather_fusion = bf16[2048,768]{1,0:T(8,128)(2,1)S(1)} fusion(bf16[4016,768]{1,0:T(8,128)(2,1)} %param.19, s32[2048]{0:T(1024)S(1)} %broadcast_clamp_fusion), kind=kCustom, calls=%fused_computation | custom fusion | bytes 6299648 | tf_op jit(solution)/shard_map/jit(_take)/gather | solution.py:596
  47.7 2.7 collective-permute-start.27
  55.9 2.6 collective-permute-done.8
  58.9 6.0 collective-permute-done.9
  67.5 3.9 collective-permute-done.11
  72.0 5.9 collective-permute-done.15.rest_1_
  78.8 48.8 %collective-permute-done.17.rest_2_ = bf16[112,2304]{1,0:T(8,128)(2,1)S(1)} collective-permute-done((bf16[112,2304]{1,0:T(8,128)(2,1)S(1)}, bf16[112,2304]{1,0:T(8,128)(2,1)S(1)}, u32[]{:S(2)}, u32[]{:S(2)}) %collective-permute-start.17) | collective-permute-done | bytes 516128 | tf_op jit(solution)/shard_map/ppermute | solution.py:507
  135.4 4.1 collective-permute-done.21.rest_3_
  155.4 6.2 collective-permute-done.30.rest_3_
  171.4 16.1 %front.1 = (bf16[1024,768]{1,0:T(8,128)(2,1)}, bf16[1024,768]{1,0:T(8,128)(2,1)}, bf16[1024,2304]{1,0:T(8,128)(2,1)}) custom-call(s32[1]{0:T(128)} %bitcast.me_ref, s32[1024,1]{1,0:T(8,128)} %fusion.26.slot_ref, bf16[2048,768]{1,0:T(8,128)(2,1)} %constant_dynamic-update-slice_fusion.reply_ref, f32[1,768]{1,0:T(1,128)} %reshape.425.gain_ref, ...), custom_call_target="tpu_custom_call" | custom-call | tf_op jit(solution)/shard_map/front/pallas_call | solution.py:249
  187.5 15.9 %attend.1 = (bf16[1024,768]{1,0:T(8,128)(2,1)}, f32[6,4,512]{2,1,0:T(4,128)}) custom-call(s32[2]{0:T(128)} %lengths_ref.3, f32[6,2,1024]{2,1,0:T(2,128)} %copy.79.diagonal_ref, bf16[1024,2304]{1,0:T(8,128)(2,1)} %get-tuple-element.72.query_ref.key_ref.value_ref, bf16[1024,2304]{1,0:T(8,128)(2,1)} %get-tuple-element.72.query_ref.key_ref.value_ref, ...), custom_call_target="tpu_custom_call" | custom-call | tf_op jit(solution)/shard_map/attend/pallas_call | solution.py:94
  203.4 35.3 %ffn.1 = (bf16[1024,768]{1,0:T(8,128)(2,1)}, bf16[1024,3072]{1,0:T(8,128)(2,1)}, bf16[1024,3072]{1,0:T(8,128)(2,1)}, bf16[1024,768]{1,0:T(8,128)(2,1)}, bf16[102...) custom-call(s32[1]{0:T(128)} %bitcast.me_ref, ...), custom_call_target="tpu_custom_call" | custom-call | tf_op jit(solution)/shard_map/ffn/pallas_call | solution.py:314
  238.8 25.6 %attend_back.1 = (bf16[1024,768]{1,0:T(8,128)(2,1)}, bf16[1024,768]{1,0:T(8,128)(2,1)}, bf16[1024,768]{1,0:T(8,128)(2,1)}, f32[6,2,1024]{2,1,0:T(2,128)}) custom-call(s32[2]{0:T(128)} %lengths_ref.3, f32[6,2,1024]{2,1,0:T(2,128)} %copy.79.diagonal_ref, bf16[1024,2304]{1,0:T(8,128)(2,1)} %get-tuple-element.72.query_ref.key_ref.value_ref, ...), custom_call_target="tpu_custom_call" | custom-call | tf_op jit(solution)/shard_map/attend_back/pallas_call | solution.py:165
  264.4 11.1 %rows_grad.3 = (f32[4,96,2304]{2,1,0:T(8,128)}, bf16[4,96,2304]{2,1,0:T(8,128)(2,1)}) custom-call(s32[1]{0:T(128)} %bitcast.me_ref, bf16[1024,768]{1,0:T(8,128)(2,1)} %get-tuple-element.117.left_ref, bf16[1024,768]{1,0:T(8,128)(2,1)} %get-tuple-element.77.query_ref.rest_0_, bf16[1024,768]{1,0:T(8,128)(2,1)} %get-tuple-element.78.key_ref.rest_1_, ...), custom_call_target="tpu_custom_call" | custom-call | tf_op jit(solution)/shard_map/rows_grad/pallas_call | solution.py:404
  275.9 4.9 rows_grad.4
  282.8 2.5 collective-permute-start.39
  294.1 8.7 %blocks_grad.1 = (f32[4,384,768]{2,1,0:T(8,128)}, bf16[4,384,768]{2,1,0:T(8,128)(2,1)}) custom-call(s32[1]{0:T(128)} %bitcast.me_ref, bf16[1024,3072]{1,0:T(8,128)(2,1)} %get-tuple-element.127.keep_left.send_left, bf16[1024,3072]{1,0:T(8,128)(2,1)} %get-tuple-element.127.keep_left.send_left, bf16[1024,768]{1,0:T(8,128)(2,1)} %get-tuple-element.128.right_ref), custom_call_target="tpu_custom_call" | custom-call | tf_op jit(solution)/shard_map/blocks_grad/pallas_call | solution.py:427
  302.7 10.9 %rows_grad.5 = (f32[4,96,3072]{2,1,0:T(8,128)}, bf16[4,96,3072]{2,1,0:T(8,128)(2,1)}) custom-call(s32[1]{0:T(128)} %bitcast.me_ref, bf16[1024,768]{1,0:T(8,128)(2,1)} %get-tuple-element.123.left_ref, bf16[1024,3072]{1,0:T(8,128)(2,1)} %get-tuple-element.124.rest_0_), custom_call_target="tpu_custom_call" | custom-call | tf_op jit(solution)/shard_map/rows_grad/pallas_call | solution.py:404
  313.6 10.7 %project_back.1 = (bf16[1024,768]{1,0:T(8,128)(2,1)}, f32[1,768]{1,0:T(1,128)}) custom-call(s32[1]{0:T(128)} %bitcast.me_ref, bf16[1024,768]{1,0:T(8,128)(2,1)} %get-tuple-element.77.query_ref.rest_0_, bf16[1024,768]{1,0:T(8,128)(2,1)} %get-tuple-element.78.key_ref.rest_1_, bf16[1024,768]{1,0:T(8,128)(2,1)} %get-tuple-element.79.value_ref.rest_2_, ...), custom_call_target="tpu_custom_call" | custom-call | tf_op jit(solution)/shard_map/project_back/pallas_call | solution.py:361
  324.3 5.6 place.7
  332.5 3.7 collective-permute-done.88
  338.9 4.3 collective-permute-done.82
  348.1 4.6 collective-permute-start.50
  362.0 24.0 %collective-permute-done.47 = bf16[1024,768]{1,0:T(8,128)(2,1)S(1)} collective-permute-done((bf16[1024,768]{1,0:T(8,128)(2,1)}, bf16[1024,768]{1,0:T(8,128)(2,1)S(1)}, u32[]{:S(2)}, u32[]{:S(2)}) %collective-permute-start.47) | collective-permute-done | bytes 1572896 | tf_op jit(solution)/shard_map/ppermute | solution.py:682
  392.8 8.7 %collective-permute-done.75.rest_2_ = bf16[256,768]{1,0:T(8,128)(2,1)S(1)} collective-permute-done((bf16[256,768]{1,0:T(8,128)(2,1)}, bf16[256,768]{1,0:T(8,128)(2,1)S(1)}, u32[]{:S(2)}, u32[]{:S(2)}) %collective-permute-start.75) | collective-permute-done | bytes 393248 | tf_op jit(solution)/shard_map/ppermute | solution.py:507
  402.2 5.6 collective-permute-done.94
  409.8 4.7 collective-permute-done.76.rest_3_
  416.4 6.2 collective-permute-done.99
  428.8 2.7 broadcast_select_fusion.2.token_ref
  431.5 5.6 place.5
  442.6 6.2 collective-permute-done.78.rest_5_
  449.3 19.1 %collective-permute-done.100 = bf16[384,768]{1,0:T(8,128)(2,1)S(1)} collective-permute-done((bf16[384,768]{1,0:T(8,128)(2,1)}, bf16[384,768]{1,0:T(8,128)(2,1)S(1)}, u32[]{:S(2)}, u32[]{:S(2)}) %collective-permute-start.100) | collective-permute-done | bytes 589856 | tf_op jit(solution)/shard_map/ppermute | solution.py:507
  470.6 2.3 fusion.7
  475.5 4.9 collective-permute-done.80.rest_7_
  483.4 2.4 collective-permute-start.65
  485.8 3.9 broadcast_select_fusion.1
  489.7 5.6 place.6
  499.4 18.4 %collective-permute-done.64.rest_5_ = bf16[256,768]{1,0:T(8,128)(2,1)} collective-permute-done((bf16[256,768]{1,0:T(8,128)(2,1)}, bf16[256,768]{1,0:T(8,128)(2,1)}, u32[]{:S(2)}, u32[]{:S(2)}) %collective-permute-start.64) | collective-permute-done | bytes 393248 | tf_op jit(solution)/shard_map/ppermute | solution.py:507
  527.9 5.6 place.4
  545.2 16.7 %collective-permute-done.71.rest_5_ = bf16[256,768]{1,0:T(8,128)(2,1)S(1)} collective-permute-done((bf16[256,768]{1,0:T(8,128)(2,1)}, bf16[256,768]{1,0:T(8,128)(2,1)S(1)}, u32[]{:S(2)}, u32[]{:S(2)}) %collective-permute-start.71) | collective-permute-done | bytes 393248 | tf_op jit(solution)/shard_map/ppermute | solution.py:507
  567.3 66.7 %psum.35 = f32[8,240]{1,0:T(8,128)S(1)} all-reduce(f32[8,240]{1,0:T(8,128)S(1)} %pad_maximum_fusion.1), channel_id=1, replica_groups=mesh['dp'=4,'fsdp'=8] {'dp','fsdp'}, use_global_device_ids=true, to_apply=%region_4.5 | all-reduce | flops 1920 | bytes 15360 | tf_op jit(solution)/shard_map/psum | solution.py:705
  635.3 17.7 %table_rows.4.rest_8_ = f32[4016,768]{1,0:T(8,128)} custom-call(s32[1,2048]{1,0:T(1,128)} %bitcast.206, bf16[256,768]{1,0:T(8,128)(2,1)} %get-tuple-element.106.rest_0_, bf16[256,768]{1,0:T(8,128)(2,1)} %copy-done.24, bf16[256,768]{1,0:T(8,128)(2,1)} %copy-done.25, bf16[256,768]{1,0:T(8,128)(2,1)} %copy-done.26, bf16[256,768]{1,0:T(8,128)(2,1)} %copy-done.27, ...), custom_call_target="tpu_custom_call" | custom-call | tf_op jit(solution)/shard_map/table_rows/pallas_call | solution.py:492
  653.1 2.3 convert_element_type.249
  658.1 18.6 %table_rows.5.rest_8_ = f32[4016,768]{1,0:T(8,128)} custom-call(s32[1,2048]{1,0:T(1,128)} %bitcast.205, bf16[256,768]{1,0:T(8,128)(2,1)} %get-tuple-element.98.rest_0_, bf16[256,768]{1,0:T(8,128)(2,1)} %copy-done.31, bf16[256,768]{1,0:T(8,128)(2,1)} %copy-done.32, bf16[256,768]{1,0:T(8,128)(2,1)} %copy-done.33, ...), custom_call_target="tpu_custom_call", output_to_operand_aliasing={{}: (9, {})} | custom-call | tf_op jit(solution)/shard_map/table_rows/pallas_call | solution.py:492
  676.7 18.6 %table_rows.6.rest_8_ = f32[4016,768]{1,0:T(8,128)} custom-call(s32[1,2048]{1,0:T(1,128)} %bitcast.204, bf16[256,768]{1,0:T(8,128)(2,1)} %get-tuple-element.90.rest_0_, bf16[256,768]{1,0:T(8,128)(2,1)} %collective-permute-done.60.rest_1_, bf16[256,768]{1,0:T(8,128)(2,1)} %copy-done.29, ...), custom_call_target="tpu_custom_call", output_to_operand_aliasing={{}: (9, {})} | custom-call | tf_op jit(solution)/shard_map/table_rows/pallas_call | solution.py:492
  695.4 18.6 %table_rows.7 = f32[4016,768]{1,0:T(8,128)} custom-call(s32[1,2048]{1,0:T(1,128)} %bitcast.203, bf16[256,768]{1,0:T(8,128)(2,1)} %get-tuple-element.82.rest_0_, bf16[256,768]{1,0:T(8,128)(2,1)} %copy-done.35, bf16[256,768]{1,0:T(8,128)(2,1)} %copy-done.36, bf16[256,768]{1,0:T(8,128)(2,1)} %collective-permute-done.55.rest_3_, ...), custom_call_target="tpu_custom_call", output_to_operand_aliasing={{}: (9, {})} | custom-call | tf_op jit(solution)/shard_map/table_rows/pallas_call | solution.py:492
  (445 shorter events, 163.2 us)
Async XLA Ops:
  7.2 645.9 %all-reduce.12.cloned.1.call-start = ((), (), s32[]{:S(2)}) async-start(), calls=%async_computation | async-start | bytes 3538944 | tf_op jit(solution)/shard_map/psum | solution.py:706
  52.2 25.7 %collective-permute-start.15 = (bf16[112,2304]{1,0:T(8,128)(2,1)S(1)}, bf16[112,2304]{1,0:T(8,128)(2,1)S(1)}, u32[]{:S(2)}, u32[]{:S(2)}) collective-permute-start(bf16[112,2304]{1,0:T(8,128)(2,1)S(1)} %copy-done.1), channel_id=1, source_target_pairs={{0,2},{1,3},{2,0},{3,1},{4,6},{5,7},{6,4},{7,5},{8,10},{9,11},{10,... | collective-permute-start | bytes 1548296 | tf_op jit(solution)/shard_map/ppermute | solution.py:507
  58.4 81.7 %collective-permute-start.29 = (bf16[864,768]{1,0:T(8,128)(2,1)}, bf16[864,768]{1,0:T(8,128)(2,1)S(1)}, u32[]{:S(2)}, u32[]{:S(2)}) collective-permute-start(bf16[864,768]{1,0:T(8,128)(2,1)} %constant_dynamic-update-slice_fusion.7.rest_0_), channel_id=1, source_target_pairs={{0,4},{1,5},{2,6},{3,7},{4,0},{5,1},{6,2},{7,3},{8,12},{9,13},{10,... | collective-permute-start | bytes 3981320 | tf_op jit(solution)/shard_map/ppermute | solution.py:507
  64.9 75.5 %collective-permute-start.28 = (bf16[864,768]{1,0:T(8,128)(2,1)}, bf16[864,768]{1,0:T(8,128)(2,1)}, u32[]{:S(2)}, u32[]{:S(2)}) collective-permute-start(bf16[864,768]{1,0:T(8,128)(2,1)} %constant_dynamic-update-slice_fusion.7.rest_0_), channel_id=1, source_target_pairs={{0,2},{1,3},{2,0},{3,1},{4,6},{5,7},{6,4},{7,5},{8,10},{9,11},{10,... | collective-permute-start | bytes 3981320 | tf_op jit(solution)/shard_map/ppermute | solution.py:507
  66.4 61.1 %collective-permute-start.17 = (bf16[112,2304]{1,0:T(8,128)(2,1)S(1)}, bf16[112,2304]{1,0:T(8,128)(2,1)S(1)}, u32[]{:S(2)}, u32[]{:S(2)}) collective-permute-start(bf16[112,2304]{1,0:T(8,128)(2,1)S(1)} %copy-done.1), channel_id=1, source_target_pairs={{0,4},{1,5},{2,6},{3,7},{4,0},{5,1},{6,2},{7,3},{8,12},{9,13},{10,... | collective-permute-start | bytes 1548296 | tf_op jit(solution)/shard_map/ppermute | solution.py:507
  71.4 61.0 %collective-permute-start.12 = (bf16[256,768]{1,0:T(8,128)(2,1)}, bf16[256,768]{1,0:T(8,128)(2,1)}, u32[]{:S(2)}, u32[]{:S(2)}) collective-permute-start(bf16[256,768]{1,0:T(8,128)(2,1)} %get-tuple-element.152), channel_id=1, source_target_pairs={{0,6},{1,7},{2,4},{3,5},{4,2},{5,3},{6,0},{7,1},{8,14},{9,15},{10,... | collective-permute-start | bytes 1179656 | tf_op jit(solution)/shard_map/ppermute | solution.py:507
  77.9 57.5 %collective-permute-start.13 = (bf16[256,768]{1,0:T(8,128)(2,1)}, bf16[256,768]{1,0:T(8,128)(2,1)}, u32[]{:S(2)}, u32[]{:S(2)}) collective-permute-start(bf16[256,768]{1,0:T(8,128)(2,1)} %get-tuple-element.151), channel_id=1, source_target_pairs={{0,7},{1,6},{2,5},{3,4},{4,3},{5,2},{6,1},{7,0},{8,15},{9,14},{10,... | collective-permute-start | bytes 1179656 | tf_op jit(solution)/shard_map/ppermute | solution.py:507
  143.8 59.6 %collective-permute-start.32 = (bf16[864,768]{1,0:T(8,128)(2,1)}, bf16[864,768]{1,0:T(8,128)(2,1)}, u32[]{:S(2)}, u32[]{:S(2)}) collective-permute-start(bf16[864,768]{1,0:T(8,128)(2,1)} %constant_dynamic-update-slice_fusion.7.rest_0_), channel_id=1, source_target_pairs={{0,1},{1,0},{2,3},{3,2},{4,5},{5,4},{6,7},{7,6},{8,9},{9,8},{10,11... | collective-permute-start | bytes 3981320 | tf_op jit(solution)/shard_map/ppermute | solution.py:507
  145.8 57.6 %collective-permute-start.33 = (bf16[864,768]{1,0:T(8,128)(2,1)}, bf16[864,768]{1,0:T(8,128)(2,1)}, u32[]{:S(2)}, u32[]{:S(2)}) collective-permute-start(bf16[864,768]{1,0:T(8,128)(2,1)} %collective-permute-done.28.rest_1_), channel_id=1, source_target_pairs={{0,1},{1,0},{2,3},{3,2},{4,5},{5,4},{6,7},{7,6},{8,9},{9,8},{10,11... | collective-permute-start | bytes 3981320 | tf_op jit(solution)/shard_map/ppermute | solution.py:507
  146.6 56.8 %collective-permute-start.34 = (bf16[864,768]{1,0:T(8,128)(2,1)S(1)}, bf16[864,768]{1,0:T(8,128)(2,1)}, u32[]{:S(2)}, u32[]{:S(2)}) collective-permute-start(bf16[864,768]{1,0:T(8,128)(2,1)S(1)} %collective-permute-done.29.rest_2_), channel_id=1, source_target_pairs={{0,1},{1,0},{2,3},{3,2},{4,5},{5,4},{6,7},{7,6},{8,9},{9,8},{10,11... | collective-permute-start | bytes 3981320 | tf_op jit(solution)/shard_map/ppermute | solution.py:507
  161.5 41.9 %collective-permute-start.35 = (bf16[432,768]{1,0:T(8,128)(2,1)}, bf16[432,768]{1,0:T(8,128)(2,1)}, u32[]{:S(2)}, u32[]{:S(2)}) collective-permute-start(bf16[432,768]{1,0:T(8,128)(2,1)} %collective-permute-done.30.rest_3_), channel_id=1, source_target_pairs={{0,1},{1,0},{2,3},{3,2},{4,5},{5,4},{6,7},{7,6},{8,9},{9,8},{10,11... | collective-permute-start | bytes 1990664 | tf_op jit(solution)/shard_map/ppermute | solution.py:507
  162.0 41.4 %collective-permute-start.36 = (bf16[432,768]{1,0:T(8,128)(2,1)}, bf16[432,768]{1,0:T(8,128)(2,1)}, u32[]{:S(2)}, u32[]{:S(2)}) collective-permute-start(bf16[432,768]{1,0:T(8,128)(2,1)} %collective-permute-done.31.rest_4_), channel_id=1, source_target_pairs={{0,1},{1,0},{2,3},{3,2},{4,5},{5,4},{6,7},{7,6},{8,9},{9,8},{10,11... | collective-permute-start | bytes 1990664 | tf_op jit(solution)/shard_map/ppermute | solution.py:507
  275.5 56.0 %collective-permute-start.81 = (bf16[4,96,2304]{2,1,0:T(8,128)(2,1)}, bf16[4,96,2304]{2,1,0:T(8,128)(2,1)S(1)}, u32[]{:S(2)}, u32[]{:S(2)}) collective-permute-start(bf16[4,96,2304]{2,1,0:T(8,128)(2,1)} %get-tuple-element.119), channel_id=1, source_target_pairs={{0,1},{1,0},{2,3},{3,2},{4,5},{5,4},{6,7},{7,6},{8,9},{9,8},{10,11... | collective-permute-start | bytes 5308424 | tf_op jit(solution)/shard_map/ppermute | solution.py:507
  289.8 40.1 %collective-permute-start.87 = (bf16[48,768]{1,0:T(8,128)(2,1)S(1)}, bf16[48,768]{1,0:T(8,128)(2,1)S(1)}, u32[]{:S(2)}, u32[]{:S(2)}) collective-permute-start(bf16[48,768]{1,0:T(8,128)(2,1)S(1)} %get-tuple-element.167), channel_id=1, source_target_pairs={{0,4},{1,5},{2,6},{3,7},{4,0},{5,1},{6,2},{7,3},{8,12},{9,13},{10,... | collective-permute-start | bytes 221192 | tf_op jit(solution)/shard_map/ppermute | solution.py:507
  291.4 38.7 %collective-permute-start.89 = (bf16[48,768]{1,0:T(8,128)(2,1)S(1)}, bf16[48,768]{1,0:T(8,128)(2,1)S(1)}, u32[]{:S(2)}, u32[]{:S(2)}) collective-permute-start(bf16[48,768]{1,0:T(8,128)(2,1)S(1)} %get-tuple-element.168), channel_id=1, source_target_pairs={{0,2},{1,3},{2,0},{3,1},{4,6},{5,7},{6,4},{7,5},{8,10},{9,11},{10,... | collective-permute-start | bytes 221192 | tf_op jit(solution)/shard_map/ppermute | solution.py:507
  292.7 52.8 %collective-permute-start.40 = (s32[3,256]{1,0:T(4,128)S(1)}, s32[3,256]{1,0:T(4,128)S(1)}, u32[]{:S(2)}, u32[]{:S(2)}) collective-permute-start(s32[3,256]{1,0:T(4,128)S(1)} %get-tuple-element.178), channel_id=1, source_target_pairs={{0,1},{1,0},{2,3},{3,2},{4,5},{5,4},{6,7},{7,6},{8,9},{9,8},{10,11... | collective-permute-start | bytes 9224 | tf_op jit(solution)/shard_map/ppermute | solution.py:507
  292.7 53.3 %collective-permute-start.41 = (s32[3,256]{1,0:T(4,128)S(1)}, s32[3,256]{1,0:T(4,128)S(1)}, u32[]{:S(2)}, u32[]{:S(2)}) collective-permute-start(s32[3,256]{1,0:T(4,128)S(1)} %get-tuple-element.177), channel_id=1, source_target_pairs={{0,2},{1,3},{2,0},{3,1},{4,6},{5,7},{6,4},{7,5},{8,10},{9,11},{10,... | collective-permute-start | bytes 9224 | tf_op jit(solution)/shard_map/ppermute | solution.py:507
  346.8 39.2 %collective-permute-start.47 = (bf16[1024,768]{1,0:T(8,128)(2,1)}, bf16[1024,768]{1,0:T(8,128)(2,1)S(1)}, u32[]{:S(2)}, u32[]{:S(2)}) collective-permute-start(bf16[1024,768]{1,0:T(8,128)(2,1)} %get-tuple-element.81.token_ref), channel_id=1, source_target_pairs={{24,16},{16,8},{8,0},{25,17},{17,9},{9,1},{26,18},{18,10},{10,2},{... | collective-permute-start | bytes 4718600 | tf_op jit(solution)/shard_map/ppermute | solution.py:682
  348.1 39.2 %collective-permute-start.50 = (bf16[1024,768]{1,0:T(8,128)(2,1)}, bf16[1024,768]{1,0:T(8,128)(2,1)S(1)}, u32[]{:S(2)}, u32[]{:S(2)}) collective-permute-start(bf16[1024,768]{1,0:T(8,128)(2,1)} %get-tuple-element.81.token_ref), channel_id=1, source_target_pairs={{0,8},{8,16},{16,24},{1,9},{9,17},{17,25},{2,10},{10,18},{18,26},{... | collective-permute-start | bytes 4718600 | tf_op jit(solution)/shard_map/ppermute | solution.py:681
  358.3 30.9 %collective-permute-start.74 = (bf16[256,768]{1,0:T(8,128)(2,1)}, bf16[256,768]{1,0:T(8,128)(2,1)S(1)}, u32[]{:S(2)}, u32[]{:S(2)}) collective-permute-start(bf16[256,768]{1,0:T(8,128)(2,1)} %get-tuple-element.107), channel_id=1, source_target_pairs={{0,1},{1,0},{2,3},{3,2},{4,5},{5,4},{6,7},{7,6},{8,9},{9,8},{10,11... | collective-permute-start | bytes 1179656 | tf_op jit(solution)/shard_map/ppermute | solution.py:507
  359.4 30.6 %collective-permute-start.83 = (bf16[96,2304]{1,0:T(8,128)(2,1)}, bf16[96,2304]{1,0:T(8,128)(2,1)S(1)}, u32[]{:S(2)}, u32[]{:S(2)}) collective-permute-start(bf16[96,2304]{1,0:T(8,128)(2,1)} %get-tuple-element.147), channel_id=1, source_target_pairs={{0,2},{1,3},{2,0},{3,1},{4,6},{5,7},{6,4},{7,5},{8,10},{9,11},{10,... | collective-permute-start | bytes 1327112 | tf_op jit(solution)/shard_map/ppermute | solution.py:507
  360.1 30.9 %collective-permute-start.85 = (bf16[96,2304]{1,0:T(8,128)(2,1)S(1)}, bf16[96,2304]{1,0:T(8,128)(2,1)S(1)}, u32[]{:S(2)}, u32[]{:S(2)}) collective-permute-start(bf16[96,2304]{1,0:T(8,128)(2,1)S(1)} %get-tuple-element.148), channel_id=1, source_target_pairs={{0,4},{1,5},{2,6},{3,7},{4,0},{5,1},{6,2},{7,3},{8,12},{9,13},{10,... | collective-permute-start | bytes 1327112 | tf_op jit(solution)/shard_map/ppermute | solution.py:507
  386.0 38.2 %collective-permute-start.48 = (bf16[1024,768]{1,0:T(8,128)(2,1)S(1)}, bf16[1024,768]{1,0:T(8,128)(2,1)}, u32[]{:S(2)}, u32[]{:S(2)}) collective-permute-start(bf16[1024,768]{1,0:T(8,128)(2,1)S(1)} %collective-permute-done.47), channel_id=1, source_target_pairs={{16,8},{8,0},{17,9},{9,1},{18,10},{10,2},{19,11},{11,3},{20,12},{1... | collective-permute-start | bytes 4718600 | tf_op jit(solution)/shard_map/ppermute | solution.py:682
  387.3 38.2 %collective-permute-start.51 = (bf16[1024,768]{1,0:T(8,128)(2,1)S(1)}, bf16[1024,768]{1,0:T(8,128)(2,1)}, u32[]{:S(2)}, u32[]{:S(2)}) collective-permute-start(bf16[1024,768]{1,0:T(8,128)(2,1)S(1)} %collective-permute-done.50), channel_id=1, source_target_pairs={{8,16},{16,24},{9,17},{17,25},{10,18},{18,26},{11,19},{19,27},{12,... | collective-permute-start | bytes 4718600 | tf_op jit(solution)/shard_map/ppermute | solution.py:681
  414.5 22.7 %collective-permute-start.77 = (bf16[256,768]{1,0:T(8,128)(2,1)}, bf16[256,768]{1,0:T(8,128)(2,1)S(1)}, u32[]{:S(2)}, u32[]{:S(2)}) collective-permute-start(bf16[256,768]{1,0:T(8,128)(2,1)} %get-tuple-element.110), channel_id=1, source_target_pairs={{0,4},{1,5},{2,6},{3,7},{4,0},{5,1},{6,2},{7,3},{8,12},{9,13},{10,... | collective-permute-start | bytes 1179656 | tf_op jit(solution)/shard_map/ppermute | solution.py:507
  415.4 21.8 %collective-permute-start.93 = (bf16[96,3072]{1,0:T(8,128)(2,1)}, bf16[96,3072]{1,0:T(8,128)(2,1)}, u32[]{:S(2)}, u32[]{:S(2)}) collective-permute-start(bf16[96,3072]{1,0:T(8,128)(2,1)} %get-tuple-element.145), channel_id=1, source_target_pairs={{0,2},{1,3},{2,0},{3,1},{4,6},{5,7},{6,4},{7,5},{8,10},{9,11},{10,... | collective-permute-start | bytes 1769480 | tf_op jit(solution)/shard_map/ppermute | solution.py:507
  424.2 59.1 %collective-permute-start.49 = (bf16[1024,768]{1,0:T(8,128)(2,1)}, bf16[1024,768]{1,0:T(8,128)(2,1)}, u32[]{:S(2)}, u32[]{:S(2)}) collective-permute-start(bf16[1024,768]{1,0:T(8,128)(2,1)} %collective-permute-done.48), channel_id=1, source_target_pairs={{8,0},{9,1},{10,2},{11,3},{12,4},{13,5},{14,6},{15,7}} | collective-permute-start | bytes 4718600 | tf_op jit(solution)/shard_map/ppermute | solution.py:682
  425.5 57.9 %collective-permute-start.52 = (bf16[1024,768]{1,0:T(8,128)(2,1)}, bf16[1024,768]{1,0:T(8,128)(2,1)}, u32[]{:S(2)}, u32[]{:S(2)}) collective-permute-start(bf16[1024,768]{1,0:T(8,128)(2,1)} %collective-permute-done.51), channel_id=1, source_target_pairs={{16,24},{17,25},{18,26},{19,27},{20,28},{21,29},{22,30},{23,31}} | collective-permute-start | bytes 4718600 | tf_op jit(solution)/shard_map/ppermute | solution.py:681
  437.2 31.2 %collective-permute-start.100 = (bf16[384,768]{1,0:T(8,128)(2,1)}, bf16[384,768]{1,0:T(8,128)(2,1)S(1)}, u32[]{:S(2)}, u32[]{:S(2)}) collective-permute-start(bf16[384,768]{1,0:T(8,128)(2,1)} %get-tuple-element.144), channel_id=1, source_target_pairs={{0,4},{1,5},{2,6},{3,7},{4,0},{5,1},{6,2},{7,3},{8,12},{9,13},{10,... | collective-permute-start | bytes 1769480 | tf_op jit(solution)/shard_map/ppermute | solution.py:507
  439.1 31.0 %collective-permute-start.98 = (bf16[384,768]{1,0:T(8,128)(2,1)}, bf16[384,768]{1,0:T(8,128)(2,1)S(1)}, u32[]{:S(2)}, u32[]{:S(2)}) collective-permute-start(bf16[384,768]{1,0:T(8,128)(2,1)} %get-tuple-element.143), channel_id=1, source_target_pairs={{0,2},{1,3},{2,0},{3,1},{4,6},{5,7},{6,4},{7,5},{8,10},{9,11},{10,... | collective-permute-start | bytes 1769480 | tf_op jit(solution)/shard_map/ppermute | solution.py:507
  448.8 25.4 %collective-permute-start.79 = (bf16[256,768]{1,0:T(8,128)(2,1)}, bf16[256,768]{1,0:T(8,128)(2,1)}, u32[]{:S(2)}, u32[]{:S(2)}) collective-permute-start(bf16[256,768]{1,0:T(8,128)(2,1)} %get-tuple-element.112), channel_id=1, source_target_pairs={{0,6},{1,7},{2,4},{3,5},{4,2},{5,3},{6,0},{7,1},{8,14},{9,15},{10,... | collective-permute-start | bytes 1179656 | tf_op jit(solution)/shard_map/ppermute | solution.py:507
  474.2 21.0 %collective-permute-start.61 = (bf16[256,768]{1,0:T(8,128)(2,1)}, bf16[256,768]{1,0:T(8,128)(2,1)S(1)}, u32[]{:S(2)}, u32[]{:S(2)}) collective-permute-start(bf16[256,768]{1,0:T(8,128)(2,1)} %get-tuple-element.92), channel_id=1, source_target_pairs={{0,2},{1,3},{2,0},{3,1},{4,6},{5,7},{6,4},{7,5},{8,10},{9,11},{10,... | collective-permute-start | bytes 1179656 | tf_op jit(solution)/shard_map/ppermute | solution.py:507
  483.3 34.5 %collective-permute-start.64 = (bf16[256,768]{1,0:T(8,128)(2,1)}, bf16[256,768]{1,0:T(8,128)(2,1)}, u32[]{:S(2)}, u32[]{:S(2)}) collective-permute-start(bf16[256,768]{1,0:T(8,128)(2,1)} %get-tuple-element.95), channel_id=1, source_target_pairs={{0,5},{1,4},{2,7},{3,6},{4,1},{5,0},{6,3},{7,2},{8,13},{9,12},{10,... | collective-permute-start | bytes 1179656 | tf_op jit(solution)/shard_map/ppermute | solution.py:507
  483.4 36.1 %collective-permute-start.65 = (bf16[256,768]{1,0:T(8,128)(2,1)}, bf16[256,768]{1,0:T(8,128)(2,1)}, u32[]{:S(2)}, u32[]{:S(2)}) collective-permute-start(bf16[256,768]{1,0:T(8,128)(2,1)} %get-tuple-element.96), channel_id=1, source_target_pairs={{0,6},{1,7},{2,4},{3,5},{4,2},{5,3},{6,0},{7,1},{8,14},{9,15},{10,... | collective-permute-start | bytes 1179656 | tf_op jit(solution)/shard_map/ppermute | solution.py:507
  495.3 38.2 %collective-permute-start.66 = (bf16[256,768]{1,0:T(8,128)(2,1)}, bf16[256,768]{1,0:T(8,128)(2,1)S(1)}, u32[]{:S(2)}, u32[]{:S(2)}) collective-permute-start(bf16[256,768]{1,0:T(8,128)(2,1)} %get-tuple-element.97), channel_id=1, source_target_pairs={{0,7},{1,6},{2,5},{3,4},{4,3},{5,2},{6,1},{7,0},{8,15},{9,14},{10,... | collective-permute-start | bytes 1179656 | tf_op jit(solution)/shard_map/ppermute | solution.py:507
  498.2 35.3 %collective-permute-start.67 = (bf16[256,768]{1,0:T(8,128)(2,1)}, bf16[256,768]{1,0:T(8,128)(2,1)S(1)}, u32[]{:S(2)}, u32[]{:S(2)}) collective-permute-start(bf16[256,768]{1,0:T(8,128)(2,1)} %get-tuple-element.99), channel_id=1, source_target_pairs={{0,1},{1,0},{2,3},{3,2},{4,5},{5,4},{6,7},{7,6},{8,9},{9,8},{10,11... | collective-permute-start | bytes 1179656 | tf_op jit(solution)/shard_map/ppermute | solution.py:507
  498.5 36.4 %collective-permute-start.68 = (bf16[256,768]{1,0:T(8,128)(2,1)}, bf16[256,768]{1,0:T(8,128)(2,1)S(1)}, u32[]{:S(2)}, u32[]{:S(2)}) collective-permute-start(bf16[256,768]{1,0:T(8,128)(2,1)} %get-tuple-element.100), channel_id=1, source_target_pairs={{0,2},{1,3},{2,0},{3,1},{4,6},{5,7},{6,4},{7,5},{8,10},{9,11},{10,... | collective-permute-start | bytes 1179656 | tf_op jit(solution)/shard_map/ppermute | solution.py:507
  517.8 18.4 %collective-permute-start.69 = (bf16[256,768]{1,0:T(8,128)(2,1)}, bf16[256,768]{1,0:T(8,128)(2,1)S(1)}, u32[]{:S(2)}, u32[]{:S(2)}) collective-permute-start(bf16[256,768]{1,0:T(8,128)(2,1)} %get-tuple-element.101), channel_id=1, source_target_pairs={{0,3},{1,2},{2,1},{3,0},{4,7},{5,6},{6,5},{7,4},{8,11},{9,10},{10,... | collective-permute-start | bytes 1179656 | tf_op jit(solution)/shard_map/ppermute | solution.py:507
  533.5 28.5 %collective-permute-start.71 = (bf16[256,768]{1,0:T(8,128)(2,1)}, bf16[256,768]{1,0:T(8,128)(2,1)S(1)}, u32[]{:S(2)}, u32[]{:S(2)}) collective-permute-start(bf16[256,768]{1,0:T(8,128)(2,1)} %get-tuple-element.103), channel_id=1, source_target_pairs={{0,5},{1,4},{2,7},{3,6},{4,1},{5,0},{6,3},{7,2},{8,13},{9,12},{10,... | collective-permute-start | bytes 1179656 | tf_op jit(solution)/shard_map/ppermute | solution.py:507
  533.6 28.5 %collective-permute-start.72 = (bf16[256,768]{1,0:T(8,128)(2,1)}, bf16[256,768]{1,0:T(8,128)(2,1)}, u32[]{:S(2)}, u32[]{:S(2)}) collective-permute-start(bf16[256,768]{1,0:T(8,128)(2,1)} %get-tuple-element.104), channel_id=1, source_target_pairs={{0,6},{1,7},{2,4},{3,5},{4,2},{5,3},{6,0},{7,1},{8,14},{9,15},{10,... | collective-permute-start | bytes 1179656 | tf_op jit(solution)/shard_map/ppermute | solution.py:507
  534.9 27.9 %collective-permute-start.73 = (bf16[256,768]{1,0:T(8,128)(2,1)}, bf16[256,768]{1,0:T(8,128)(2,1)}, u32[]{:S(2)}, u32[]{:S(2)}) collective-permute-start(bf16[256,768]{1,0:T(8,128)(2,1)} %get-tuple-element.105), channel_id=1, source_target_pairs={{0,7},{1,6},{2,5},{3,4},{4,3},{5,2},{6,1},{7,0},{8,15},{9,14},{10,... | collective-permute-start | bytes 1179656 | tf_op jit(solution)/shard_map/ppermute | solution.py:507
  536.2 27.8 %collective-permute-start.53 = (bf16[256,768]{1,0:T(8,128)(2,1)}, bf16[256,768]{1,0:T(8,128)(2,1)S(1)}, u32[]{:S(2)}, u32[]{:S(2)}) collective-permute-start(bf16[256,768]{1,0:T(8,128)(2,1)} %get-tuple-element.83), channel_id=1, source_target_pairs={{0,1},{1,0},{2,3},{3,2},{4,5},{5,4},{6,7},{7,6},{8,9},{9,8},{10,11... | collective-permute-start | bytes 1179656 | tf_op jit(solution)/shard_map/ppermute | solution.py:507
  536.7 28.6 %collective-permute-start.54 = (bf16[256,768]{1,0:T(8,128)(2,1)}, bf16[256,768]{1,0:T(8,128)(2,1)S(1)}, u32[]{:S(2)}, u32[]{:S(2)}) collective-permute-start(bf16[256,768]{1,0:T(8,128)(2,1)} %get-tuple-element.84), channel_id=1, source_target_pairs={{0,2},{1,3},{2,0},{3,1},{4,6},{5,7},{6,4},{7,5},{8,10},{9,11},{10,... | collective-permute-start | bytes 1179656 | tf_op jit(solution)/shard_map/ppermute | solution.py:507
  561.9 133.4 %collective-permute-start.55 = (bf16[256,768]{1,0:T(8,128)(2,1)}, bf16[256,768]{1,0:T(8,128)(2,1)}, u32[]{:S(2)}, u32[]{:S(2)}) collective-permute-start(bf16[256,768]{1,0:T(8,128)(2,1)} %get-tuple-element.85), channel_id=1, source_target_pairs={{0,3},{1,2},{2,1},{3,0},{4,7},{5,6},{6,5},{7,4},{8,11},{9,10},{10,... | collective-permute-start | bytes 1179656 | tf_op jit(solution)/shard_map/ppermute | solution.py:507
  562.1 133.3 %collective-permute-start.56 = (bf16[256,768]{1,0:T(8,128)(2,1)}, bf16[256,768]{1,0:T(8,128)(2,1)}, u32[]{:S(2)}, u32[]{:S(2)}) collective-permute-start(bf16[256,768]{1,0:T(8,128)(2,1)} %get-tuple-element.86), channel_id=1, source_target_pairs={{0,4},{1,5},{2,6},{3,7},{4,0},{5,1},{6,2},{7,3},{8,12},{9,13},{10,... | collective-permute-start | bytes 1179656 | tf_op jit(solution)/shard_map/ppermute | solution.py:507
  562.8 132.6 %collective-permute-start.57 = (bf16[256,768]{1,0:T(8,128)(2,1)}, bf16[256,768]{1,0:T(8,128)(2,1)}, u32[]{:S(2)}, u32[]{:S(2)}) collective-permute-start(bf16[256,768]{1,0:T(8,128)(2,1)} %get-tuple-element.87), channel_id=1, source_target_pairs={{0,5},{1,4},{2,7},{3,6},{4,1},{5,0},{6,3},{7,2},{8,13},{9,12},{10,... | collective-permute-start | bytes 1179656 | tf_op jit(solution)/shard_map/ppermute | solution.py:507
  564.0 131.4 %collective-permute-start.58 = (bf16[256,768]{1,0:T(8,128)(2,1)}, bf16[256,768]{1,0:T(8,128)(2,1)}, u32[]{:S(2)}, u32[]{:S(2)}) collective-permute-start(bf16[256,768]{1,0:T(8,128)(2,1)} %get-tuple-element.88), channel_id=1, source_target_pairs={{0,6},{1,7},{2,4},{3,5},{4,2},{5,3},{6,0},{7,1},{8,14},{9,15},{10,... | collective-permute-start | bytes 1179656 | tf_op jit(solution)/shard_map/ppermute | solution.py:507
  565.2 130.2 %collective-permute-start.59 = (bf16[256,768]{1,0:T(8,128)(2,1)}, bf16[256,768]{1,0:T(8,128)(2,1)}, u32[]{:S(2)}, u32[]{:S(2)}) collective-permute-start(bf16[256,768]{1,0:T(8,128)(2,1)} %get-tuple-element.89), channel_id=1, source_target_pairs={{0,7},{1,6},{2,5},{3,4},{4,3},{5,2},{6,1},{7,0},{8,15},{9,14},{10,... | collective-permute-start | bytes 1179656 | tf_op jit(solution)/shard_map/ppermute | solution.py:507
  (120 other events, 2701.5 us)
Sparse Core Ops, SparseCore 0:
  473.1 78.2 all-reduce.11

commit v3 on v2

v3 whole, which is shorter than its diff:
```python
import functools
import jax
import jax.numpy as jnp
from jax import lax
from jax.experimental import pallas as pl
from jax.experimental.pallas import tpu as pltpu
from jax.sharding import PartitionSpec as P

EPS = 1e-06
NEG = -1000000000.0
LIMITS = (12, 16, 23, 32, 46, 64, 91)
HIGH = lax.Precision.HIGHEST
LOW = jnp.bfloat16
F32 = jnp.float32
VMEM_LIMIT = 56 * 1024 * 1024
PAIR = 128
ROOT = (2.0 / 3.141592653589793) ** 0.5
CUBE = 0.044715


def dot(left, right):
    return jnp.dot(left, right, preferred_element_type=F32)


def dot_nt(left, right):
    return lax.dot_general(left, right, (((1,), (1,)), ((), ())), preferred_element_type=F32)


def dot_tn(left, right):
    return lax.dot_general(left, right, (((0,), (0,)), ((), ())), preferred_element_type=F32)


def params():
    return pltpu.CompilerParams(vmem_limit_bytes=VMEM_LIMIT)


def cost(micros):
    return pl.CostEstimate(flops=int(micros * 1.15e9), bytes_accessed=int(micros * 3.6e6), transcendentals=0)


def half_lanes(size):
    return lax.broadcasted_iota(jnp.int32, (size, PAIR), 1) < PAIR // 2


def spread_bias(diagonal, seq_len):
    wide = jnp.broadcast_to(diagonal, (seq_len, 2 * seq_len))
    wide = pltpu.roll(wide, seq_len + 1, 1, stride=1, stride_axis=0)
    return wide[:, :seq_len]


def gather_bias(grad):
    seq_len = grad.shape[0]
    blocks = seq_len // PAIR
    total = None
    for block in range(blocks):
        ahead = PAIR * (blocks - 1 - block)
        parts = [grad[block * PAIR : (block + 1) * PAIR, :], jnp.zeros((PAIR, seq_len - ahead), F32)]
        if ahead:
            parts = [jnp.zeros((PAIR, ahead), F32)] + parts
        wide = jnp.concatenate(parts, axis=1)
        total = wide if total is None else total + wide
    eight = None
    for group in range(PAIR // 8):
        moved = pltpu.roll(total[8 * group : 8 * group + 8, :], PAIR - 8 - 8 * group, 1)
        eight = moved if eight is None else eight + moved
    return sum(pltpu.roll(eight[sub : sub + 1, :], 7 - sub, 1) for sub in range(8))


def attend_kernel(lengths_ref, diagonal_ref, query_ref, key_ref, value_ref, out_ref, log_ref):
    rows = lengths_ref.shape[0]
    seq_len = query_ref.shape[0] // rows
    first = half_lanes(seq_len)
    key_at = lax.broadcasted_iota(jnp.int32, (seq_len, 1), 0)
    results = [[None, None] for _ in range(rows)]
    for head in range(2):
        bias = spread_bias(diagonal_ref[0, head : head + 1, :], seq_len)
        for row in range(rows):
            span = pl.ds(row * seq_len, seq_len)
            queries = query_ref[span, :]
            queries = jnp.where(first if head == 0 else ~first, queries, jnp.zeros_like(queries))
            scores = dot_nt(key_ref[span, :], queries) + bias
            scores = jnp.where(key_at < lengths_ref[row], scores, NEG)
            largest = jnp.max(scores, axis=0, keepdims=True)
            raised = jnp.exp(scores - largest)
            totals = jnp.sum(raised, axis=0, keepdims=True)
            probs = (raised * (1.0 / totals)).astype(LOW)
            results[row][head] = dot_tn(probs, value_ref[span, :])
            log_ref[0, 2 * row + head : 2 * row + head + 1, :] = largest + jnp.log(totals)
    for row in range(rows):
        out_ref[pl.ds(row * seq_len, seq_len), :] = jnp.where(first, *results[row]).astype(LOW)


def attend(lengths, diagonal, joint, heads):
    tokens = joint.shape[0]
    pairs = heads // 2
    rows = lengths.shape[0]
    seq_len = tokens // rows
    return pl.pallas_call(
        attend_kernel,
        grid=(pairs,),
        in_specs=[
            pl.BlockSpec(memory_space=pltpu.SMEM),
            pl.BlockSpec((1, 2, 2 * seq_len), lambda p: (p, 0, 0)),
            pl.BlockSpec((tokens, PAIR), lambda p: (0, p)),
            pl.BlockSpec((tokens, PAIR), lambda p: (0, pairs + p)),
            pl.BlockSpec((tokens, PAIR), lambda p: (0, 2 * pairs + p)),
        ],
        out_specs=[
            pl.BlockSpec((tokens, PAIR), lambda p: (0, p)),
            pl.BlockSpec((1, 2 * rows, seq_len), lambda p: (p, 0, 0)),
        ],
        out_shape=[
            jax.ShapeDtypeStruct((tokens, pairs * PAIR), LOW),
            jax.ShapeDtypeStruct((pairs, 2 * rows, seq_len), F32),
        ],
        compiler_params=params(),
        cost_estimate=cost(16),
        name="attend",
    )(lengths, diagonal.reshape(pairs, 2, 2 * seq_len), joint, joint, joint)


def attend_back_kernel(
    lengths_ref, diagonal_ref, query_ref, key_ref, value_ref, grad_ref, log_ref, *outs
):
    query_out, key_out, value_out, bias_out = outs[-4:]
    rows = lengths_ref.shape[0]
    seq_len = query_ref.shape[0] // rows
    first = half_lanes(seq_len)
    key_at = lax.broadcasted_iota(jnp.int32, (seq_len, 1), 0)
    results = [[None, None] for _ in range(rows)]
    for head in range(2):
        bias = spread_bias(diagonal_ref[0, head : head + 1, :], seq_len)
        keep = first if head == 0 else ~first
        total = None
        for row in range(rows):
            span = pl.ds(row * seq_len, seq_len)
            queries = query_ref[span, :]
            keys = key_ref[span, :]
            values = value_ref[span, :]
            grads = grad_ref[span, :]
            only = jnp.where(keep, queries, jnp.zeros_like(queries))
            scores = dot_nt(keys, only) + bias
            scores = jnp.where(key_at < lengths_ref[row], scores, NEG)
            probs = jnp.exp(scores - log_ref[0, 2 * row + head : 2 * row + head + 1, :])
            grad_values = dot(probs.astype(LOW), grads)
            grad_only = jnp.where(keep, grads, jnp.zeros_like(grads))
            grad_probs = dot_nt(values, grad_only)
            weighted = jnp.sum(probs * grad_probs, axis=0, keepdims=True)
            grad_scores = (probs * (grad_probs - weighted)).astype(LOW)
            grad_keys = dot(grad_scores, queries)
            grad_queries = dot_tn(grad_scores, keys)
            wide = grad_scores.astype(F32)
            total = wide if total is None else total + wide
            results[row][head] = (grad_queries, grad_keys, grad_values)
        bias_out[0, head : head + 1, :] = gather_bias(total)
    for row in range(rows):
        span = pl.ds(row * seq_len, seq_len)
        for out_ref, one, two in zip((query_out, key_out, value_out), *results[row]):
            out_ref[span, :] = jnp.where(first, one, two).astype(LOW)


def attend_back(lengths, diagonal, joint, grad_attended, logs, heads, first, count, before=()):
    tokens = joint.shape[0]
    pairs = heads // 2
    rows = lengths.shape[0]
    seq_len = tokens // rows
    part = pl.BlockSpec((tokens, PAIR), lambda p: (0, first + p))
    whole = jax.ShapeDtypeStruct((tokens, pairs * PAIR), LOW)
    lines = pl.BlockSpec((1, 2, 2 * seq_len), lambda p: (first + p, 0, 0))
    return pl.pallas_call(
        attend_back_kernel,
        grid=(count,),
        in_specs=[
            pl.BlockSpec(memory_space=pltpu.SMEM),
            lines,
            part,
            pl.BlockSpec((tokens, PAIR), lambda p: (0, pairs + first + p)),
            pl.BlockSpec((tokens, PAIR), lambda p: (0, 2 * pairs + first + p)),
            part,
            pl.BlockSpec((1, 2 * rows, seq_len), lambda p: (first + p, 0, 0)),
        ]
        + [pl.BlockSpec(memory_space=pl.ANY)] * len(before),
        out_specs=[part, part, part, lines],
        out_shape=[whole, whole, whole, jax.ShapeDtypeStruct((pairs, 2, 2 * seq_len), F32)],
        input_output_aliases={7 + i: i for i in range(len(before))},
        compiler_params=params(),
        cost_estimate=cost(4.4 * count),
        name="attend_back",
    )(lengths, diagonal.reshape(pairs, 2, 2 * seq_len), joint, joint, joint, grad_attended, logs, *before)


def weight_copy(me, number, load, refs, targets, semaphores):
    source, target, column, relative, shard_rows, first, start, rows = load
    width = refs[source].shape[1]
    place = first if relative is None else pl.multiple_of((me ^ relative) * shard_rows + first, 16)
    return pltpu.make_async_copy(
        refs[source].at[pl.ds(start, rows), :],
        targets[target].at[pl.ds(place, rows), pl.ds(column, width)],
        semaphores.at[number],
    )


def weights_of(me_ref, plans, refs, targets, semaphores):
    def each(act):
        for value, loads in enumerate(plans):

            @pl.when(me_ref[1] == value)
            def _():
                for number, load in enumerate(loads):
                    act(number, load)

    def start():
        each(lambda number, load: weight_copy(me_ref[0], number, load, refs, targets, semaphores).start())

    def wait(target):
        def act(number, load):
            if load[1] == target:
                weight_copy(me_ref[0], number, load, refs, targets, semaphores).wait()

        @pl.when(pl.program_id(0) == 0)
        def _():
            each(act)

    return start, wait


def plan_loads(pieces, sections):
    loads = []
    for source, (relative, first, part) in enumerate(pieces):
        start = 0
        for target, rows, column, shard_rows, offset in sections:
            low = max(start, first)
            high = min(start + rows, first + part.shape[0])
            if low < high:
                loads.append((source, target, column, relative, shard_rows, offset + low - start, low - first, high - low))
            start += rows
    return loads


def front_kernel(loads, count, me_ref, slot_ref, reply_ref, gain_ref, *rest):
    refs, (x_ref, normed_ref, joint_ref), (weight, semaphores) = rest[:count], rest[count : count + 3], rest[count + 3 :]

    start, wait = weights_of(me_ref, loads, refs, [weight], semaphores)
    pl.when(pl.program_id(0) == 0)(start)
    rows = slot_ref.shape[0]
    slots = reply_ref.shape[0]
    hot = slot_ref[...] == lax.broadcasted_iota(jnp.int32, (rows, slots), 1)
    x = dot(hot.astype(F32).astype(LOW), reply_ref[...])
    x_ref[...] = x.astype(LOW)
    scale = lax.rsqrt(jnp.mean(x * x, axis=-1, keepdims=True) + EPS)
    normed = (x * scale * gain_ref[...]).astype(LOW)
    normed_ref[...] = normed
    wait(0)
    joint_ref[...] = dot(normed, weight[...]).astype(LOW)


ANY = pl.BlockSpec(memory_space=pl.ANY)
SMEM = pl.BlockSpec(memory_space=pltpu.SMEM)
BLOCK = 256


def full(shape):
    return pl.BlockSpec(shape, lambda *ids: (0,) * len(shape))


def down(width, rows=BLOCK):
    return pl.BlockSpec((rows, width), lambda i: (i, 0))


def front(me, slot, replies, gain, pieces, loads, width):
    tokens = slot.shape[0]
    model = replies.shape[1]
    return pl.pallas_call(
        functools.partial(front_kernel, loads, len(pieces)),
        grid=(tokens // BLOCK,),
        in_specs=[SMEM, down(1), full(replies.shape), full((1, model))] + [ANY] * len(pieces),
        out_specs=[down(model), down(model), down(width)],
        out_shape=[
            jax.ShapeDtypeStruct((tokens, model), LOW),
            jax.ShapeDtypeStruct((tokens, model), LOW),
            jax.ShapeDtypeStruct((tokens, width), LOW),
        ],
        scratch_shapes=[pltpu.VMEM((model, width), LOW), pltpu.SemaphoreType.DMA((max(len(plan) for plan in loads),))],
        compiler_params=params(),
        cost_estimate=cost(15),
        name="front",
    )(me, slot, replies, gain, *pieces)


def ffn_kernel(loads, count, me_ref, x_ref, attended_ref, d_out_ref, seed_ref, gain_ref, *rest):
    refs = rest[:count]
    (y_ref, act_ref, grad_pre_ref, grad_low_ref, normed_ref, hidden_out, low_out, attended_out, gain_out) = rest[count : count + 9]
    w_out, w_in, w_back, semaphores = rest[count + 9 :]

    start_weights, wait = weights_of(me_ref, loads, refs, [w_out, w_in, w_back], semaphores)

    @pl.when(pl.program_id(0) == 0)
    def _():
        start_weights()
        gain_out[...] = jnp.zeros_like(gain_out)

    wait(0)
    hidden = x_ref[...].astype(F32) + dot(attended_ref[...], w_out[...])
    scale = lax.rsqrt(jnp.mean(hidden * hidden, axis=-1, keepdims=True) + EPS)
    unit = hidden * scale
    gain = gain_ref[...]
    normed = (unit * gain).astype(LOW)
    normed_ref[...] = normed
    grad_out = d_out_ref[...].astype(F32) * seed_ref[...]
    grad_low = grad_out.astype(LOW)
    grad_low_ref[...] = grad_low
    wait(1)
    wait(2)
    result = hidden
    back = jnp.zeros_like(hidden)
    model = hidden.shape[1]
    for start in range(0, w_in.shape[1], model):
        span = pl.ds(start, model)
        pre = dot(normed, w_in[:, span])
        square = pre * pre
        tanh = jnp.tanh(ROOT * (pre + CUBE * square * pre))
        half = 0.5 * (1.0 + tanh)
        act = (pre * half).astype(LOW)
        slope = half + 0.5 * pre * (1.0 - tanh * tanh) * ROOT * (1.0 + 3.0 * CUBE * square)
        act_ref[:, span] = act
        result = result + dot(act, w_back[span, :])
        grad_pre = (dot_nt(grad_low, w_back[span, :]) * slope).astype(LOW)
        grad_pre_ref[:, span] = grad_pre
        back = back + dot_nt(grad_pre, w_in[:, span])
    y_ref[...] = result.astype(LOW)
    gain_out[...] += jnp.sum(back * unit, axis=0, keepdims=True)
    scaled = back * gain
    grad_hidden = grad_out + scale * (scaled - unit * jnp.mean(scaled * unit, axis=-1, keepdims=True))
    hidden_out[...] = grad_hidden
    low = grad_hidden.astype(LOW)
    low_out[...] = low
    attended_out[...] = dot_nt(low, w_out[...]).astype(LOW)


def ffn(me, x, attended, d_out, seed, gain, pieces, loads, inner, ff_width):
    tokens, model = x.shape
    low = jax.ShapeDtypeStruct((tokens, model), LOW)
    wide = jax.ShapeDtypeStruct((tokens, ff_width), LOW)
    return pl.pallas_call(
        functools.partial(ffn_kernel, loads, len(pieces)),
        grid=(tokens // BLOCK,),
        in_specs=[SMEM, down(model), down(inner), down(model), down(1), full((1, model))] + [ANY] * len(pieces),
        out_specs=[
            down(model), down(ff_width), down(ff_width), down(model), down(model), down(model), down(model), down(inner),
            full((1, model)),
        ],
        out_shape=[
            low, wide, wide, low, low, jax.ShapeDtypeStruct((tokens, model), F32), low,
            jax.ShapeDtypeStruct((tokens, inner), LOW), jax.ShapeDtypeStruct((1, model), F32),
        ],
        scratch_shapes=[
            pltpu.VMEM((inner, model), LOW),
            pltpu.VMEM((model, ff_width), LOW),
            pltpu.VMEM((ff_width, model), LOW),
            pltpu.SemaphoreType.DMA((max(len(plan) for plan in loads),)),
        ],
        compiler_params=params(),
        cost_estimate=cost(35),
        name="ffn",
    )(me, x, attended, d_out, seed, gain, *pieces)


def project_back_kernel(loads, count, me_ref, query_ref, key_ref, value_ref, x_ref, hidden_ref, gain_ref, *rest):
    refs, (out_ref, gain_out), (weight, semaphores) = rest[:count], rest[count : count + 2], rest[count + 2 :]

    start_weights, wait = weights_of(me_ref, loads, refs, [weight], semaphores)

    @pl.when(pl.program_id(0) == 0)
    def _():
        start_weights()
        gain_out[...] = jnp.zeros_like(gain_out)

    wait(0)
    inner = query_ref.shape[1]
    back = dot_nt(query_ref[...], weight[:, :inner])
    back = back + dot_nt(key_ref[...], weight[:, inner : 2 * inner])
    back = back + dot_nt(value_ref[...], weight[:, 2 * inner :])
    x = x_ref[...].astype(F32)
    scale = lax.rsqrt(jnp.mean(x * x, axis=-1, keepdims=True) + EPS)
    unit = x * scale
    gain_out[...] += jnp.sum(back * unit, axis=0, keepdims=True)
    scaled = back * gain_ref[...]
    grad = hidden_ref[...] + scale * (scaled - unit * jnp.mean(scaled * unit, axis=-1, keepdims=True))
    out_ref[...] = grad.astype(LOW)


def project_back(me, grads, x, grad_hidden, gain, pieces, loads):
    tokens, model = x.shape
    inner = grads[0].shape[1]
    return pl.pallas_call(
        functools.partial(project_back_kernel, loads, len(pieces)),
        grid=(tokens // BLOCK,),
        in_specs=[SMEM] + [down(inner)] * 3 + [down(model), down(model), full((1, model))] + [ANY] * len(pieces),
        out_specs=[down(model), full((1, model))],
        out_shape=[jax.ShapeDtypeStruct((tokens, model), LOW), jax.ShapeDtypeStruct((1, model), F32)],
        scratch_shapes=[pltpu.VMEM((model, 3 * inner), LOW), pltpu.SemaphoreType.DMA((max(len(plan) for plan in loads),))],
        compiler_params=params(),
        cost_estimate=cost(11),
        name="project_back",
    )(me, *grads, x, grad_hidden, gain, *pieces)


def store_shards(me, value, shards, first, keep_ref, send_ref):
    rows = value.shape[0] // shards
    for shard in range(shards):
        relative = me ^ shard
        part = value[shard * rows : (shard + 1) * rows, :].astype(LOW)

        @pl.when(relative % 2 == 0)
        def _():
            keep_ref[relative // 2, pl.ds(first, rows), :] = part

        @pl.when(relative % 2 == 1)
        def _():
            send_ref[relative // 2, pl.ds(first, rows), :] = part


def blocks_grad_kernel(me_ref, keep_left, send_left, right_ref, keep_ref, send_ref):
    right = right_ref[...]
    keep_ref[0] = dot_tn(keep_left[...], right).astype(LOW)
    send_ref[0] = dot_tn(send_left[...], right).astype(LOW)


def columns_grad_kernel(shards, me_ref, left_ref, right_ref, unused_keep, unused_send, keep_ref, send_ref):
    store_shards(me_ref[0], dot_tn(left_ref[...], right_ref[...]), shards, 0, keep_ref, send_ref)


def add_columns(me, left, right, shards, keep, send, start):
    tokens, model = left.shape
    rows = model // shards
    shape = jax.ShapeDtypeStruct(keep.shape, LOW)
    cuts = right.shape[1] // model
    out = pl.BlockSpec((shards // 2, rows, model), lambda i: (0, start // rows + i, 0))
    return pl.pallas_call(
        functools.partial(columns_grad_kernel, shards),
        grid=(cuts,),
        in_specs=[SMEM, full((tokens, model)), pl.BlockSpec((tokens, model), lambda i: (0, i)), ANY, ANY],
        out_specs=[out, out],
        out_shape=[shape, shape],
        input_output_aliases={3: 0, 4: 1},
        compiler_params=params(),
        cost_estimate=cost(1 + 2.5 * cuts),
        name="columns_grad",
    )(me, left, right, keep, send)


def ffn_grads(me, act, grad_low, normed, grad_pre, attended, hidden_low, shards):
    tokens, model = grad_low.shape
    wide = act.shape[1]
    first = wide // shards
    rows = model // shards
    cuts = wide // model
    shape = jax.ShapeDtypeStruct((shards // 2, first + (cuts + 1) * rows, model), LOW)
    out = pl.BlockSpec((1, first, model), lambda i, me: (i, 0, 0))
    keep, send = pl.pallas_call(
        blocks_grad_kernel,
        grid_spec=pltpu.PrefetchScalarGridSpec(
            num_scalar_prefetch=1,
            grid=(shards // 2,),
            in_specs=[
                pl.BlockSpec((tokens, first), lambda i, me: (0, me[0] ^ (2 * i))),
                pl.BlockSpec((tokens, first), lambda i, me: (0, me[0] ^ (2 * i + 1))),
                pl.BlockSpec((tokens, model), lambda i, me: (0, 0)),
            ],
            out_specs=[out, out],
        ),
        out_shape=[shape, shape],
        compiler_params=params(),
        cost_estimate=cost(9),
        name="back_grad",
    )(me, act, act, grad_low)
    keep, send = add_columns(me, normed, grad_pre, shards, keep, send, first)
    return add_columns(me, attended, hidden_low, shards, keep, send, first + cuts * rows)


SMALL_ROWS = 16


def rest_grads_kernel(shards, me_ref, normed_ref, query_ref, key_ref, value_ref, small_ref, keep_ref, send_ref):
    rows = normed_ref.shape[1] // shards
    me = me_ref[0]
    start = 0
    for right_ref in (query_ref, key_ref, value_ref):
        store_shards(me, dot_tn(normed_ref[...], right_ref[...]), shards, start, keep_ref, send_ref)
        start += rows
    store_shards(me, small_ref[...], shards, start, keep_ref, send_ref)


def rest_grads(me, normed, grads, small, shards):
    tokens, model = normed.shape
    shape = jax.ShapeDtypeStruct((shards // 2, 3 * (model // shards) + SMALL_ROWS, model), LOW)
    return pl.pallas_call(
        functools.partial(rest_grads_kernel, shards),
        in_specs=[SMEM] + [full((tokens, model))] * 4 + [full(small.shape)],
        out_specs=[full(shape.shape)] * 2,
        out_shape=[shape, shape],
        compiler_params=params(),
        cost_estimate=cost(11),
        name="rest_grads",
    )(me, normed, *grads, small)


def place_kernel(count, slot_ref, choice_ref, *rest):
    options, (out_ref, tokens, semaphore) = rest[:count], rest[count:]

    @pl.when(pl.program_id(0) == 0)
    def _():
        for number, option in enumerate(options):

            @pl.when(choice_ref[0] == number)
            def _():
                copy = pltpu.make_async_copy(option, tokens, semaphore)
                copy.start()
                copy.wait()

    rows = out_ref.shape[0]
    at = lax.broadcasted_iota(jnp.int32, (rows, tokens.shape[0]), 0) + pl.program_id(0) * rows
    out_ref[...] = dot((at == slot_ref[...]).astype(F32).astype(LOW), tokens[...]).astype(LOW)


def place(slot, choice, options, slots):
    tokens, model = options[0].shape
    return pl.pallas_call(
        functools.partial(place_kernel, len(options)),
        grid=(slots // 512,),
        in_specs=[full((1, tokens)), SMEM] + [ANY] * len(options),
        out_specs=down(model, 512),
        out_shape=jax.ShapeDtypeStruct((slots, model), LOW),
        scratch_shapes=[pltpu.VMEM((tokens, model), LOW), pltpu.SemaphoreType.DMA],
        compiler_params=params(),
        cost_estimate=cost(6),
        name="place",
    )(slot, choice, *options)


TABLE_BLOCK = 512


def table_kernel(ids_ref, rows_ref, *rest):
    out_ref = rest[-1]
    rows = out_ref.shape[0]
    at = lax.broadcasted_iota(jnp.int32, (rows, ids_ref.shape[1]), 0) + pl.program_id(0) * rows
    total = dot((at == ids_ref[...]).astype(F32).astype(LOW), rows_ref[...])
    if len(rest) > 1:
        total = total + rest[0][...]
    out_ref[...] = total


def add_to_table(ids, token_rows, before, vshard):
    model = token_rows.shape[1]
    more = [] if before is None else [before]
    return pl.pallas_call(
        table_kernel,
        grid=(pl.cdiv(vshard, TABLE_BLOCK),),
        in_specs=[full(ids.shape), full(token_rows.shape)] + [down(model, TABLE_BLOCK)] * len(more),
        out_specs=down(model, TABLE_BLOCK),
        out_shape=jax.ShapeDtypeStruct((vshard, model), F32),
        input_output_aliases={2: 0} if more else {},
        compiler_params=params(),
        cost_estimate=cost(18),
        name="table_rows",
    )(ids, token_rows, *more)


def flip(value, bits):
    shards = lax.axis_size("fsdp")
    return lax.ppermute(value, "fsdp", [(i, i ^ bits) for i in range(shards)])


def flip_line(value, bits):
    groups = lax.axis_size("dp")
    return lax.ppermute(value, "dp", [(i, i ^ bits) for i in range(groups)])


def after(value, *others):
    return lax.optimization_barrier((value,) + others)[0]


def exchange(value):
    return lax.all_to_all(value, "fsdp", split_axis=0, concat_axis=0, tiled=True)


def gather_near(own):
    return own, flip(own, 2), flip(own, 4)


def gather_far(near):
    own, by_x, by_y = near
    half = own.shape[0] // 32 * 16
    pieces = [(0, 0, own), (2, 0, by_x), (4, 0, by_y)]
    return pieces + [(6, 0, flip(by_y[:half], 2)), (6, half, flip(by_x[half:], 4))]


def gather_core(pieces):
    return pieces + [(bits ^ 1, first, flip(part, 1)) for bits, first, part in pieces]


def scatter_first(keep, arrived):
    rows = keep.shape[1]
    half = rows // 32 * 16
    across = (keep[3].astype(F32) + arrived[3].astype(F32)).astype(LOW)
    return flip(across[:half], 2), flip(across[half:], 4)


def scatter_between(keep, arrived, from_x, from_y):
    rows, columns = keep.shape[1:]
    half = from_x.shape[0]
    pad_x = jnp.concatenate([from_x, jnp.zeros((rows - half, columns), LOW)])
    pad_y = jnp.concatenate([jnp.zeros((half, columns), LOW), from_y])
    to_y = (keep[2].astype(F32) + arrived[2].astype(F32) + pad_x.astype(F32)).astype(LOW)
    to_x = (keep[1].astype(F32) + arrived[1].astype(F32) + pad_y.astype(F32)).astype(LOW)
    return to_x, to_y


def scatter_second(to_x, to_y):
    return flip(to_x, 2), flip(to_y, 4)


def scatter_last(keep, arrived, by_x, by_y):
    return (keep[0].astype(F32) + arrived[0].astype(F32) + by_x.astype(F32) + by_y.astype(F32)).astype(LOW)


def bucket_of(offset):
    distance = jnp.abs(offset)
    far_bucket = 8 + sum(((distance >= limit).astype(jnp.int32) for limit in LIMITS))
    upper = jnp.where(offset > 0, 16, 0).astype(jnp.int32)
    return upper + jnp.where(distance < 8, distance, far_bucket)


def per_device(
    token_ids,
    task_ids,
    lengths,
    instruction,
    table,
    attn_gain,
    w_query,
    w_key,
    w_value,
    w_out,
    ffn_gain,
    w_in,
    w_back,
    rel_bias,
    d_out,
):
    rows_dev, seq_len = token_ids.shape
    vshard, model = table.shape
    inner = w_query.shape[1]
    ff_width = w_in.shape[1]
    heads = rel_bias.shape[1]
    shards = lax.axis_size("fsdp")
    groups = lax.axis_size("dp")
    me = lax.axis_index("fsdp")
    at = lax.axis_index("dp")
    odd = at % 2
    me_ref = jnp.stack([me, odd]).astype(jnp.int32)
    tokens = rows_dev * seq_len
    capacity = 2 * tokens // shards
    task_count = rows_dev * groups * shards // 4
    own_gain = attn_gain.shape[0]
    buckets = rel_bias.shape[0] * shards

    flat_ids = token_ids.reshape(tokens)
    owner = flat_ids // vshard
    local_row = flat_ids - owner * vshard
    owner_hot = (owner[:, None] == jnp.arange(shards, dtype=jnp.int32)[None, :]).astype(LOW)
    token_at = jnp.arange(tokens, dtype=jnp.int32)
    before = (token_at[:, None] > token_at[None, :]).astype(LOW)
    ranks = jnp.dot(before, owner_hot, preferred_element_type=F32)
    rank_within = jnp.sum(ranks * owner_hot.astype(F32), axis=1).astype(jnp.int32)
    slot = owner * capacity + rank_within
    slots = jnp.arange(shards * capacity, dtype=jnp.int32)
    slot_hot = slots[:, None] == slot[None, :]
    requests = (jnp.sum(jnp.where(slot_hot, local_row[None, :] + 1, 0), axis=1) - 1).reshape(shards, capacity)
    small = jnp.concatenate([attn_gain, ffn_gain, rel_bias.reshape(-1)])
    small_size = small.shape[0]
    joint_own = jnp.concatenate([w_query, w_key, w_value], axis=1)
    own_rows = w_query.shape[0]
    cuts = ff_width // model
    split = shards == 8 and groups == 4
    if split:
        extra = jnp.pad(small, (0, 16 * 3 * inner - small_size)).reshape(16, 3 * inner)
        joint_near = gather_near(jnp.concatenate([joint_own, extra]))
        slab = jnp.concatenate([w_out] + [w_in[:, i * model : (i + 1) * model] for i in range(cuts)] + [w_back])
        half_rows = slab.shape[0] // 2
        ffn_near = gather_near(lax.dynamic_slice_in_dim(slab, odd * half_rows, half_rows))
    task_rows = jnp.broadcast_to(task_ids[None, :], (shards, rows_dev))
    told = exchange(jnp.concatenate([requests, task_rows], axis=1))
    if split:
        told = after(told, *joint_near)
        joint_pieces = gather_far(joint_near)
    asked = told[:, :capacity]
    task_hot = (told[:, capacity:].reshape(-1, 1) == jnp.arange(task_count, dtype=jnp.int32)[None, :]).astype(jnp.int32)
    plane_counts = jnp.sum(task_hot, axis=0)
    looked = jnp.take(table, jnp.maximum(asked, 0).reshape(-1), axis=0)
    if split:
        looked = after(looked, *ffn_near, *(part for unused_bits, unused_first, part in joint_pieces))
        joint_pieces = gather_core(joint_pieces)
        joint_loads = [plan_loads(joint_pieces, [(0, own_rows, 0, own_rows, 0)])] * 2
        lines = {
            bits: part[own_rows - first, :small_size]
            for bits, first, part in joint_pieces
            if first <= own_rows < first + part.shape[0]
        }
        small_all = jnp.stack([lines[bits] for bits in range(shards)])[jnp.arange(shards) ^ me]
        joint_pieces = [part for unused_bits, unused_first, part in joint_pieces]
    replies = exchange(looked.reshape(shards, capacity, model)).reshape(shards * capacity, model)
    if split:
        halves = gather_far(tuple(after(part, looked) for part in ffn_near))[1:]
        others = [(bits, first, flip_line(part, 1)) for bits, first, part in halves]
        replies = after(replies, *(part for unused_bits, unused_first, part in halves + others[:2]))
    if not split:
        joint_pieces, small_all, *ffn_pieces = (
            lax.all_gather(part, "fsdp", axis=0, tiled=True) for part in (joint_own, small[None], w_out, w_in, w_back)
        )
        joint_pieces = [joint_pieces]
        joint_loads = [[(0, 0, 0, None, 0, 0, 0, model)]] * 2
        ffn_loads = [[(i, i, 0, None, 0, 0, 0, part.shape[0]) for i, part in enumerate(ffn_pieces)]] * 2
    first_gain = small_all[:, :own_gain].reshape(1, model).astype(F32)
    second_gain = small_all[:, own_gain : 2 * own_gain].reshape(1, model).astype(F32)
    rel_all = small_all[:, 2 * own_gain :].reshape(buckets, heads).astype(F32)

    message = jnp.concatenate([slot, requests.reshape(-1), plane_counts])
    message = after(message, replies)
    slot_of = [slot]
    away = []
    counts = plane_counts
    for bits in range(1, groups):
        theirs = flip_line(message, bits)
        slot_of.append(theirs[:tokens])
        away.append(theirs[tokens : tokens + shards * capacity].reshape(shards, capacity))
        counts = counts + theirs[tokens + shards * capacity :]
    away = jnp.stack(away, axis=1)
    own_hot = (task_ids[:, None] == jnp.arange(task_count, dtype=jnp.int32)[None, :]).astype(F32)
    row_weight = 1.0 / jnp.sum(own_hot * counts.astype(F32)[None, :], axis=1)
    positions = jnp.arange(seq_len, dtype=jnp.int32)
    pool_mask = ((positions[None, :] < lengths[:, None]) & (instruction == 0)).astype(F32)
    seed = (pool_mask * row_weight[:, None]).reshape(tokens, 1)

    offsets = (seq_len - 1) - jnp.arange(2 * seq_len, dtype=jnp.int32)
    bucket_hot = (jnp.arange(buckets, dtype=jnp.int32)[:, None] == bucket_of(offsets)[None, :]).astype(F32)
    diagonal = lax.dot_general(rel_all, bucket_hot, (((0,), (0,)), ((), ())), precision=HIGH)

    x, normed_one, joint = front(me_ref, slot[:, None], replies, first_gain, joint_pieces, joint_loads, 3 * inner)
    away = exchange(after(away, joint))
    asked_of = [asked] + [away[:, i] for i in range(groups - 1)]
    joint = after(joint, counts)
    if split:
        joint = after(joint, *(part for unused_bits, unused_first, part in others))
        owns = gather_core([(0, 0, after(slab, replies))])
        halves = gather_core([(bits, first, after(part, replies)) for bits, first, part in halves])
        others = gather_core([(bits, first, after(part, joint)) for bits, first, part in others])
        sections = [(0, own_rows, 0, own_rows, 0)]
        sections += [(1, own_rows, i * model, own_rows, 0) for i in range(cuts)]
        sections += [(2, w_back.shape[0], 0, w_back.shape[0], 0)]
        ffn_loads = []
        for at_half in (0, half_rows):
            near = [(bits, first + at_half, part) for bits, first, part in halves]
            away_half = [(bits, first + half_rows - at_half, part) for bits, first, part in others]
            ffn_loads.append(plan_loads(owns + near + away_half, sections))
        ffn_pieces = [part for unused_bits, unused_first, part in owns + halves + others]
    attended, logs = attend(lengths, diagonal, joint, heads)
    result, act, grad_pre, grad_low, normed_two, grad_hidden, hidden_low, grad_attended, grad_second = ffn(
        me_ref, x, after(attended, away), d_out.reshape(tokens, model), seed, second_gain, ffn_pieces, ffn_loads, inner, ff_width
    )
    backward = functools.partial(attend_back, lengths, diagonal, joint)
    if split:
        keep, send = ffn_grads(me_ref, act, grad_low, normed_two, grad_pre, attended, hidden_low, shards)
        arrived = flip(send, 1)
        grads = backward(after(grad_attended, send), logs, heads, 0, 2)
        first_hop = scatter_first(keep, after(arrived, *grads))
        grads = backward(after(grad_attended, arrived, *grads), logs, heads, 2, 3, grads)
        between = scatter_between(keep, arrived, *(after(part, *grads) for part in first_hop))
        second_hop = scatter_second(*between)
        grads = backward(after(grad_attended, *between), logs, heads, 5, 1, grads)
    else:
        grads = backward(grad_attended, logs, heads, 0, heads // 2)
    *grad_joint, bias_sums = grads
    bias_sums = bias_sums.reshape(heads, 2 * seq_len)
    grad_rel = lax.dot_general(bucket_hot, bias_sums, (((1,), (1,)), ((), ())), precision=HIGH)
    token_grads, grad_first = project_back(me_ref, grad_joint, x, grad_hidden, first_gain, joint_pieces, joint_loads)
    small_grad = jnp.concatenate(
        [grad_first.reshape(shards, -1), grad_second.reshape(shards, -1), grad_rel.reshape(shards, -1)], axis=1
    )

    def shift(sent, step, *gates):
        pairs = [(i, i + 1) for i in range(step - 1, groups - 1)]
        back = [(groups - 1 - i, groups - 1 - j) for i, j in pairs]
        to_right, to_left = (after(part, *gates) for part in sent)
        return lax.ppermute(to_right, "dp", pairs), lax.ppermute(to_left, "dp", back)

    def shift(sent, step):
        pairs = [(i, i + 1) for i in range(max(step - 2, 0), groups - 1)]
        back = [(groups - 1 - i, groups - 1 - j) for i, j in pairs]
        to_right, to_left = sent
        if split and step > 1:
            to_right = to_right + jnp.where(at == step - 2, ffn_rows, jnp.zeros((), LOW))
            to_left = to_left + jnp.where(at == groups + 1 - step, ffn_rows, jnp.zeros((), LOW))
        return lax.ppermute(to_right, "dp", pairs), lax.ppermute(to_left, "dp", back)

    def place_from(number, passed, *gates):
        distance = (at ^ number) - at
        steps = sorted({(i ^ number) - i for i in range(groups)})
        options = [passed[abs(step)][step > 0] for step in steps]
        choice = sum((distance == step).astype(jnp.int32) * i for i, step in enumerate(steps))
        return place(after(slot_of[number][None, :], *gates), choice.reshape(1), options, shards * capacity)

    def table_rows(number, incoming, table_grad):
        return add_to_table(asked_of[number].reshape(1, -1), incoming, table_grad, vshard)

    gates = ()
    if split:
        small_rows = jnp.pad(small_grad[:, None], ((0, 0), (0, SMALL_ROWS - 1), (0, model - small_size)))
        small_rows = small_rows.reshape(shards * SMALL_ROWS, model)
        rest_keep, rest_send = rest_grads(me_ref, normed_one, grad_joint, small_rows, shards)
        gates = second_hop + (rest_send,)
    passed = [(token_grads, token_grads)]
    rows = place_from(0, passed, *gates)
    came = table_grad = None
    extras = second_hop if split else ()
    for number in range(groups):
        incoming = exchange(rows.reshape(shards, capacity, model)).reshape(shards * capacity, model)
        if number > 0:
            table_grad = table_rows(number - 1, came, table_grad)
        if split and number == 0:
            ffn_sum = scatter_last(keep, arrived, *extras)
            ffn_rows = jnp.pad(ffn_sum, ((0, tokens - ffn_sum.shape[0]), (0, 0)))
            rest_arrived = flip(rest_send, 1)
            extras = scatter_first(rest_keep, rest_arrived)
        elif split and number == 1:
            extras = (after(part, table_grad) for part in extras)
            extras = scatter_second(*scatter_between(rest_keep, rest_arrived, *extras))
        elif split:
            extras = tuple(after(part, table_grad) for part in extras)
            rest = scatter_last(rest_keep, rest_arrived, *extras) if number == 2 else extras[0] + extras[1]
            extras = (rest, flip_line(rest, number - 1))
        if split or number + 1 < groups:
            passed.append(shift(passed[-1], number + 1))
        if number + 1 < groups:
            rows = place_from(number + 1, passed)
            held = (incoming, rows, *passed[-1], *extras) + (() if table_grad is None else (table_grad,))
            held = lax.optimization_barrier(held)
            came, rows = held[:2]
            passed[-1] = held[2:4]
            extras = held[4 : 4 + len(extras)]
            table_grad = None if table_grad is None else held[-1]
    table_grad = table_rows(groups - 1, incoming, table_grad)

    if split:
        ffn_rows = after(ffn_rows, table_grad).astype(F32)
        extras = tuple(after(part, table_grad) for part in extras)
        for step in range(2, groups + 1):
            ffn_rows = ffn_rows + jnp.where(at == step - 1, passed[step][0], jnp.zeros((), LOW)).astype(F32)
            ffn_rows = ffn_rows + jnp.where(at == groups - step, passed[step][1], jnp.zeros((), LOW)).astype(F32)
        ffn_sum = ffn_rows[: ffn_sum.shape[0]]
        back_rows = w_back.shape[0]
        in_rows = ffn_sum[back_rows : back_rows + cuts * own_rows]
        grad_back = ffn_sum[:back_rows]
        grad_in = jnp.concatenate([in_rows[i * own_rows : (i + 1) * own_rows] for i in range(cuts)], axis=1)
        grad_out = ffn_sum[back_rows + cuts * own_rows :]
        rest = extras[0].astype(F32) + extras[1].astype(F32)
        grad_query, grad_key, grad_value = (rest[i * own_rows : (i + 1) * own_rows] for i in range(3))
        small_grad = rest[3 * own_rows, :small_size]
    else:

        def owned(left, right):
            part = dot_tn(left, right).astype(LOW)
            return lax.psum(lax.psum_scatter(part, "fsdp", scatter_dimension=0, tiled=True), "dp").astype(F32)

        grad_back = owned(act, grad_low)
        grad_in = owned(normed_two, grad_pre)
        grad_query, grad_key, grad_value = (owned(normed_one, grad) for grad in grad_joint)
        grad_out = owned(attended, hidden_low)
        small_grad = lax.psum(small_grad, ("dp", "fsdp"))[me]
    return (
        result.reshape(rows_dev, seq_len, model),
        table_grad,
        small_grad[:own_gain],
        grad_query,
        grad_key,
        grad_value,
        grad_out,
        small_grad[own_gain : 2 * own_gain],
        grad_in,
        grad_back,
        small_grad[2 * own_gain :].reshape(rel_bias.shape),
    )


def solution(mesh):
    both = ("dp", "fsdp")
    in_specs = (
        P(both, None),
        P(both),
        P(both),
        P(both, None),
        P("fsdp", None),
        P("fsdp"),
        P("fsdp", None),
        P("fsdp", None),
        P("fsdp", None),
        P("fsdp", None),
        P("fsdp"),
        P("fsdp", None),
        P("fsdp", None),
        P("fsdp", None),
        P(both, None, None),
    )
    out_specs = (
        P(both, None, None),
        P("fsdp", None),
        P("fsdp"),
        P("fsdp", None),
        P("fsdp", None),
        P("fsdp", None),
        P("fsdp", None),
        P("fsdp"),
        P("fsdp", None),
        P("fsdp", None),
        P("fsdp", None),
    )
    return jax.shard_map(per_device, mesh=mesh, in_specs=in_specs, out_specs=out_specs, check_vma=False)
```

time: 727 us -> 520 us (0.72)
  waiting for transfers between devices: 216 us -> 71.2 us
  blocking collectives: 66.7 us -> 0 us
  between operations: 15.5 us -> 2.2 us
  local copies, waits for them, and re-layouts: 62 us -> 50.1 us
  starting transfers between devices: 90 us -> 100 us
  other arithmetic: 34.2 us -> 43.3 us
    ppermute x90 -> x32, waiting for transfers between devices: 188 us -> 23.7 us  [flip(): return lax.ppermute(value, 'fsdp', [(i, i ^ bits) for i in range(shards)])]
    psum x1 -> x0, blocking collectives: 66.7 us -> none  [per_device(): small_grad = lax.psum(small_grad, ('dp', 'fsdp'))[me]]
    ppermute x90 -> x32, starting transfers between devices: 68.7 us -> 30.1 us  [flip(): return lax.ppermute(value, 'fsdp', [(i, i ^ bits) for i in range(shards)])]
    all_to_all x0 -> x7, starting transfers between devices: none -> 28.7 us  [exchange(): lax.all_to_all(value, 'fsdp', split_axis=0, concat_axis=0, tiled=True)]
    add x9, other arithmetic: 2.61 us -> 20.4 us  [the longest x2 7.53 us: shift(): to_left + jnp.where(at == groups + 1 - step, ffn_rows, jnp.zeros((), LOW))]
    ppermute x6 -> x8, waiting for transfers between devices: 25.5 us -> 42.2 us  [the longest x4 40 us: shift(): lax.ppermute(to_left, 'dp', back)]
    ppermute x5 -> x9, starting transfers between devices: 8.78 us -> 22.4 us  [flip_line(): return lax.ppermute(value, 'dp', [(i, i ^ bits) for i in range(groups)])]
    unnamed x156 -> x94, local copies, waits for them, and re-layouts: 22 us -> 8.93 us
  transfers between devices with their start and end apart: 102 -> 56, of which waited for: 32 -> 10; matrix products, arithmetic and copies ran while one was open for 13% -> 14% of each run, Pallas kernels for 20% -> 36%
where the time goes in v3:
time: 520 us; the launch traced here: 510 us
  Pallas kernels  242 us (47%)
  starting transfers between devices  100 us (19%)
  waiting for transfers between devices  71.2 us (14%)
  local copies, waits for them, and re-layouts  50.1 us (10%)
  other arithmetic  43.3 us (8%)
    pallas_call x4, Pallas kernels, add_to_table(): pl.pallas_call(table_kernel, grid=(pl.cdiv(vshard, TABLE_BLOCK),), in_spe...  73.1 us
    ppermute x4, waiting for transfers between devices, shift(): lax.ppermute(to_left, 'dp', back)  40 us
    pallas_call x1, Pallas kernels, ffn(): pl.pallas_call(functools.partial(ffn_kernel, loads, len(pieces)), grid=(t...  34.9 us
    ppermute x32, starting transfers between devices, flip(): return lax.ppermute(value, 'fsdp', [(i, i ^ bits) for i in range(shards)])  30.1 us
    pallas_call x3, Pallas kernels, attend_back(): pl.pallas_call(attend_back_kernel, grid=(count,), in_specs=[pl.BlockSpec(...  29.7 us
    all_to_all x7, starting transfers between devices, exchange(): lax.all_to_all(value, 'fsdp', split_axis=0, concat_axis=0, tiled=True)  28.7 us
    pallas_call x4, Pallas kernels, place(): pl.pallas_call(functools.partial(place_kernel, len(options)), grid=(slots...  28.3 us
    ppermute x32, waiting for transfers between devices, flip(): return lax.ppermute(value, 'fsdp', [(i, i ^ bits) for i in range(shards)])  23.7 us
  transfers between devices with their start and end apart: 56, of which 10 were waited for; matrix products, arithmetic and copies ran while one was open for 14% of the time, Pallas kernels for 36%

profile of v3, /device:TPU:0, one launch (start us, length us, event | category | flops | bytes accessed | tf_op | source)
XLA Modules:
  0.0 510.1 jit_solution(7951305475891192485)
XLA Ops:
  3.5 3.0 collective-permute-start.1
  10.8 3.3 all-to-all-start
  15.4 1.9 collective-permute-start.3
  26.9 12.0 %gather_fusion = bf16[2048,768]{1,0:T(8,128)(2,1)S(1)} fusion(bf16[4016,768]{1,0:T(8,128)(2,1)} %param.19, s32[2048]{0:T(1024)S(1)} %broadcast_clamp_fusion), kind=kCustom, calls=%fused_computation | custom fusion | bytes 6299648 | tf_op jit(solution)/shard_map/jit(_take)/gather | solution.py:701
  40.8 3.7 all-to-all-start.1
  47.9 2.1 fusion.16.slot_ref
  66.3 22.1 %collective-permute-done.6.rest_4_ = bf16[208,768]{1,0:T(8,128)(2,1)} collective-permute-done((bf16[208,768]{1,0:T(8,128)(2,1)}, bf16[208,768]{1,0:T(8,128)(2,1)}, u32[]{:S(2)}, u32[]{:S(2)}) %collective-permute-start.6) | collective-permute-done | bytes 319520 | tf_op jit(solution)/shard_map/ppermute | solution.py:572
  90.5 3.7 collective-permute-start.17
  94.9 15.1 %front.1 = (bf16[1024,768]{1,0:T(8,128)(2,1)}, bf16[1024,768]{1,0:T(8,128)(2,1)}, bf16[1024,2304]{1,0:T(8,128)(2,1)}) custom-call(s32[2]{0:T(128)} %pad_add_fusion.3.me_ref, s32[1024,1]{1,0:T(8,128)} %fusion.16.slot_ref, bf16[2048,768]{1,0:T(8,128)(2,1)} %bitcast.117, f32[1,768]{1,0:T(1,128)} %reshape.466.gain_ref, bf16[112,2304]{1,0:T(8,128)(2,1)} %copy-done.18, ...), custom_call_target="tpu_custom_call" | custom-call | flops 17250000896 | bytes 54000000 | tf_op jit(solution)/shard_map/front/pallas_call | solution.py:273
  113.8 3.6 all-to-all-start.2
  118.5 15.9 %attend.1 = (bf16[1024,768]{1,0:T(8,128)(2,1)}, f32[6,4,512]{2,1,0:T(4,128)}) custom-call(s32[2]{0:T(128)} %lengths_ref.7, f32[6,2,1024]{2,1,0:T(2,128)} %copy.88.diagonal_ref, bf16[1024,2304]{1,0:T(8,128)(2,1)} %get-tuple-element.111.query_ref.key_ref.value_ref, bf16[1024,2304]{1,0:T(8,128)(2,1)} %get-tuple-element.111.query_ref.key_ref.value_ref, ...), custom_call_target="tpu_custom_call" | custom-call | flops 18400000000 | bytes 57600000 | tf_op jit(solution)/shard_map/attend/pallas_call | solution.py:98
  137.3 34.9 %ffn.1 = (bf16[1024,768]{1,0:T(8,128)(2,1)}, bf16[1024,3072]{1,0:T(8,128)(2,1)}, bf16[1024,3072]{1,0:T(8,128)(2,1)}, bf16[1024,768]{1,0:T(8,128)(2,1)}, bf16[102...) custom-call(s32[2]{0:T(128)} %pad_add_fusion.3.me_ref, ...), custom_call_target="tpu_custom_call" | custom-call | flops 40249999360 | bytes 126000000 | tf_op jit(solution)/shard_map/ffn/pallas_call | solution.py:344
  172.2 9.3 %back_grad.1 = (bf16[4,864,768]{2,1,0:T(8,128)(2,1)}, bf16[4,864,768]{2,1,0:T(8,128)(2,1)}) custom-call(s32[2]{0:T(128)} %pad_add_fusion.3.me_ref, bf16[1024,3072]{1,0:T(8,128)(2,1)} %get-tuple-element.128.keep_left.send_left, bf16[1024,3072]{1,0:T(8,128)(2,1)} %get-tuple-element.128.keep_left.send_left, bf16[1024,768]{1,0:T(8,128)(2,1)} %get-tuple-element.129.right_ref), custom_call_target="tpu_custom_call" | custom-call | flops 10350000128 | bytes 32400000 | tf_op jit(solution)/shard_map/back_grad/pallas_call | solution.py:460
  181.5 10.2 %columns_grad.2 = (bf16[4,864,768]{2,1,0:T(8,128)(2,1)}, bf16[4,864,768]{2,1,0:T(8,128)(2,1)}) custom-call(s32[2]{0:T(128)} %pad_add_fusion.3.me_ref, bf16[1024,768]{1,0:T(8,128)(2,1)} %get-tuple-element.126.left_ref, bf16[1024,3072]{1,0:T(8,128)(2,1)} %get-tuple-element.127.right_ref, ...), custom_call_target="tpu_custom_call", output_to_operand_aliasing={{0}: (3, {}), {1}: (4, {})} | custom-call | flops 12650000384 | bytes 39600000 | tf_op jit(solution)/shard_map/columns_grad/pallas_call | solution.py:439
  191.8 4.6 columns_grad.3
  197.5 10.0 %attend_back.3 = (bf16[1024,768]{1,0:T(8,128)(2,1)}, bf16[1024,768]{1,0:T(8,128)(2,1)}, bf16[1024,768]{1,0:T(8,128)(2,1)}, f32[6,2,1024]{2,1,0:T(2,128)}) custom-call(s32[2]{0:T(128)} %lengths_ref.7, f32[6,2,1024]{2,1,0:T(2,128)} %copy.88.diagonal_ref, bf16[1024,2304]{1,0:T(8,128)(2,1)} %get-tuple-element.111.query_ref.key_ref.value_ref, ...), custom_call_target="tpu_custom_call" | custom-call | flops 10119999488 | bytes 31680000 | tf_op jit(solution)/shard_map/attend_back/pallas_call | solution.py:170
  212.5 13.9 %attend_back.4 = (bf16[1024,768]{1,0:T(8,128)(2,1)}, bf16[1024,768]{1,0:T(8,128)(2,1)}, bf16[1024,768]{1,0:T(8,128)(2,1)}, f32[6,2,1024]{2,1,0:T(2,128)}) custom-call(s32[2]{0:T(128)} %lengths_ref.7, f32[6,2,1024]{2,1,0:T(2,128)} %copy.88.diagonal_ref, ...), custom_call_target="tpu_custom_call", output_to_operand_aliasing={{0}: (7, {}), {1}: (8, {}), {2}: (9, {}), {3}: (10, {})} | custom-call | flops 15180000256 | bytes 47520000 | tf_op jit(solution)/shard_map/attend_back/pallas_call | solution.py:170
  227.9 4.0 fusion.3
  234.0 5.8 %attend_back.5 = (bf16[1024,768]{1,0:T(8,128)(2,1)}, bf16[1024,768]{1,0:T(8,128)(2,1)}, bf16[1024,768]{1,0:T(8,128)(2,1)}, f32[6,2,1024]{2,1,0:T(2,128)}) custom-call(s32[2]{0:T(128)} %lengths_ref.7, f32[6,2,1024]{2,1,0:T(2,128)} %copy.88.diagonal_ref, ...), custom_call_target="tpu_custom_call", output_to_operand_aliasing={{0}: (7, {}), {1}: (8, {}), {2}: (9, {}), {3}: (10, {})} | custom-call | flops 5059999744 | bytes 15840000 | tf_op jit(solution)/shard_map/attend_back/pallas_call | solution.py:170
  240.6 10.6 %project_back.1 = (bf16[1024,768]{1,0:T(8,128)(2,1)}, f32[1,768]{1,0:T(1,128)}) custom-call(s32[2]{0:T(128)} %pad_add_fusion.3.me_ref, bf16[1024,768]{1,0:T(8,128)(2,1)} %get-tuple-element.153.query_ref, bf16[1024,768]{1,0:T(8,128)(2,1)} %get-tuple-element.154.key_ref, bf16[1024,768]{1,0:T(8,128)(2,1)} %get-tuple-element.155.value_ref, ...), custom_call_target="tpu_custom_call" | custom-call | flops 12650000384 | bytes 39600000 | tf_op jit(solution)/shard_map/project_back/pallas_call | solution.py:395
  253.1 10.6 %rest_grads.1 = (bf16[4,304,768]{2,1,0:T(8,128)(2,1)}, bf16[4,304,768]{2,1,0:T(8,128)(2,1)}) custom-call(s32[2]{0:T(128)} %pad_add_fusion.3.me_ref, bf16[1024,768]{1,0:T(8,128)(2,1)} %get-tuple-element.151.normed_ref, bf16[1024,768]{1,0:T(8,128)(2,1)} %get-tuple-element.153.query_ref, bf16[1024,768]{1,0:T(8,128)(2,1)} %get-tuple-element.154.key_ref, ...), custom_call_target="tpu_custom_call" | custom-call | flops 12650000384 | bytes 39600000 | tf_op jit(solution)/shard_map/rest_grads/pallas_call | solution.py:497
  263.7 7.2 %place.4 = bf16[2048,768]{1,0:T(8,128)(2,1)} custom-call(s32[1,1024]{1,0:T(1,128)} %fusion.31.slot_ref, s32[1]{0:T(128)} %constant.98.clone.1.choice_ref, bf16[1024,768]{1,0:T(8,128)(2,1)} %get-tuple-element.162.rest_0_), custom_call_target="tpu_custom_call" | custom-call | flops 6899999744 | bytes 21600000 | tf_op jit(solution)/shard_map/place/pallas_call | solution.py:528
  270.9 4.5 all-to-all-start.3
  276.7 5.9 %collective-permute-start.34 = (bf16[1024,768]{1,0:T(8,128)(2,1)}, bf16[1024,768]{1,0:T(8,128)(2,1)}, u32[]{:S(2)}, u32[]{:S(2)}) collective-permute-start(bf16[1024,768]{1,0:T(8,128)(2,1)} %get-tuple-element.162.rest_0_), channel_id=1, source_target_pairs={{0,8},{8,16},{16,24},{1,9},{9,17},{17,25},{2,10},{10,18},{18,26},{... | collective-permute-start | bytes 4718600 | tf_op jit(solution)/shard_map/ppermute | solution.py:805
  287.7 3.3 fusion.2
  292.2 2.0 collective-permute-start.37
  295.7 18.9 %collective-permute-done.35.rest_1_.rest_2_ = bf16[1024,768]{1,0:T(8,128)(2,1)} collective-permute-done((bf16[1024,768]{1,0:T(8,128)(2,1)}, bf16[1024,768]{1,0:T(8,128)(2,1)}, u32[]{:S(2)}, u32[]{:S(2)}) %collective-permute-start.35) | collective-permute-done | bytes 1572896 | tf_op jit(solution)/shard_map/ppermute | solution.py:805
  315.8 7.0 %place.5 = bf16[2048,768]{1,0:T(8,128)(2,1)} custom-call(s32[1,1024]{1,0:T(1,128)} %bitcast.149, s32[1]{0:T(128)} %bitcast.24.choice_ref, bf16[1024,768]{1,0:T(8,128)(2,1)} %collective-permute-done.34.rest_0_.rest_1_, bf16[1024,768]{1,0:T(8,128)(2,1)} %collective-permute-done.35.rest_1_.rest_2_), custom_call_target="tpu_custom_call" | custom-call | flops 6899999744 | bytes 21600000 | tf_op jit(solution)/shard_map/place/pallas_call | solution.py:528
  322.9 4.5 all-to-all-start.4
  327.4 3.8 select_add_fusion
  332.4 5.1 %collective-permute-start.39 = (bf16[1024,768]{1,0:T(8,128)(2,1)S(1)}, bf16[1024,768]{1,0:T(8,128)(2,1)S(1)}, u32[]{:S(2)}, u32[]{:S(2)}) collective-permute-start(bf16[1024,768]{1,0:T(8,128)(2,1)S(1)} %get-tuple-element.210), channel_id=1, source_target_pairs={{0,8},{8,16},{16,24},{1,9},{9,17},{17,25},{2,10},{10,18},{18,26},{... | collective-permute-start | bytes 4718600 | tf_op jit(solution)/shard_map/ppermute | solution.py:805
  337.6 17.5 %table_rows.4.rest_0_ = f32[4016,768]{1,0:T(8,128)} custom-call(s32[1,2048]{1,0:T(1,128)} %bitcast.143, bf16[2048,768]{1,0:T(8,128)(2,1)} %bitcast.22.rows_ref), custom_call_target="tpu_custom_call" | custom-call | flops 20700000256 | bytes 64800000 | tf_op jit(solution)/shard_map/table_rows/pallas_call | solution.py:557
  355.0 2.4 fusion.13
  360.8 9.8 %collective-permute-done.40.rest_1_ = bf16[1024,768]{1,0:T(8,128)(2,1)S(1)} collective-permute-done((bf16[1024,768]{1,0:T(8,128)(2,1)}, bf16[1024,768]{1,0:T(8,128)(2,1)S(1)}, u32[]{:S(2)}, u32[]{:S(2)}) %collective-permute-start.40) | collective-permute-done | bytes 1572896 | tf_op jit(solution)/shard_map/ppermute | solution.py:805
  372.8 7.0 %place.6 = bf16[2048,768]{1,0:T(8,128)(2,1)} custom-call(s32[1,1024]{1,0:T(1,128)} %bitcast.148, s32[1]{0:T(128)} %bitcast.30.choice_ref, bf16[1024,768]{1,0:T(8,128)(2,1)} %copy-done.8, bf16[1024,768]{1,0:T(8,128)(2,1)} %copy-done.5), custom_call_target="tpu_custom_call" | custom-call | flops 6899999744 | bytes 21600000 | tf_op jit(solution)/shard_map/place/pallas_call | solution.py:528
  380.6 4.6 all-to-all-start.5
  385.2 3.8 fusion.8
  391.0 18.5 %table_rows.5.rest_0_ = f32[4016,768]{1,0:T(8,128)} custom-call(s32[1,2048]{1,0:T(1,128)} %bitcast.146, bf16[2048,768]{1,0:T(8,128)(2,1)} %bitcast.28.rows_ref, f32[4016,768]{1,0:T(8,128)} %table_rows.4.rest_0_), custom_call_target="tpu_custom_call", output_to_operand_aliasing={{}: (2, {})} | custom-call | flops 20700000256 | bytes 64800000 | tf_op jit(solution)/shard_map/table_rows/pallas_call | solution.py:557
  411.0 6.5 %collective-permute-start.45 = (bf16[304,768]{1,0:T(8,128)(2,1)S(1)}, bf16[304,768]{1,0:T(8,128)(2,1)}, u32[]{:S(2)}, u32[]{:S(2)}) collective-permute-start(bf16[304,768]{1,0:T(8,128)(2,1)S(1)} %fusion.12), channel_id=1, source_target_pairs={{0,8},{8,0},{16,24},{24,16},{1,9},{9,1},{17,25},{25,17},{2,10},{10... | collective-permute-start | bytes 1400840 | tf_op jit(solution)/shard_map/ppermute | solution.py:577
  417.6 11.2 %collective-permute-done.44.rest_3_ = bf16[1024,768]{1,0:T(8,128)(2,1)S(1)} collective-permute-done((bf16[1024,768]{1,0:T(8,128)(2,1)}, bf16[1024,768]{1,0:T(8,128)(2,1)S(1)}, u32[]{:S(2)}, u32[]{:S(2)}) %collective-permute-start.44) | collective-permute-done | bytes 1572896 | tf_op jit(solution)/shard_map/ppermute | solution.py:805
  430.5 7.1 %place.7 = bf16[2048,768]{1,0:T(8,128)(2,1)} custom-call(s32[1,1024]{1,0:T(1,128)} %bitcast.147, s32[1]{0:T(128)} %bitcast.37.choice_ref, bf16[1024,768]{1,0:T(8,128)(2,1)} %copy-done.2, bf16[1024,768]{1,0:T(8,128)(2,1)} %collective-permute-done.34.rest_0_.rest_1_, bf16[1024,768]{1,0:T(8,128)(2,1)} %collective-permute-done.35.rest_1_.rest_2_, ...), custom_call_target="tpu_custom_call" | custom-call | flops 6899999744 | bytes 21600000 | tf_op jit(solution)/shard_map/place/pallas_call | solution.py:528
  438.6 4.6 all-to-all-start.6
  443.2 4.4 fusion.7
  451.0 18.5 %table_rows.6.rest_0_ = f32[4016,768]{1,0:T(8,128)} custom-call(s32[1,2048]{1,0:T(1,128)} %bitcast.145, bf16[2048,768]{1,0:T(8,128)(2,1)} %bitcast.35.rows_ref, f32[4016,768]{1,0:T(8,128)} %table_rows.5.rest_0_), custom_call_target="tpu_custom_call", output_to_operand_aliasing={{}: (2, {})} | custom-call | flops 20700000256 | bytes 64800000 | tf_op jit(solution)/shard_map/table_rows/pallas_call | solution.py:557
  470.7 7.3 %collective-permute-start.46 = (bf16[304,768]{1,0:T(8,128)(2,1)S(1)}, bf16[304,768]{1,0:T(8,128)(2,1)}, u32[]{:S(2)}, u32[]{:S(2)}) collective-permute-start(bf16[304,768]{1,0:T(8,128)(2,1)S(1)} %add.355), channel_id=1, source_target_pairs={{0,16},{8,24},{16,0},{24,8},{1,17},{9,25},{17,1},{25,9},{2,18},{10... | collective-permute-start | bytes 1400840 | tf_op jit(solution)/shard_map/ppermute | solution.py:577
  478.0 3.1 all-to-all-done.6
  481.1 18.6 %table_rows.7 = f32[4016,768]{1,0:T(8,128)} custom-call(s32[1,2048]{1,0:T(1,128)} %bitcast.144, bf16[2048,768]{1,0:T(8,128)(2,1)} %bitcast.41.rows_ref, f32[4016,768]{1,0:T(8,128)} %table_rows.6.rest_0_), custom_call_target="tpu_custom_call", output_to_operand_aliasing={{}: (2, {})} | custom-call | flops 20700000256 | bytes 64800000 | tf_op jit(solution)/shard_map/table_rows/pallas_call | solution.py:557
  502.6 3.3 convert_add_fusion
  (279 shorter events, 97.0 us)
Async XLA Ops:
  3.5 16.4 %collective-permute-start.1 = (bf16[112,2304]{1,0:T(8,128)(2,1)S(1)}, bf16[112,2304]{1,0:T(8,128)(2,1)}, u32[]{:S(2)}, u32[]{:S(2)}) collective-permute-start(bf16[112,2304]{1,0:T(8,128)(2,1)S(1)} %pad_maximum_fusion.1.rest_0_), channel_id=1, source_target_pairs={{0,4},{1,5},{2,6},{3,7},{4,0},{5,1},{6,2},{7,3},{8,12},{9,13},{10,... | collective-permute-start | bytes 1548296 | tf_op jit(solution)/shard_map/ppermute | solution.py:572
  6.5 16.5 %collective-permute-start = (bf16[112,2304]{1,0:T(8,128)(2,1)S(1)}, bf16[112,2304]{1,0:T(8,128)(2,1)}, u32[]{:S(2)}, u32[]{:S(2)}) collective-permute-start(bf16[112,2304]{1,0:T(8,128)(2,1)S(1)} %pad_maximum_fusion.1.rest_0_), channel_id=1, source_target_pairs={{0,2},{1,3},{2,0},{3,1},{4,6},{5,7},{6,4},{7,5},{8,10},{9,11},{10,... | collective-permute-start | bytes 1548296 | tf_op jit(solution)/shard_map/ppermute | solution.py:572
  15.4 25.5 %collective-permute-start.3 = (bf16[432,768]{1,0:T(8,128)(2,1)}, bf16[432,768]{1,0:T(8,128)(2,1)}, u32[]{:S(2)}, u32[]{:S(2)}) collective-permute-start(bf16[432,768]{1,0:T(8,128)(2,1)} %constant_dynamic-slice_fusion), channel_id=1, source_target_pairs={{0,4},{1,5},{2,6},{3,7},{4,0},{5,1},{6,2},{7,3},{8,12},{9,13},{10,... | collective-permute-start | bytes 1990664 | tf_op jit(solution)/shard_map/ppermute | solution.py:572
  17.3 23.5 %collective-permute-start.2 = (bf16[432,768]{1,0:T(8,128)(2,1)}, bf16[432,768]{1,0:T(8,128)(2,1)}, u32[]{:S(2)}, u32[]{:S(2)}) collective-permute-start(bf16[432,768]{1,0:T(8,128)(2,1)} %constant_dynamic-slice_fusion), channel_id=1, source_target_pairs={{0,2},{1,3},{2,0},{3,1},{4,6},{5,7},{6,4},{7,5},{8,10},{9,11},{10,... | collective-permute-start | bytes 1990664 | tf_op jit(solution)/shard_map/ppermute | solution.py:572
  21.5 19.3 %collective-permute-start.4 = (bf16[48,2304]{1,0:T(8,128)(2,1)}, bf16[48,2304]{1,0:T(8,128)(2,1)}, u32[]{:S(2)}, u32[]{:S(2)}) collective-permute-start(bf16[48,2304]{1,0:T(8,128)(2,1)} %slice.302), channel_id=1, source_target_pairs={{0,2},{1,3},{2,0},{3,1},{4,6},{5,7},{6,4},{7,5},{8,10},{9,11},{10,... | collective-permute-start | bytes 663560 | tf_op jit(solution)/shard_map/ppermute | solution.py:572
  25.4 15.4 %collective-permute-start.5 = (bf16[64,2304]{1,0:T(8,128)(2,1)}, bf16[64,2304]{1,0:T(8,128)(2,1)}, u32[]{:S(2)}, u32[]{:S(2)}) collective-permute-start(bf16[64,2304]{1,0:T(8,128)(2,1)} %slice.303), channel_id=1, source_target_pairs={{0,4},{1,5},{2,6},{3,7},{4,0},{5,1},{6,2},{7,3},{8,12},{9,13},{10,... | collective-permute-start | bytes 884744 | tf_op jit(solution)/shard_map/ppermute | solution.py:572
  40.8 49.6 %all-to-all-start.1 = ((bf16[8,256,768]{2,1,0:T(8,128)(2,1)}), bf16[8,256,768]{2,1,0:T(8,128)(2,1)S(1)}, u32[]{:S(2)}, u32[]{:S(2)}) async-start(bf16[8,256,768]{2,1,0:T(8,128)(2,1)} %bitcast.4), calls=%async_computation.1 | async-start | bytes 6291456 | tf_op jit(solution)/shard_map/all_to_all | solution.py:585
  47.5 11.9 %collective-permute-start.11 = (bf16[112,2304]{1,0:T(8,128)(2,1)}, bf16[112,2304]{1,0:T(8,128)(2,1)}, u32[]{:S(2)}, u32[]{:S(2)}) collective-permute-start(bf16[112,2304]{1,0:T(8,128)(2,1)} %collective-permute-done.rest_1_), channel_id=1, source_target_pairs={{0,1},{1,0},{2,3},{3,2},{4,5},{5,4},{6,7},{7,6},{8,9},{9,8},{10,11... | collective-permute-start | bytes 1548296 | tf_op jit(solution)/shard_map/ppermute | solution.py:572
  50.0 40.5 %collective-permute-start.8 = (bf16[432,768]{1,0:T(8,128)(2,1)}, bf16[432,768]{1,0:T(8,128)(2,1)}, u32[]{:S(2)}, u32[]{:S(2)}) collective-permute-start(bf16[432,768]{1,0:T(8,128)(2,1)} %collective-permute-done.2.rest_2_), channel_id=1, source_target_pairs={{0,8},{8,0},{16,24},{24,16},{1,9},{9,1},{17,25},{25,17},{2,10},{10... | collective-permute-start | bytes 1990664 | tf_op jit(solution)/shard_map/ppermute | solution.py:577
  51.6 38.8 %collective-permute-start.9 = (bf16[432,768]{1,0:T(8,128)(2,1)}, bf16[432,768]{1,0:T(8,128)(2,1)}, u32[]{:S(2)}, u32[]{:S(2)}) collective-permute-start(bf16[432,768]{1,0:T(8,128)(2,1)} %collective-permute-done.3.rest_3_), channel_id=1, source_target_pairs={{0,8},{8,0},{16,24},{24,16},{1,9},{9,1},{17,25},{25,17},{2,10},{10... | collective-permute-start | bytes 1990664 | tf_op jit(solution)/shard_map/ppermute | solution.py:577
  53.9 36.1 %collective-permute-start.7 = (bf16[224,768]{1,0:T(8,128)(2,1)S(1)}, bf16[224,768]{1,0:T(8,128)(2,1)}, u32[]{:S(2)}, u32[]{:S(2)}) collective-permute-start(bf16[224,768]{1,0:T(8,128)(2,1)S(1)} %slice.235), channel_id=1, source_target_pairs={{0,4},{1,5},{2,6},{3,7},{4,0},{5,1},{6,2},{7,3},{8,12},{9,13},{10,... | collective-permute-start | bytes 1032200 | tf_op jit(solution)/shard_map/ppermute | solution.py:572
  59.5 28.9 %collective-permute-start.6 = (bf16[208,768]{1,0:T(8,128)(2,1)}, bf16[208,768]{1,0:T(8,128)(2,1)}, u32[]{:S(2)}, u32[]{:S(2)}) collective-permute-start(bf16[208,768]{1,0:T(8,128)(2,1)} %slice.234), channel_id=1, source_target_pairs={{0,2},{1,3},{2,0},{3,1},{4,6},{5,7},{6,4},{7,5},{8,10},{9,11},{10,... | collective-permute-start | bytes 958472 | tf_op jit(solution)/shard_map/ppermute | solution.py:572
  63.0 31.1 %collective-permute-start.14 = (bf16[48,2304]{1,0:T(8,128)(2,1)}, bf16[48,2304]{1,0:T(8,128)(2,1)}, u32[]{:S(2)}, u32[]{:S(2)}) collective-permute-start(bf16[48,2304]{1,0:T(8,128)(2,1)} %collective-permute-done.4.rest_3_), channel_id=1, source_target_pairs={{0,1},{1,0},{2,3},{3,2},{4,5},{5,4},{6,7},{7,6},{8,9},{9,8},{10,11... | collective-permute-start | bytes 663560 | tf_op jit(solution)/shard_map/ppermute | solution.py:572
  88.4 21.8 %collective-permute-start.18 = (bf16[208,768]{1,0:T(8,128)(2,1)}, bf16[208,768]{1,0:T(8,128)(2,1)}, u32[]{:S(2)}, u32[]{:S(2)}) collective-permute-start(bf16[208,768]{1,0:T(8,128)(2,1)} %collective-permute-done.6.rest_4_), channel_id=1, source_target_pairs={{0,8},{8,0},{16,24},{24,16},{1,9},{9,1},{17,25},{25,17},{2,10},{10... | collective-permute-start | bytes 958472 | tf_op jit(solution)/shard_map/ppermute | solution.py:577
  90.0 20.2 %collective-permute-start.19 = (bf16[224,768]{1,0:T(8,128)(2,1)}, bf16[224,768]{1,0:T(8,128)(2,1)}, u32[]{:S(2)}, u32[]{:S(2)}) collective-permute-start(bf16[224,768]{1,0:T(8,128)(2,1)} %collective-permute-done.7.rest_5_), channel_id=1, source_target_pairs={{0,8},{8,0},{16,24},{24,16},{1,9},{9,1},{17,25},{25,17},{2,10},{10... | collective-permute-start | bytes 1032200 | tf_op jit(solution)/shard_map/ppermute | solution.py:577
  90.5 19.5 %collective-permute-start.17 = (s32[3088]{0:T(1024)S(1)}, s32[3088]{0:T(1024)S(1)}, u32[]{:S(2)}, u32[]{:S(2)}) collective-permute-start(s32[3088]{0:T(1024)S(1)} %pad_add_fusion.1), channel_id=1, source_target_pairs={{0,24},{8,16},{16,8},{24,0},{1,25},{9,17},{17,9},{25,1},{2,26},{10... | collective-permute-start | bytes 37064 | tf_op jit(solution)/shard_map/ppermute | solution.py:577
  94.1 16.0 %collective-permute-start.16 = (s32[3088]{0:T(1024)S(1)}, s32[3088]{0:T(1024)S(1)}, u32[]{:S(2)}, u32[]{:S(2)}) collective-permute-start(s32[3088]{0:T(1024)S(1)} %pad_add_fusion.1), channel_id=1, source_target_pairs={{0,16},{8,24},{16,0},{24,8},{1,17},{9,25},{17,1},{25,9},{2,18},{10... | collective-permute-start | bytes 37064 | tf_op jit(solution)/shard_map/ppermute | solution.py:577
  94.1 16.0 %collective-permute-start.15 = (s32[3088]{0:T(1024)S(1)}, s32[3088]{0:T(1024)S(1)}, u32[]{:S(2)}, u32[]{:S(2)}) collective-permute-start(s32[3088]{0:T(1024)S(1)} %pad_add_fusion.1), channel_id=1, source_target_pairs={{0,8},{8,0},{16,24},{24,16},{1,9},{9,1},{17,25},{25,17},{2,10},{10... | collective-permute-start | bytes 37064 | tf_op jit(solution)/shard_map/ppermute | solution.py:577
  113.1 22.7 %collective-permute-start.21 = (bf16[432,768]{1,0:T(8,128)(2,1)}, bf16[432,768]{1,0:T(8,128)(2,1)S(1)}, u32[]{:S(2)}, u32[]{:S(2)}) collective-permute-start(bf16[432,768]{1,0:T(8,128)(2,1)} %collective-permute-done.2.rest_2_), channel_id=1, source_target_pairs={{0,1},{1,0},{2,3},{3,2},{4,5},{5,4},{6,7},{7,6},{8,9},{9,8},{10,11... | collective-permute-start | bytes 1990664 | tf_op jit(solution)/shard_map/ppermute | solution.py:572
  113.8 22.0 %all-to-all-start.2 = ((s32[8,3,256]{2,1,0:T(4,128)}), s32[8,3,256]{2,1,0:T(4,128)S(1)}, u32[]{:S(2)}, u32[]{:S(2)}) async-start(s32[8,3,256]{2,1,0:T(4,128)} %pad_add_fusion), calls=%async_computation.2 | async-start | bytes 65536 | tf_op jit(solution)/shard_map/all_to_all | solution.py:585
  117.4 18.4 %collective-permute-start.22 = (bf16[432,768]{1,0:T(8,128)(2,1)}, bf16[432,768]{1,0:T(8,128)(2,1)S(1)}, u32[]{:S(2)}, u32[]{:S(2)}) collective-permute-start(bf16[432,768]{1,0:T(8,128)(2,1)} %collective-permute-done.3.rest_3_), channel_id=1, source_target_pairs={{0,1},{1,0},{2,3},{3,2},{4,5},{5,4},{6,7},{7,6},{8,9},{9,8},{10,11... | collective-permute-start | bytes 1990664 | tf_op jit(solution)/shard_map/ppermute | solution.py:572
  117.9 17.9 %collective-permute-start.20 = (bf16[864,768]{1,0:T(8,128)(2,1)}, bf16[864,768]{1,0:T(8,128)(2,1)S(1)}, u32[]{:S(2)}, u32[]{:S(2)}) collective-permute-start(bf16[864,768]{1,0:T(8,128)(2,1)} %copy-done.19), channel_id=1, source_target_pairs={{0,1},{1,0},{2,3},{3,2},{4,5},{5,4},{6,7},{7,6},{8,9},{9,8},{10,11... | collective-permute-start | bytes 3981320 | tf_op jit(solution)/shard_map/ppermute | solution.py:572
  118.0 17.8 %collective-permute-start.25 = (bf16[432,768]{1,0:T(8,128)(2,1)}, bf16[432,768]{1,0:T(8,128)(2,1)}, u32[]{:S(2)}, u32[]{:S(2)}) collective-permute-start(bf16[432,768]{1,0:T(8,128)(2,1)} %collective-permute-done.8.rest_10_), channel_id=1, source_target_pairs={{0,1},{1,0},{2,3},{3,2},{4,5},{5,4},{6,7},{7,6},{8,9},{9,8},{10,11... | collective-permute-start | bytes 1990664 | tf_op jit(solution)/shard_map/ppermute | solution.py:572
  118.4 17.4 %collective-permute-start.26 = (bf16[432,768]{1,0:T(8,128)(2,1)}, bf16[432,768]{1,0:T(8,128)(2,1)}, u32[]{:S(2)}, u32[]{:S(2)}) collective-permute-start(bf16[432,768]{1,0:T(8,128)(2,1)} %collective-permute-done.9.rest_11_), channel_id=1, source_target_pairs={{0,1},{1,0},{2,3},{3,2},{4,5},{5,4},{6,7},{7,6},{8,9},{9,8},{10,11... | collective-permute-start | bytes 1990664 | tf_op jit(solution)/shard_map/ppermute | solution.py:572
  196.4 11.1 %collective-permute-start.29 = (bf16[4,864,768]{2,1,0:T(8,128)(2,1)}, bf16[4,864,768]{2,1,0:T(8,128)(2,1)}, u32[]{:S(2)}, u32[]{:S(2)}) collective-permute-start(bf16[4,864,768]{2,1,0:T(8,128)(2,1)} %get-tuple-element.135), channel_id=1, source_target_pairs={{0,1},{1,0},{2,3},{3,2},{4,5},{5,4},{6,7},{7,6},{8,9},{9,8},{10,11... | collective-permute-start | bytes 15925256 | tf_op jit(solution)/shard_map/ppermute | solution.py:572
  209.2 17.2 %collective-permute-start.32 = (bf16[432,768]{1,0:T(8,128)(2,1)S(1)}, bf16[432,768]{1,0:T(8,128)(2,1)S(1)}, u32[]{:S(2)}, u32[]{:S(2)}) collective-permute-start(bf16[432,768]{1,0:T(8,128)(2,1)S(1)} %get-tuple-element.211), channel_id=1, source_target_pairs={{0,2},{1,3},{2,0},{3,1},{4,6},{5,7},{6,4},{7,5},{8,10},{9,11},{10,... | collective-permute-start | bytes 1990664 | tf_op jit(solution)/shard_map/ppermute | solution.py:572
  211.0 16.9 %collective-permute-start.30 = (bf16[432,768]{1,0:T(8,128)(2,1)S(1)}, bf16[432,768]{1,0:T(8,128)(2,1)S(1)}, u32[]{:S(2)}, u32[]{:S(2)}) collective-permute-start(bf16[432,768]{1,0:T(8,128)(2,1)S(1)} %get-tuple-element.212), channel_id=1, source_target_pairs={{0,4},{1,5},{2,6},{3,7},{4,0},{5,1},{6,2},{7,3},{8,12},{9,13},{10,... | collective-permute-start | bytes 1990664 | tf_op jit(solution)/shard_map/ppermute | solution.py:572
  231.9 31.7 %collective-permute-start.33 = (bf16[864,768]{1,0:T(8,128)(2,1)}, bf16[864,768]{1,0:T(8,128)(2,1)S(1)}, u32[]{:S(2)}, u32[]{:S(2)}) collective-permute-start(bf16[864,768]{1,0:T(8,128)(2,1)} %get-tuple-element.195), channel_id=1, source_target_pairs={{0,4},{1,5},{2,6},{3,7},{4,0},{5,1},{6,2},{7,3},{8,12},{9,13},{10,... | collective-permute-start | bytes 3981320 | tf_op jit(solution)/shard_map/ppermute | solution.py:572
  233.4 30.3 %collective-permute-start.31 = (bf16[864,768]{1,0:T(8,128)(2,1)}, bf16[864,768]{1,0:T(8,128)(2,1)S(1)}, u32[]{:S(2)}, u32[]{:S(2)}) collective-permute-start(bf16[864,768]{1,0:T(8,128)(2,1)} %get-tuple-element.196), channel_id=1, source_target_pairs={{0,2},{1,3},{2,0},{3,1},{4,6},{5,7},{6,4},{7,5},{8,10},{9,11},{10,... | collective-permute-start | bytes 3981320 | tf_op jit(solution)/shard_map/ppermute | solution.py:572
  263.7 27.3 %collective-permute-start.36 = (bf16[4,304,768]{2,1,0:T(8,128)(2,1)}, bf16[4,304,768]{2,1,0:T(8,128)(2,1)}, u32[]{:S(2)}, u32[]{:S(2)}) collective-permute-start(bf16[4,304,768]{2,1,0:T(8,128)(2,1)} %get-tuple-element.160), channel_id=1, source_target_pairs={{0,1},{1,0},{2,3},{3,2},{4,5},{5,4},{6,7},{7,6},{8,9},{9,8},{10,11... | collective-permute-start | bytes 5603336 | tf_op jit(solution)/shard_map/ppermute | solution.py:572
  270.9 51.9 %all-to-all-start.3 = ((bf16[8,256,768]{2,1,0:T(8,128)(2,1)}), bf16[8,256,768]{2,1,0:T(8,128)(2,1)}, u32[]{:S(2)}, u32[]{:S(2)}) async-start(bf16[8,256,768]{2,1,0:T(8,128)(2,1)} %bitcast.118), calls=%async_computation.3 | async-start | bytes 6291456 | tf_op jit(solution)/shard_map/all_to_all | solution.py:585
  275.4 39.2 %collective-permute-start.35 = (bf16[1024,768]{1,0:T(8,128)(2,1)}, bf16[1024,768]{1,0:T(8,128)(2,1)}, u32[]{:S(2)}, u32[]{:S(2)}) collective-permute-start(bf16[1024,768]{1,0:T(8,128)(2,1)} %get-tuple-element.162.rest_0_), channel_id=1, source_target_pairs={{24,16},{16,8},{8,0},{25,17},{17,9},{9,1},{26,18},{18,10},{10,2},{... | collective-permute-start | bytes 4718600 | tf_op jit(solution)/shard_map/ppermute | solution.py:805
  276.7 39.1 %collective-permute-start.34 = (bf16[1024,768]{1,0:T(8,128)(2,1)}, bf16[1024,768]{1,0:T(8,128)(2,1)}, u32[]{:S(2)}, u32[]{:S(2)}) collective-permute-start(bf16[1024,768]{1,0:T(8,128)(2,1)} %get-tuple-element.162.rest_0_), channel_id=1, source_target_pairs={{0,8},{8,16},{16,24},{1,9},{9,17},{17,25},{2,10},{10,18},{18,26},{... | collective-permute-start | bytes 4718600 | tf_op jit(solution)/shard_map/ppermute | solution.py:805
  292.2 30.7 %collective-permute-start.37 = (bf16[144,768]{1,0:T(8,128)(2,1)S(1)}, bf16[144,768]{1,0:T(8,128)(2,1)}, u32[]{:S(2)}, u32[]{:S(2)}) collective-permute-start(bf16[144,768]{1,0:T(8,128)(2,1)S(1)} %slice_bitcast_fusion.3), channel_id=1, source_target_pairs={{0,2},{1,3},{2,0},{3,1},{4,6},{5,7},{6,4},{7,5},{8,10},{9,11},{10,... | collective-permute-start | bytes 663560 | tf_op jit(solution)/shard_map/ppermute | solution.py:572
  294.2 28.7 %collective-permute-start.38 = (bf16[160,768]{1,0:T(8,128)(2,1)S(1)}, bf16[160,768]{1,0:T(8,128)(2,1)S(1)}, u32[]{:S(2)}, u32[]{:S(2)}) collective-permute-start(bf16[160,768]{1,0:T(8,128)(2,1)S(1)} %slice_bitcast_fusion.2), channel_id=1, source_target_pairs={{0,4},{1,5},{2,6},{3,7},{4,0},{5,1},{6,2},{7,3},{8,12},{9,13},{10,... | collective-permute-start | bytes 737288 | tf_op jit(solution)/shard_map/ppermute | solution.py:572
  322.9 56.9 %all-to-all-start.4 = ((bf16[8,256,768]{2,1,0:T(8,128)(2,1)}), bf16[8,256,768]{2,1,0:T(8,128)(2,1)}, u32[]{:S(2)}, u32[]{:S(2)}) async-start(bf16[8,256,768]{2,1,0:T(8,128)(2,1)} %bitcast.119), calls=%async_computation.4 | async-start | bytes 6291456 | tf_op jit(solution)/shard_map/all_to_all | solution.py:585
  331.1 39.5 %collective-permute-start.40 = (bf16[1024,768]{1,0:T(8,128)(2,1)}, bf16[1024,768]{1,0:T(8,128)(2,1)S(1)}, u32[]{:S(2)}, u32[]{:S(2)}) collective-permute-start(bf16[1024,768]{1,0:T(8,128)(2,1)} %get-tuple-element.209), channel_id=1, source_target_pairs={{24,16},{16,8},{8,0},{25,17},{17,9},{9,1},{26,18},{18,10},{10,2},{... | collective-permute-start | bytes 4718600 | tf_op jit(solution)/shard_map/ppermute | solution.py:805
  332.4 39.2 %collective-permute-start.39 = (bf16[1024,768]{1,0:T(8,128)(2,1)S(1)}, bf16[1024,768]{1,0:T(8,128)(2,1)S(1)}, u32[]{:S(2)}, u32[]{:S(2)}) collective-permute-start(bf16[1024,768]{1,0:T(8,128)(2,1)S(1)} %get-tuple-element.210), channel_id=1, source_target_pairs={{0,8},{8,16},{16,24},{1,9},{9,17},{17,25},{2,10},{10,18},{18,26},{... | collective-permute-start | bytes 4718600 | tf_op jit(solution)/shard_map/ppermute | solution.py:805
  357.4 22.4 %collective-permute-start.42 = (bf16[304,768]{1,0:T(8,128)(2,1)}, bf16[304,768]{1,0:T(8,128)(2,1)S(1)}, u32[]{:S(2)}, u32[]{:S(2)}) collective-permute-start(bf16[304,768]{1,0:T(8,128)(2,1)} %get-tuple-element.197), channel_id=1, source_target_pairs={{0,4},{1,5},{2,6},{3,7},{4,0},{5,1},{6,2},{7,3},{8,12},{9,13},{10,... | collective-permute-start | bytes 1400840 | tf_op jit(solution)/shard_map/ppermute | solution.py:572
  359.3 20.5 %collective-permute-start.41 = (bf16[304,768]{1,0:T(8,128)(2,1)}, bf16[304,768]{1,0:T(8,128)(2,1)S(1)}, u32[]{:S(2)}, u32[]{:S(2)}) collective-permute-start(bf16[304,768]{1,0:T(8,128)(2,1)} %get-tuple-element.198), channel_id=1, source_target_pairs={{0,2},{1,3},{2,0},{3,1},{4,6},{5,7},{6,4},{7,5},{8,10},{9,11},{10,... | collective-permute-start | bytes 1400840 | tf_op jit(solution)/shard_map/ppermute | solution.py:572
  380.6 58.0 %all-to-all-start.5 = ((bf16[8,256,768]{2,1,0:T(8,128)(2,1)}), bf16[8,256,768]{2,1,0:T(8,128)(2,1)}, u32[]{:S(2)}, u32[]{:S(2)}) async-start(bf16[8,256,768]{2,1,0:T(8,128)(2,1)} %bitcast.120), calls=%async_computation.5 | async-start | bytes 6291456 | tf_op jit(solution)/shard_map/all_to_all | solution.py:585
  389.0 39.8 %collective-permute-start.44 = (bf16[1024,768]{1,0:T(8,128)(2,1)}, bf16[1024,768]{1,0:T(8,128)(2,1)S(1)}, u32[]{:S(2)}, u32[]{:S(2)}) collective-permute-start(bf16[1024,768]{1,0:T(8,128)(2,1)} %get-tuple-element.207), channel_id=1, source_target_pairs={{16,8},{8,0},{17,9},{9,1},{18,10},{10,2},{19,11},{11,3},{20,12},{1... | collective-permute-start | bytes 4718600 | tf_op jit(solution)/shard_map/ppermute | solution.py:805
  390.3 38.5 %collective-permute-start.43 = (bf16[1024,768]{1,0:T(8,128)(2,1)}, bf16[1024,768]{1,0:T(8,128)(2,1)S(1)}, u32[]{:S(2)}, u32[]{:S(2)}) collective-permute-start(bf16[1024,768]{1,0:T(8,128)(2,1)} %get-tuple-element.208), channel_id=1, source_target_pairs={{8,16},{16,24},{9,17},{17,25},{10,18},{18,26},{11,19},{19,27},{12,... | collective-permute-start | bytes 4718600 | tf_op jit(solution)/shard_map/ppermute | solution.py:805
  411.0 27.6 %collective-permute-start.45 = (bf16[304,768]{1,0:T(8,128)(2,1)S(1)}, bf16[304,768]{1,0:T(8,128)(2,1)}, u32[]{:S(2)}, u32[]{:S(2)}) collective-permute-start(bf16[304,768]{1,0:T(8,128)(2,1)S(1)} %fusion.12), channel_id=1, source_target_pairs={{0,8},{8,0},{16,24},{24,16},{1,9},{9,1},{17,25},{25,17},{2,10},{10... | collective-permute-start | bytes 1400840 | tf_op jit(solution)/shard_map/ppermute | solution.py:577
  438.6 42.5 %all-to-all-start.6 = ((bf16[8,256,768]{2,1,0:T(8,128)(2,1)}), bf16[8,256,768]{2,1,0:T(8,128)(2,1)}, u32[]{:S(2)}, u32[]{:S(2)}) async-start(bf16[8,256,768]{2,1,0:T(8,128)(2,1)} %bitcast.121), calls=%async_computation.6 | async-start | bytes 6291456 | tf_op jit(solution)/shard_map/all_to_all | solution.py:585
  447.7 54.9 %collective-permute-start.47 = (bf16[1024,768]{1,0:T(8,128)(2,1)}, bf16[1024,768]{1,0:T(8,128)(2,1)}, u32[]{:S(2)}, u32[]{:S(2)}) collective-permute-start(bf16[1024,768]{1,0:T(8,128)(2,1)} %get-tuple-element.204), channel_id=1, source_target_pairs={{16,24},{17,25},{18,26},{19,27},{20,28},{21,29},{22,30},{23,31}} | collective-permute-start | bytes 4718600 | tf_op jit(solution)/shard_map/ppermute | solution.py:805
  449.4 53.1 %collective-permute-start.48 = (bf16[1024,768]{1,0:T(8,128)(2,1)}, bf16[1024,768]{1,0:T(8,128)(2,1)}, u32[]{:S(2)}, u32[]{:S(2)}) collective-permute-start(bf16[1024,768]{1,0:T(8,128)(2,1)} %get-tuple-element.205), channel_id=1, source_target_pairs={{8,0},{9,1},{10,2},{11,3},{12,4},{13,5},{14,6},{15,7}} | collective-permute-start | bytes 4718600 | tf_op jit(solution)/shard_map/ppermute | solution.py:805
  470.7 29.0 %collective-permute-start.46 = (bf16[304,768]{1,0:T(8,128)(2,1)S(1)}, bf16[304,768]{1,0:T(8,128)(2,1)}, u32[]{:S(2)}, u32[]{:S(2)}) collective-permute-start(bf16[304,768]{1,0:T(8,128)(2,1)S(1)} %add.355), channel_id=1, source_target_pairs={{0,16},{8,24},{16,0},{24,8},{1,17},{9,25},{17,1},{25,9},{2,18},{10... | collective-permute-start | bytes 1400840 | tf_op jit(solution)/shard_map/ppermute | solution.py:577
  (47 other events, 462.3 us)
